TPU v7x, 256 devices: a whole 4x4x8 slice. The times are simulated.
256 devices in a mesh: dp: 8 (over z_lo, x), seq: 32 (over z_hi, y, core).
Axes of the slice: x: 4, y: 4, z: 8 (z_hi: 4, z_lo: 2; z = z_hi * 2 + z_lo), core: 2. Of those that a mesh axis runs over, the one named last changes fastest.
Arguments:
- inputs: bfloat16 [128, 1024, 1024], P('seq', 'dp'), may hold values from -6 to 6
- gates: bfloat16 [128, 1024, 1024], P('seq', 'dp'), may hold values from -6 to 6
- kernel: bfloat16 [128, 1024, 1024], P('seq', 'dp'), may hold values from -5 to 5
- first_factor: bfloat16 [1024, 1024], replicated, may hold values from -0.1875 to 0.1875
- second_factor: bfloat16 [128, 128], replicated, may hold values from -0.5 to 0.5
- upstream: bfloat16 [128, 1024, 1024], P('seq', 'dp'), may hold values from -6 to 6
Outputs:
- output: bfloat16 [128, 1024, 1024], P('seq', 'dp')
- grad_inputs: bfloat16 [128, 1024, 1024], P('seq', 'dp')
- grad_gates: bfloat16 [128, 1024, 1024], P('seq', 'dp')
- grad_kernel: bfloat16 [128, 1024, 1024], P('seq', 'dp')
- grad_first: float32 [1024, 1024], P('seq')
- grad_second: float32 [128, 128], P('seq')
All inputs are finite; a program needn't handle non-finite values.
Results may differ from a plain program's by a relative error of at most 0.0065.
Values may be sent and summed in bfloat16 or wider, within the bound.
No kernel may reach another device: no remote copies, remote signals or barrier semaphores. Data moves between devices by JAX's collectives and lax.ppermute only.
A program may use at most 64 MiB of HBM per device.

v0:
```python
import math

import jax
import jax.numpy as jnp
from jax import lax
from jax.sharding import PartitionSpec as P


def on_device(inputs, gates, kernel, first_factor, second_factor, upstream):
    local_blocks, channels, width = inputs.shape
    seq_count = lax.axis_size("seq")
    all_channels = channels * lax.axis_size("dp")
    sig = jax.nn.sigmoid(gates.astype(jnp.float32))
    mixed_in = (inputs.astype(jnp.float32) * sig).astype(jnp.bfloat16)
    flat_in = mixed_in.reshape(local_blocks * channels, width)
    blocks = lax.dot_general(
        flat_in, first_factor, (((1,), (1,)), ((), ())), preferred_element_type=jnp.float32
    )
    blocks = blocks.astype(jnp.bfloat16).reshape(local_blocks, channels, width)
    kerneled = (blocks.astype(jnp.float32) * kernel.astype(jnp.float32)).astype(jnp.bfloat16)
    kern_rows = kerneled.reshape(local_blocks, channels * width)
    up_rows = upstream.reshape(local_blocks, channels * width)
    flat_moved = lax.all_to_all(kern_rows, "seq", split_axis=1, concat_axis=0, tiled=True)
    all_blocks = flat_moved.shape[0]
    across = jnp.dot(second_factor, flat_moved, preferred_element_type=jnp.float32).astype(
        jnp.bfloat16
    )
    output = lax.all_to_all(across, "seq", split_axis=0, concat_axis=1, tiled=True).reshape(
        local_blocks, channels, width
    )
    flat_up = lax.all_to_all(up_rows, "seq", split_axis=1, concat_axis=0, tiled=True)
    grad_across = lax.dot_general(
        second_factor, flat_up, (((0,), (0,)), ((), ())), preferred_element_type=jnp.float32
    )
    grad_across = grad_across.astype(jnp.bfloat16)
    grad_mid = lax.all_to_all(grad_across, "seq", split_axis=0, concat_axis=1, tiled=True).reshape(
        local_blocks, channels, width
    )
    grad_kernel = (grad_mid.astype(jnp.float32) * blocks.astype(jnp.float32)).astype(jnp.bfloat16)
    grad_blocks = (grad_mid.astype(jnp.float32) * kernel.astype(jnp.float32)).astype(jnp.bfloat16)
    flat_grad = grad_blocks.reshape(local_blocks * channels, width)
    grad_mixed = jnp.dot(flat_grad, first_factor, preferred_element_type=jnp.float32).reshape(
        local_blocks, channels, width
    )
    grad_inputs = (grad_mixed * sig).astype(jnp.bfloat16)
    grad_gates = (grad_mixed * inputs.astype(jnp.float32) * sig * (1.0 - sig)).astype(jnp.bfloat16)
    first_norm = 1.0 / math.sqrt(all_blocks * all_channels)
    second_norm = 1.0 / math.sqrt(all_channels * width)
    first_owned = width // seq_count
    second_owned = all_blocks // seq_count
    first_full = lax.dot_general(
        flat_grad, flat_in, (((0,), (0,)), ((), ())), preferred_element_type=jnp.float32
    )
    second_full = lax.dot_general(
        flat_up, flat_moved, (((1,), (1,)), ((), ())), preferred_element_type=jnp.float32
    )
    first_total, second_total = lax.psum((first_full, second_full), ("dp", "seq"))
    position = lax.axis_index("seq")
    first_sum = lax.dynamic_slice_in_dim(first_total, position * first_owned, first_owned, 0)
    second_sum = lax.dynamic_slice_in_dim(second_total, position * second_owned, second_owned, 0)
    grad_first = first_sum * first_norm
    grad_second = second_sum * second_norm
    return (output, grad_inputs, grad_gates, grad_kernel, grad_first, grad_second)


def solution(mesh):
    in_specs = (
        P("seq", "dp", None),
        P("seq", "dp", None),
        P("seq", "dp", None),
        P(),
        P(),
        P("seq", "dp", None),
    )
    out_specs = (
        P("seq", "dp", None),
        P("seq", "dp", None),
        P("seq", "dp", None),
        P("seq", "dp", None),
        P("seq", None),
        P("seq", None),
    )
    return jax.shard_map(
        on_device, mesh=mesh, in_specs=in_specs, out_specs=out_specs, check_vma=False
    )
```

profile of v0, /device:TPU:65, one launch (start us, length us, event | category | flops | bytes accessed | tf_op | source)
XLA Modules:
  0.0 434.4 jit_solution(16927520540910148546)
XLA Ops:
  7.2 0.0 copy-start
  7.2 1.9 all_to_all.57
  9.0 0.8 copy.18
  9.9 0.0 copy-start.5
  9.9 40.2 %all_to_all.67 = bf16[4,32,4096]{2,0,1:T(4,128)(2,1)} all-to-all(bf16[4,32,4096]{2,0,1:T(4,128)(2,1)S(1)} %copy.18), channel_id=1, replica_groups=mesh['dp'=8,'seq'=32] {'seq'}, dimensions={1} | all-to-all | bytes 2097152 | tf_op jit(solution)/shard_map/all_to_all | solution.py:31
  50.0 1.3 all_to_all.60
  51.4 0.0 copy-done.5
  51.4 1.4 convolution_convert_fusion.1
  52.8 2.2 all_to_all.61
  55.1 34.2 %all_to_all.68 = bf16[32,4,4096]{2,1,0:T(4,128)(2,1)S(1)} all-to-all(bf16[32,4,4096]{2,1,0:T(4,128)(2,1)} %all_to_all.61), channel_id=1, replica_groups=mesh['dp'=8,'seq'=32] {'seq'}, dimensions={0} | all-to-all | bytes 2097152 | tf_op jit(solution)/shard_map/all_to_all | solution.py:36
  89.2 0.2 convert_bitcast_fusion
  89.5 2.6 copy.19
  92.0 2.9 reshape.49
  94.9 0.0 copy-done
  94.9 5.7 %fusion.4 = (bf16[4,128,1024]{2,1,0:T(8,128)(2,1)}, bf16[4,128,1024]{2,1,0:T(8,128)(2,1)}, bf16[4,128,1024]{2,1,0:T(8,128)(2,1)S(1)}) fusion(bf16[4,128,1024]{2,1,0:T(8,128)(2,1)} %param.6, bf16[4,128,1024]{2,1,0:T(8,128)(2,1)} %param.7, bf16[1024,1024]{1,0:T(8,128)(2,1)S(1)} %copy-done, f32[4,128,1024]{2,1,0:T(8,128)} %reshape.49, ...), kind=kOutput, calls=%fused_computation.12 | convolution fusion | flops 1082654720 | bytes 10485760 | tf_op jit(solution)/shard_map/dot_general | solution.py:42
  100.6 0.0 copy-start.4
  100.6 0.0 copy-start.1
  100.6 0.0 copy-start.3
  100.6 1.3 convolution_convert_fusion.2
  101.9 0.0 copy-done.4
  101.9 0.6 copy-done.1
  102.5 0.3 copy-done.3
  102.8 2.0 fusion.7
  104.8 2.5 all_to_all.50
  107.3 3.0 copy.16
  110.3 5.3 %all-to-all-start = ((bf16[4,32,4096]{2,0,1:T(4,128)(2,1)}), bf16[4,32,4096]{2,0,1:T(4,128)(2,1)}, u32[]{:S(2)}, u32[]{:S(2)}) async-start(bf16[4,32,4096]{2,0,1:T(4,128)(2,1)} %copy.16), calls=%async_computation | async-start | bytes 2097152 | tf_op jit(solution)/shard_map/all_to_all | solution.py:23
  115.6 0.2 all-reduce.3.cloned.1.call-start
  115.8 5.4 %convolution_bitcast_fusion = f32[1024,1024]{1,0:T(8,128)} fusion(bf16[4,128,1024]{2,1,0:T(8,128)(2,1)} %copy-done.4, f32[4,128,1024]{2,1,0:T(8,128)} %reshape.49, bf16[4,128,1024]{2,1,0:T(8,128)(2,1)} %param.8), kind=kOutput, calls=%fused_computation.8 | convolution fusion | flops 1075314688 | bytes 8388608 | tf_op jit(solution)/shard_map/dot_general | solution.py:51
  121.2 23.1 %all-to-all-done = bf16[4,32,4096]{2,0,1:T(4,128)(2,1)} async-done(((bf16[4,32,4096]{2,0,1:T(4,128)(2,1)}), bf16[4,32,4096]{2,0,1:T(4,128)(2,1)}, u32[]{:S(2)}, u32[]{:S(2)}) %all-to-all-start) | async-done | bytes 1048608 | tf_op jit(solution)/shard_map/all_to_all | solution.py:23
  144.3 2.1 all_to_all.53
  146.4 2.3 convolution_bitcast_fusion.1
  148.7 0.0 copy-start.2
  148.7 0.0 all-reduce.3.cloned.1.call-update
  148.7 1.2 copy-done.2
  149.9 1.4 fusion
  151.3 2.3 all_to_all.54
  153.6 5.2 %all-to-all-start.1 = ((bf16[32,4,4096]{2,1,0:T(4,128)(2,1)}), bf16[32,4,4096]{2,1,0:T(4,128)(2,1)S(1)}, u32[]{:S(2)}, u32[]{:S(2)}) async-start(bf16[32,4,4096]{2,1,0:T(4,128)(2,1)} %all_to_all.54), calls=%async_computation.1 | async-start | bytes 2097152 | tf_op jit(solution)/shard_map/all_to_all | solution.py:28
  158.9 31.1 %all-to-all-done.1 = bf16[32,4,4096]{2,1,0:T(4,128)(2,1)S(1)} async-done(((bf16[32,4,4096]{2,1,0:T(4,128)(2,1)}), bf16[32,4,4096]{2,1,0:T(4,128)(2,1)S(1)}, u32[]{:S(2)}, u32[]{:S(2)}) %all-to-all-start.1) | async-done | bytes 1048608 | tf_op jit(solution)/shard_map/all_to_all | solution.py:28
  190.0 1.6 copy.17
  191.7 2.5 reshape.47
  194.2 230.3 %all-reduce.3.cloned.1.call-done = (f32[1024,1024]{1,0:T(8,128)}, f32[128,128]{0,1:T(8,128)}) async-done(((f32[1024,1024]{1,0:T(8,128)}, f32[128,128]{0,1:T(8,128)}), (f32[1024,1024]{1,0:T(8,128)}, f32[128,128]{0,1:T(8,128)})) %all-reduce.3.cloned.1.call-update) | async-done | bytes 4259856 | tf_op jit(solution)/shard_map/psum | solution.py:57
  424.4 0.9 dynamic-slice_multiply_fusion.1
  425.4 0.7 copy.21
  426.0 1.6 dynamic-slice_multiply_fusion
Async XLA Ops:
  7.2 87.7 %copy-start = (bf16[1024,1024]{1,0:T(8,128)(2,1)S(1)}, bf16[1024,1024]{1,0:T(8,128)(2,1)}, u32[]{:S(2)}) copy-start(bf16[1024,1024]{1,0:T(8,128)(2,1)} %param.9) | copy-start | bytes 6291460
  9.9 41.5 %copy-start.5 = (bf16[128,128]{1,0:T(8,128)(2,1)S(1)}, bf16[128,128]{1,0:T(8,128)(2,1)}, u32[]{:S(2)}) copy-start(bf16[128,128]{1,0:T(8,128)(2,1)} %param.10) | copy-start | bytes 98308
  100.6 1.3 copy-start.4
  100.6 2.0 copy-start.1
  100.6 2.2 copy-start.3
  110.3 34.0 %all-to-all-start = ((bf16[4,32,4096]{2,0,1:T(4,128)(2,1)}), bf16[4,32,4096]{2,0,1:T(4,128)(2,1)}, u32[]{:S(2)}, u32[]{:S(2)}) async-start(bf16[4,32,4096]{2,0,1:T(4,128)(2,1)} %copy.16), calls=%async_computation | async-start | bytes 2097152 | tf_op jit(solution)/shard_map/all_to_all | solution.py:23
  115.6 308.9 %all-reduce.3.cloned.1.call-start = ((), (), s32[]{:S(2)}) async-start(), calls=%async_computation.4 | async-start | bytes 8519680 | tf_op jit(solution)/shard_map/psum | solution.py:57
  148.7 1.2 copy-start.2
  153.6 36.4 %all-to-all-start.1 = ((bf16[32,4,4096]{2,1,0:T(4,128)(2,1)}), bf16[32,4,4096]{2,1,0:T(4,128)(2,1)S(1)}, u32[]{:S(2)}, u32[]{:S(2)}) async-start(bf16[32,4,4096]{2,1,0:T(4,128)(2,1)} %all_to_all.54), calls=%async_computation.1 | async-start | bytes 2097152 | tf_op jit(solution)/shard_map/all_to_all | solution.py:28
Sparse Core Ops, SparseCore 0:
  148.9 275.5 all-reduce.2
where the time goes:
time: 437 us; the launch traced here: 434 us
  waiting for transfers between devices  284 us (65%)
  blocking collectives  74.3 us (17%)
  local copies, waits for them, and re-layouts  28.5 us (7%)
  matrix products  17.5 us (4%)
  between operations  14.1 us (3%)
  starting transfers between devices  10.8 us (2%)
  other arithmetic  4.69 us (1%)
    psum x1, waiting for transfers between devices, on_device(): lax.psum((first_full, second_full), ('dp', 'seq'))  230 us
    all_to_all x1, blocking collectives, on_device(): lax.all_to_all(up_rows, 'seq', split_axis=1, concat_axis=0, tiled=True)  40.2 us
    all_to_all x1, blocking collectives, on_device(): lax.all_to_all(grad_across, 'seq', split_axis=0, concat_axis=1, tiled=True)  34.2 us
    all_to_all x1, waiting for transfers between devices, on_device(): lax.all_to_all(across, 'seq', split_axis=0, concat_axis=1, tiled=True)  31.1 us
    all_to_all x1, waiting for transfers between devices, on_device(): lax.all_to_all(kern_rows, 'seq', split_axis=1, concat_axis=0, tiled=True)  23.1 us
  transfers between devices with their start and end apart: 3, of which 3 were waited for; matrix products, arithmetic and copies ran while one was open for 3% of the time, Pallas kernels for 0%

commit v1 on v0

v1 whole, which is shorter than its diff:
```python
import functools
import math

import jax
import jax.numpy as jnp
from jax import lax
from jax.experimental import pallas as pl
from jax.experimental.pallas import tpu as pltpu
from jax.sharding import Mesh
from jax.sharding import PartitionSpec as P

AXES = ("zl", "x", "zh", "y", "c")
BF = jnp.bfloat16
F32 = jnp.float32
PEERS, LOCAL, ROWS, HALF = 16, 4, 8, 512
CHANNELS, WIDTH = PEERS * ROWS, 2 * HALF
NB = PEERS * 2 * LOCAL
SIDE = PEERS * LOCAL * ROWS
LIMIT = 32 * 1024 * 1024


def swap(value):
    return lax.ppermute(value, "c", [(0, 1), (1, 0)])


def flip(value, axis, bit):
    size = lax.axis_size(axis)
    return lax.ppermute(value, axis, [(i, i ^ bit) for i in range(size)])


def shift(value, axis, step):
    size = lax.axis_size(axis)
    return lax.ppermute(value, axis, [(i, (i + step) % size) for i in range(size)])


def exchange(value):
    return lax.all_to_all(value, ("zh", "y"), 0, 0, tiled=True)


def after(value, *others):
    return lax.optimization_barrier((value,) + others)[0]


def to_owner():
    perm = []
    for zl in range(2):
        for x in range(4):
            for zh in range(4):
                for y in range(4):
                    for c in range(2):
                        place = 16 * c + 4 * x + y
                        source = (((zl * 4 + x) * 4 + zh) * 4 + y) * 2 + c
                        target = (((zl * 4 + zh) * 4 + place // 8) * 4 + place // 2 % 4) * 2 + place % 2
                        perm.append((source, target))
    return perm


def call(body, scalars, operands, in_specs, out_shapes, out_specs, grid=(1,), scratch=(), flops=0, moved=0):
    return pl.pallas_call(
        body,
        out_shape=out_shapes,
        grid_spec=pltpu.PrefetchScalarGridSpec(
            num_scalar_prefetch=len(scalars),
            grid=grid,
            in_specs=in_specs,
            out_specs=out_specs,
            scratch_shapes=list(scratch),
        ),
        compiler_params=pltpu.CompilerParams(vmem_limit_bytes=LIMIT),
        cost_estimate=pl.CostEstimate(flops=flops, bytes_accessed=moved, transcendentals=0),
    )(*scalars, *operands)


def whole(shape):
    return pl.BlockSpec(shape, lambda *_: (0,) * len(shape))


def struct(shape, dtype=BF):
    return jax.ShapeDtypeStruct(shape, dtype)


def sigmoid(gates):
    return jax.nn.sigmoid(gates.astype(F32))


def pack_body(in_ref, out_ref):
    for b in range(LOCAL):
        out_ref[:, b] = in_ref[b].reshape(PEERS, ROWS, WIDTH)


def pack(value):
    return call(
        pack_body,
        (),
        (value,),
        [whole((LOCAL, CHANNELS, WIDTH))],
        struct((PEERS, LOCAL, ROWS, WIDTH)),
        whole((PEERS, LOCAL, ROWS, WIDTH)),
        moved=4 << 20,
    )


def widen_body(core_ref, sf_ref, wide_ref, turned_ref):
    core = core_ref[0]
    size = 2 * SIDE
    n = lax.broadcasted_iota(jnp.int32, (size, NB), 0)
    o = lax.broadcasted_iota(jnp.int32, (size, NB), 1)
    rel = n // SIDE
    real = rel + core - 2 * rel * core
    source = (n // (LOCAL * ROWS)) % PEERS * (2 * LOCAL) + real * LOCAL + (n // ROWS) % LOCAL
    pick = jnp.where(source == o, 1.0, 0.0).astype(BF)
    row = lax.broadcasted_iota(jnp.int32, (size, size), 0) % ROWS
    column = lax.broadcasted_iota(jnp.int32, (size, size), 1) % ROWS
    same = row == column
    for ref, dim in ((wide_ref, 0), (turned_ref, 1)):
        tall = lax.dot_general(pick, sf_ref[...], (((1,), (dim,)), ((), ())), preferred_element_type=F32)
        full = lax.dot_general(tall.astype(BF), pick, (((1,), (1,)), ((), ())), preferred_element_type=F32)
        ref[...] = jnp.where(same, full, 0.0).astype(BF)


def widen(core, sf):
    shape = (2 * SIDE, 2 * SIDE)
    return call(
        widen_body,
        (core,),
        (sf,),
        [whole((NB, NB))],
        [struct(shape), struct(shape)],
        [whole(shape), whole(shape)],
        flops=1 << 30,
        moved=4 << 20,
    )


GROUP = 4
STEP_ROWS = GROUP * LOCAL * ROWS


def forward_body(
    core_ref, in_ref, gate_ref, kernel_ref, ff_ref, mixed_ref, blocks_ref, own_ref, oth_ref, kown_ref, koth_ref, flat
):
    core = core_ref[0]
    for b in range(LOCAL):
        mixed = (in_ref[b].astype(F32) * sigmoid(gate_ref[b])).astype(BF)
        for g in range(GROUP):
            piece = mixed[g * ROWS : (g + 1) * ROWS]
            mixed_ref[g, b] = piece
            flat[(g * LOCAL + b) * ROWS : (g * LOCAL + b + 1) * ROWS] = piece
    blocks = lax.dot_general(flat[...], ff_ref[...], (((1,), (1,)), ((), ())), preferred_element_type=F32)
    blocks = blocks.astype(BF).reshape(GROUP, LOCAL, ROWS, WIDTH)
    blocks_ref[...] = blocks
    for b in range(LOCAL):
        weight = kernel_ref[b].reshape(GROUP, ROWS, WIDTH)
        kern = (blocks[:, b].astype(F32) * weight.astype(F32)).astype(BF)
        low, high = kern[..., :HALF], kern[..., HALF:]
        own_ref[:, b] = jnp.where(core == 0, low, high)
        oth_ref[:, b] = jnp.where(core == 0, high, low)
        low, high = weight[..., :HALF], weight[..., HALF:]
        kown_ref[:, b] = jnp.where(core == 0, low, high)
        koth_ref[:, b] = jnp.where(core == 0, high, low)


def natural_spec():
    return pl.BlockSpec((LOCAL, GROUP * ROWS, WIDTH), lambda i, *_: (0, i, 0))


def rows_spec(width):
    return pl.BlockSpec((GROUP, LOCAL, ROWS, width), lambda i, *_: (i, 0, 0, 0))


def forward(core, inputs, gates, kernel, ff):
    full, part = struct((PEERS, LOCAL, ROWS, WIDTH)), struct((PEERS, LOCAL, ROWS, HALF))
    return call(
        forward_body,
        (core,),
        (inputs, gates, kernel, ff),
        [natural_spec()] * 3 + [whole((WIDTH, WIDTH))],
        [full, full, part, part, part, part],
        [rows_spec(WIDTH)] * 2 + [rows_spec(HALF)] * 4,
        grid=(PEERS // GROUP,),
        scratch=[pltpu.VMEM((STEP_ROWS, WIDTH), BF)],
        flops=1 << 30,
        moved=9 << 20,
    )


CHUNK = 256


def across_body(core_ref, wide_ref, own_ref, oth_ref, out_ref):
    own = own_ref[...].reshape(SIDE, CHUNK)
    oth = oth_ref[...].reshape(SIDE, CHUNK)
    total = jnp.dot(wide_ref[:, :SIDE], own, preferred_element_type=F32)
    total = total + jnp.dot(wide_ref[:, SIDE:], oth, preferred_element_type=F32)
    total = total.astype(BF)
    for rel in range(2):
        out_ref[:, rel] = total[rel * SIDE : (rel + 1) * SIDE].reshape(PEERS, LOCAL, ROWS, CHUNK)


def across(core, wide, own, oth):
    steps = HALF // CHUNK
    block = (PEERS, LOCAL, ROWS, CHUNK)
    if own.shape[-1] == WIDTH:
        own_spec = pl.BlockSpec(block, lambda i, core: (0, 0, 0, core[0] * steps + i))
    else:
        own_spec = pl.BlockSpec(block, lambda i, core: (0, 0, 0, i))
    return call(
        across_body,
        (core,),
        (wide, own, oth),
        [whole((2 * SIDE, 2 * SIDE)), own_spec, pl.BlockSpec(block, lambda i, core: (0, 0, 0, i))],
        struct((PEERS, 2, LOCAL, ROWS, HALF)),
        pl.BlockSpec((PEERS, 2, LOCAL, ROWS, CHUNK), lambda i, core: (0, 0, 0, 0, i)),
        grid=(steps,),
        flops=1 << 30,
        moved=4 << 20,
    )


def second_body(core_ref, up_ref, up_oth_ref, own_ref, oth_ref, out_ref):
    core = core_ref[0]
    size = 2 * SIDE
    ups = [ref[...].reshape(SIDE, HALF) for ref in (up_ref, up_oth_ref)]
    kerns = [ref[...].reshape(SIDE, HALF) for ref in (own_ref, oth_ref)]
    row = lax.broadcasted_iota(jnp.int32, (SIDE, SIDE), 0) % ROWS
    column = lax.broadcasted_iota(jnp.int32, (SIDE, SIDE), 1) % ROWS
    same = row == column
    n = lax.broadcasted_iota(jnp.int32, (size, NB), 0)
    o = lax.broadcasted_iota(jnp.int32, (size, NB), 1)

    def place(m, per):
        rel = m // (PEERS * LOCAL * per)
        real = rel + core - 2 * rel * core
        return (m // (LOCAL * per)) % PEERS * (2 * LOCAL) + real * LOCAL + (m // per) % LOCAL

    pick = jnp.where(place(n, ROWS) == o, 1.0, 0.0)
    tall = []
    for up in ups:
        wide = []
        for kern in kerns:
            full = lax.dot_general(up, kern, (((1,), (1,)), ((), ())), preferred_element_type=F32)
            full = jnp.where(same, full, 0.0).reshape(SIDE // ROWS, ROWS, SIDE)
            wide.append(full.sum(1))
        tall.append(jnp.concatenate(wide, 1))
    tall = jnp.concatenate(tall, 0)
    total = jnp.dot(tall, pick, precision=lax.Precision.HIGHEST, preferred_element_type=F32)
    n = lax.broadcasted_iota(jnp.int32, (NB, NB), 1)
    o = lax.broadcasted_iota(jnp.int32, (NB, NB), 0)
    pick = jnp.where(place(n, 1) == o, 1.0, 0.0)
    out_ref[...] = jnp.dot(pick, total, precision=lax.Precision.HIGHEST, preferred_element_type=F32)


def second(core, up, up_oth, own, oth):
    block = (PEERS, LOCAL, ROWS, HALF)
    return call(
        second_body,
        (core,),
        (up, up_oth, own, oth),
        [pl.BlockSpec(block, lambda i, core: (0, 0, 0, core[0]))] + [whole(block)] * 3,
        struct((NB, NB), F32),
        whole((NB, NB)),
        flops=1 << 30,
        moved=2 << 20,
    )


ORDER = (2, 1, 3, 0)
SHARE = HALF // 4


def first_body(x_ref, mid_ref, kown_ref, koth_ref, own_ref, oth_ref, *out_refs):
    total = 0.0
    for rel, (weight, mixed) in enumerate(((kown_ref, own_ref), (koth_ref, oth_ref))):
        grad = mid_ref[:, rel].reshape(SIDE, SHARE).astype(F32) * weight[...].reshape(SIDE, SHARE).astype(F32)
        total = total + lax.dot_general(
            grad.astype(BF),
            mixed[...].reshape(SIDE, WIDTH),
            (((0,), (0,)), ((), ())),
            preferred_element_type=F32,
        )
    for step, ref in enumerate(out_refs):

        @pl.when(pl.program_id(0) == step)
        def _():
            ref[...] = total.astype(ref.dtype)


def first_terms(x, mid, kown, koth, own, oth):
    def chunk(i, x):
        step = jnp.where(i == 0, 2, jnp.where(i == 2, 3, jnp.where(i == 1, 1, 0)))
        return lax.rem(x[0] + step, 4)

    weight = pl.BlockSpec((PEERS, LOCAL, ROWS, SHARE), lambda i, x: (0, 0, 0, chunk(i, x)))
    mixed = whole((PEERS, LOCAL, ROWS, WIDTH))
    out = (SHARE, WIDTH)
    return call(
        first_body,
        (x,),
        (mid, kown, koth, own, oth),
        [pl.BlockSpec((PEERS, 2, LOCAL, ROWS, SHARE), lambda i, x: (0, 0, 0, 0, chunk(i, x))), weight, weight]
        + [mixed, mixed],
        [struct(out), struct(out), struct(out), struct(out, F32)],
        [whole(out)] * 4,
        grid=(4,),
        flops=1 << 30,
        moved=5 << 20,
    )


def grads_body(
    core_ref, mid_ref, got_ref, blocks_ref, kown_ref, koth_ref, in_ref, gate_ref, ff_ref, gin_ref, ggate_ref, gkern_ref
):
    core = core_ref[0]
    own = pl.ds(pl.multiple_of(core * HALF, HALF), HALF)
    oth = pl.ds(pl.multiple_of((1 - core) * HALF, HALF), HALF)
    total = 0.0
    for at, mid, weight in ((own, mid_ref[:, 0], kown_ref), (oth, got_ref[...], koth_ref)):
        mid = mid.astype(F32)
        grad = (mid * blocks_ref[:, :, :, at].astype(F32)).astype(BF)
        for b in range(LOCAL):
            gkern_ref[b, :, at] = grad[:, b].reshape(GROUP * ROWS, HALF)
        grad = (mid * weight[...].astype(F32)).astype(BF).reshape(STEP_ROWS, HALF)
        total = total + jnp.dot(grad, ff_ref[at, :], preferred_element_type=F32)
    total = total.reshape(GROUP, LOCAL, ROWS, WIDTH)
    for b in range(LOCAL):
        grad = total[:, b].reshape(GROUP * ROWS, WIDTH)
        sig = sigmoid(gate_ref[b])
        gin_ref[b] = (grad * sig).astype(BF)
        ggate_ref[b] = (grad * in_ref[b].astype(F32) * sig * (1.0 - sig)).astype(BF)


def grads(core, mid, got, blocks, kown, koth, inputs, gates, ff):
    out = struct((LOCAL, CHANNELS, WIDTH))
    return call(
        grads_body,
        (core,),
        (mid, got, blocks, kown, koth, inputs, gates, ff),
        [
            pl.BlockSpec((GROUP, 1, LOCAL, ROWS, HALF), lambda i, *_: (i, 0, 0, 0, 0)),
            rows_spec(HALF),
            rows_spec(WIDTH),
            rows_spec(HALF),
            rows_spec(HALF),
            natural_spec(),
            natural_spec(),
            whole((WIDTH, WIDTH)),
        ],
        [out, out, out],
        [natural_spec()] * 3,
        grid=(PEERS // GROUP,),
        flops=1 << 30,
        moved=10 << 20,
    )


def join_body(core_ref, mid_ref, got_ref, out_ref):
    core = core_ref[0]
    own = pl.ds(pl.multiple_of(core * HALF, HALF), HALF)
    oth = pl.ds(pl.multiple_of((1 - core) * HALF, HALF), HALF)
    for b in range(LOCAL):
        out_ref[b, :, own] = mid_ref[:, 0, b].reshape(GROUP * ROWS, HALF)
        out_ref[b, :, oth] = got_ref[:, b].reshape(GROUP * ROWS, HALF)


def join(core, mid, got):
    return call(
        join_body,
        (core,),
        (mid, got),
        [pl.BlockSpec((GROUP, 1, LOCAL, ROWS, HALF), lambda i, *_: (i, 0, 0, 0, 0)), rows_spec(HALF)],
        struct((LOCAL, CHANNELS, WIDTH)),
        natural_spec(),
        grid=(PEERS // GROUP,),
        moved=4 << 20,
    )


def on_device(inputs, gates, kernel, first_factor, second_factor, upstream):
    core, x, y = (lax.axis_index(axis) for axis in ("c", "x", "y"))
    core_at, x_at = (value.reshape(1).astype(jnp.int32) for value in (core, x))
    all_channels = CHANNELS * lax.axis_size("zl") * lax.axis_size("x")

    up = exchange(pack(upstream))
    wide, turned = widen(core_at, second_factor)
    mixed, blocks, kern_own, kern_oth, kown, koth = forward(core_at, inputs, gates, kernel, first_factor)
    kern_oth = swap(kern_oth)
    koth_got = swap(koth)
    mixed_got = swap(mixed)

    kern_own = exchange(after(kern_own, up))
    up_oth = swap(lax.dynamic_slice_in_dim(up, (1 - core) * HALF, HALF, 3))
    mid = across(core_at, turned, up, up_oth)
    mid = exchange(after(mid, kern_own))
    kern_oth = exchange(after(kern_oth, mid))
    out = exchange(across(core_at, wide, kern_own, kern_oth))
    output = join(core_at, out, swap(out[:, 1]))

    sent2, sent1, sent3, total = first_terms(x_at, mid, kown, koth_got, mixed, mixed_got)
    got = [shift(sent2, "x", 2), shift(sent1, "x", 1), shift(sent3, "x", 3)]
    total = total + got[1].astype(F32) + got[2].astype(F32) + got[0].astype(F32)
    total = total.reshape(4, SHARE // 4, WIDTH)
    parts = total.astype(BF)
    got = [shift(lax.dynamic_index_in_dim(parts, lax.rem(y + step, 4), 0, False), "y", step) for step in (2, 1, 3)]
    total = lax.dynamic_index_in_dim(total, y, 0, False)
    for part in got:
        total = total + part.astype(F32)
    for axis, bit in (("zl", 1), ("zh", 1), ("zh", 2)):
        part = total.astype(BF)
        total = part.astype(F32) + flip(part, axis, bit).astype(F32)
    total = total * (1.0 / math.sqrt(NB * all_channels))
    grad_first = lax.ppermute(total, AXES, to_owner())

    got = swap(mid[:, 1])
    grad_inputs, grad_gates, grad_kernel = grads(core_at, mid, got, blocks, kown, koth, inputs, gates, first_factor)

    total = second(core_at, up, up_oth, kern_own, kern_oth)
    for axis, bit in (("c", 1), ("x", 1), ("x", 2), ("zl", 1), ("y", 1), ("y", 2), ("zh", 1), ("zh", 2)):
        total = total + flip(total, axis, bit)
    place = (lax.axis_index("zh") * 4 + y) * 2 + core
    grad_second = lax.dynamic_slice_in_dim(total, place * LOCAL, LOCAL, 0)
    grad_second = grad_second * (1.0 / math.sqrt(all_channels * WIDTH))
    return (output, grad_inputs, grad_gates, grad_kernel, grad_first, grad_second)


def solution(mesh):
    fine = Mesh(mesh.devices.reshape(2, 4, 4, 4, 2), AXES)
    seq, dp = ("zh", "y", "c"), ("zl", "x")
    big = P(seq, dp, None)
    return jax.shard_map(
        on_device,
        mesh=fine,
        in_specs=(big, big, big, P(), P(), big),
        out_specs=(big, big, big, big, P(seq, None), P(seq, None)),
        check_vma=False,
    )
```

time: 437 us -> 217 us (0.50)
  waiting for transfers between devices: 284 us -> 70.9 us
  blocking collectives: 74.3 us -> 0 us
  starting transfers between devices: 10.8 us -> 81.9 us
  Pallas kernels: 0 us -> 26.4 us
  matrix products: 17.5 us -> 0 us
  between operations: 14.1 us -> 0.98 us
    psum x1 -> x0, waiting for transfers between devices: 230 us -> none  [on_device(): lax.psum((first_full, second_full), ('dp', 'seq'))]
    all_to_all x2 -> x0, blocking collectives: 74.3 us -> none  [the longest x1 40.2 us: on_device(): lax.all_to_all(up_rows, 'seq', split_axis=1, concat_axis=0, tiled=True)]
    ppermute x0 -> x24, starting transfers between devices: none -> 42.5 us  [the longest x11 16.8 us: flip(): return lax.ppermute(value, axis, [(i, i ^ bit) for i in range(size)])]
    all_to_all x2 -> x5, starting transfers between devices: 10.5 us -> 39.4 us  [exchange(): return lax.all_to_all(value, ('zh', 'y'), 0, 0, tiled=True)]
    pallas_call x0 -> x9, Pallas kernels: none -> 26.4 us  [call(): pl.pallas_call(body, out_shape=out_shapes, grid_spec=pltpu.PrefetchScalar...]
    unnamed x13 -> x61, local copies, waits for them, and re-layouts: 2.78 us -> 27 us
    all_to_all x9 -> x0, local copies, waits for them, and re-layouts: 17.8 us -> none  [the longest x3 7.62 us: on_device(): lax.all_to_all(kern_rows, 'seq', split_axis=1, concat_axis=0, tiled=True)]
    ppermute x0 -> x24, waiting for transfers between devices: none -> 17.8 us  [the longest x6 12.3 us: shift(): lax.ppermute(value, axis, [(i, (i + step) % size) for i in range(size)])]
  transfers between devices with their start and end apart: 3 -> 29, of which waited for: 3 -> 10; matrix products, arithmetic and copies ran while one was open for 3% -> 3% of each run, Pallas kernels for 0% -> 11%
where the time goes in v1:
time: 217 us; the launch traced here: 214 us
  starting transfers between devices  81.9 us (38%)
  waiting for transfers between devices  70.9 us (33%)
  local copies, waits for them, and re-layouts  29.8 us (14%)
  Pallas kernels  26.4 us (12%)
  other arithmetic  4 us (2%)
    all_to_all x5, waiting for transfers between devices, exchange(): return lax.all_to_all(value, ('zh', 'y'), 0, 0, tiled=True)  53.1 us
    all_to_all x5, starting transfers between devices, exchange(): return lax.all_to_all(value, ('zh', 'y'), 0, 0, tiled=True)  39.4 us
    unnamed x61, local copies, waits for them, and re-layouts  27 us
    pallas_call x9, Pallas kernels, call(): pl.pallas_call(body, out_shape=out_shapes, grid_spec=pltpu.PrefetchScalar...  26.4 us
    ppermute x11, starting transfers between devices, flip(): return lax.ppermute(value, axis, [(i, i ^ bit) for i in range(size)])  16.8 us
    ppermute x6, waiting for transfers between devices, shift(): lax.ppermute(value, axis, [(i, (i + step) % size) for i in range(size)])  12.3 us
    ppermute x6, starting transfers between devices, swap(): return lax.ppermute(value, 'c', [(0, 1), (1, 0)])  10.9 us
    ppermute x6, starting transfers between devices, shift(): lax.ppermute(value, axis, [(i, (i + step) % size) for i in range(size)])  8.38 us
  transfers between devices with their start and end apart: 29, of which 10 were waited for; matrix products, arithmetic and copies ran while one was open for 3% of the time, Pallas kernels for 11%

profile of v1, /device:TPU:65, one launch (start us, length us, event | category | flops | bytes accessed | tf_op | source)
XLA Modules:
  0.0 213.9 jit_solution(14702239487322507852)
XLA Ops:
  0.7 1.4 copy-done.19
  2.1 1.0 copy-done.9
  3.1 10.2 %all-to-all-start = ((bf16[16,4,8,1024]{3,2,1,0:T(8,128)(2,1)}), bf16[16,4,8,1024]{3,2,1,0:T(8,128)(2,1)S(1)}, u32[]{:S(2)}, u32[]{:S(2)}) async-start(bf16[16,4,8,1024]{3,2,1,0:T(8,128)(2,1)} %copy-done.9), calls=%async_computation | async-start | bytes 2097152 | tf_op jit(solution)/shard_map/all_to_all | solution.py:37
  13.3 1.2 copy-done.5
  14.5 1.2 copy-done.7
  15.7 1.2 copy-done.20
  16.9 3.7 %shard_map.110 = (bf16[16,4,8,1024]{3,2,1,0:T(8,128)(2,1)S(1)}, bf16[16,4,8,1024]{3,2,1,0:T(8,128)(2,1)S(1)}, bf16[16,4,8,512]{3,2,1,0:T(8,128)(2,1)S(1)}, bf16[...) custom-call(s32[1]{0:T(128)} %bitcast.core_ref, ...), custom_call_target="tpu_custom_call" | custom-call | flops 1073741824 | bytes 9437184 | tf_op jit(solution)/shard_map/pallas_call | solution.py:59
  21.5 1.0 copy-done.15
  22.5 1.0 copy-done.17
  25.8 9.4 %all-to-all-done.own_ref.up_ref = bf16[16,4,8,1024]{3,2,1,0:T(8,128)(2,1)S(1)} async-done(((bf16[16,4,8,1024]{3,2,1,0:T(8,128)(2,1)}), bf16[16,4,8,1024]{3,2,1,0:T(8,128)(2,1)S(1)}, u32[]{:S(2)}, u32[]{:S(2)}) %all-to-all-start) | async-done | bytes 1048608 | tf_op jit(solution)/shard_map/all_to_all | solution.py:37
  35.2 11.3 %all-to-all-start.1 = ((bf16[16,4,8,512]{3,2,1,0:T(8,128)(2,1)}), bf16[16,4,8,512]{3,2,1,0:T(8,128)(2,1)}, u32[]{:S(2)}, u32[]{:S(2)}) async-start(bf16[16,4,8,512]{3,2,1,0:T(8,128)(2,1)} %copy-done.26), calls=%async_computation.1 | async-start | bytes 1048576 | tf_op jit(solution)/shard_map/all_to_all | solution.py:37
  46.6 1.9 collective-permute-start.1
  48.5 1.6 shard_map.109
  50.1 1.3 copy-done.13
  51.4 1.6 shard_map.112
  53.0 1.0 copy-done.4
  54.8 9.0 %all-to-all-done.1.own_ref = bf16[16,4,8,512]{3,2,1,0:T(8,128)(2,1)} async-done(((bf16[16,4,8,512]{3,2,1,0:T(8,128)(2,1)}), bf16[16,4,8,512]{3,2,1,0:T(8,128)(2,1)}, u32[]{:S(2)}, u32[]{:S(2)}) %all-to-all-start.1) | async-done | bytes 524320 | tf_op jit(solution)/shard_map/all_to_all | solution.py:37
  63.8 5.3 %all-to-all-start.2 = ((bf16[16,2,4,8,512]{4,3,2,1,0:T(8,128)(2,1)}), bf16[16,2,4,8,512]{4,3,2,1,0:T(8,128)(2,1)S(1)}, u32[]{:S(2)}, u32[]{:S(2)}) async-start(bf16[16,2,4,8,512]{4,3,2,1,0:T(8,128)(2,1)} %copy-done.4), calls=%async_computation.2 | async-start | bytes 2097152 | tf_op jit(solution)/shard_map/all_to_all | solution.py:37
  69.1 1.1 collective-permute-start
  70.1 1.9 collective-permute-done
  72.0 22.8 %all-to-all-done.2.mid_ref = bf16[16,2,4,8,512]{4,3,2,1,0:T(8,128)(2,1)S(1)} async-done(((bf16[16,2,4,8,512]{4,3,2,1,0:T(8,128)(2,1)}), bf16[16,2,4,8,512]{4,3,2,1,0:T(8,128)(2,1)S(1)}, u32[]{:S(2)}, u32[]{:S(2)}) %all-to-all-start.2) | async-done | bytes 1048608 | tf_op jit(solution)/shard_map/all_to_all | solution.py:37
  94.8 6.2 %all-to-all-start.3 = ((bf16[16,4,8,512]{3,2,1,0:T(8,128)(2,1)}), bf16[16,4,8,512]{3,2,1,0:T(8,128)(2,1)}, u32[]{:S(2)}, u32[]{:S(2)}) async-start(bf16[16,4,8,512]{3,2,1,0:T(8,128)(2,1)} %collective-permute-done), calls=%async_computation.3 | async-start | bytes 1048576 | tf_op jit(solution)/shard_map/all_to_all | solution.py:37
  101.0 1.3 collective-permute-start.5
  102.4 11.9 %all-to-all-done.3.oth_ref = bf16[16,4,8,512]{3,2,1,0:T(8,128)(2,1)} async-done(((bf16[16,4,8,512]{3,2,1,0:T(8,128)(2,1)}), bf16[16,4,8,512]{3,2,1,0:T(8,128)(2,1)}, u32[]{:S(2)}, u32[]{:S(2)}) %all-to-all-start.3) | async-done | bytes 524320 | tf_op jit(solution)/shard_map/all_to_all | solution.py:37
  114.3 1.6 copy-done.14
  115.8 2.5 %shard_map.113 = bf16[16,2,4,8,512]{4,3,2,1,0:T(8,128)(2,1)S(1)} custom-call(s32[1]{0:T(128)} %bitcast.core_ref, bf16[1024,1024]{1,0:T(8,128)(2,1)S(1)} %copy-done.14, bf16[16,4,8,512]{3,2,1,0:T(8,128)(2,1)} %all-to-all-done.1.own_ref, bf16[16,4,8,512]{3,2,1,0:T(8,128)(2,1)} %all-to-all-done.3.oth_ref), custom_call_target="tpu_custom_call" | custom-call | flops 1073741824 | bytes 4194304 | tf_op jit(solution)/shard_map/pallas_call | solution.py:59
  118.4 1.0 copy-done.3
  119.4 6.5 %all-to-all-start.4 = ((bf16[16,2,4,8,512]{4,3,2,1,0:T(8,128)(2,1)}), bf16[16,2,4,8,512]{4,3,2,1,0:T(8,128)(2,1)}, u32[]{:S(2)}, u32[]{:S(2)}) async-start(bf16[16,2,4,8,512]{4,3,2,1,0:T(8,128)(2,1)} %copy-done.3), calls=%async_computation.4 | async-start | bytes 2097152 | tf_op jit(solution)/shard_map/all_to_all | solution.py:37
  125.9 1.0 copy-done.11
  126.9 1.2 copy-done.18
  128.1 4.9 %shard_map.116 = (bf16[128,1024]{1,0:T(8,128)(2,1)S(1)}, bf16[128,1024]{1,0:T(8,128)(2,1)}, bf16[128,1024]{1,0:T(8,128)(2,1)}, f32[128,1024]{1,0:T(8,128)S(1)}) custom-call(s32[1]{0:T(128)} %bitcast.3.x_ref, bf16[16,2,4,8,512]{4,3,2,1,0:T(8,128)(2,1)S(1)} %all-to-all-done.2.mid_ref, bf16[16,4,8,512]{3,2,1,0:T(8,128)(2,1)S(1)} %copy-done.11, ...), custom_call_target="tpu_custom_call" | custom-call | flops 1073741824 | bytes 5242880 | tf_op jit(solution)/shard_map/pallas_call | solution.py:59
  133.8 1.2 collective-permute-start.6
  135.0 1.5 collective-permute-start.7
  136.5 1.5 collective-permute-start.8
  138.0 3.4 %collective-permute-done.6 = bf16[128,1024]{1,0:T(8,128)(2,1)} collective-permute-done((bf16[128,1024]{1,0:T(8,128)(2,1)}, bf16[128,1024]{1,0:T(8,128)(2,1)}, u32[]{:S(2)}, u32[]{:S(2)}) %collective-permute-start.6) | collective-permute-done | bytes 262176 | tf_op jit(solution)/shard_map/ppermute | solution.py:33
  141.4 6.6 %collective-permute-done.8 = bf16[128,1024]{1,0:T(8,128)(2,1)} collective-permute-done((bf16[128,1024]{1,0:T(8,128)(2,1)S(1)}, bf16[128,1024]{1,0:T(8,128)(2,1)}, u32[]{:S(2)}, u32[]{:S(2)}) %collective-permute-start.8) | collective-permute-done | bytes 262176 | tf_op jit(solution)/shard_map/ppermute | solution.py:33
  148.0 1.4 convert_add_fusion
  150.2 3.8 %shard_map.117 = f32[128,128]{1,0:T(8,128)S(1)} custom-call(s32[1]{0:T(128)} %bitcast.core_ref, bf16[16,4,8,1024]{3,2,1,0:T(8,128)(2,1)S(1)} %copy-done.2, bf16[16,4,8,512]{3,2,1,0:T(8,128)(2,1)S(1)} %copy-done.24, bf16[16,4,8,512]{3,2,1,0:T(8,128)(2,1)} %all-to-all-done.1.own_ref, bf16[16,4,8,512]{3,2,1,0:T(8,128)(2,1)} %all-to-all-done.3.oth_ref), custom_call_target="tpu_custom_call" | custom-call | flops 1073741824 | bytes 2097152 | tf_op jit(solution)/shard_map/pallas_call | solution.py:59
  154.1 2.7 %collective-permute-start.16 = (f32[128,128]{1,0:T(8,128)S(1)}, f32[128,128]{1,0:T(8,128)S(1)}, u32[]{:S(2)}, u32[]{:S(2)}) collective-permute-start(f32[128,128]{1,0:T(8,128)S(1)} %shard_map.117), channel_id=1, source_target_pairs={{0,1},{1,0},{2,3},{3,2},{4,5},{5,4},{6,7},{7,6},{8,9},{9,8},{10,11... | collective-permute-start | bytes 196616 | tf_op jit(solution)/shard_map/ppermute | solution.py:28
  156.8 1.2 collective-permute-start.10
  158.0 1.5 collective-permute-start.11
  159.5 1.5 collective-permute-start.9
  161.0 0.9 collective-permute-start.17
  161.9 2.3 %collective-permute-done.9 = bf16[32,1024]{1,0:T(8,128)(2,1)} collective-permute-done((bf16[32,1024]{1,0:T(8,128)(2,1)S(1)}, bf16[32,1024]{1,0:T(8,128)(2,1)}, u32[]{:S(2)}, u32[]{:S(2)}) %collective-permute-start.9) | collective-permute-done | bytes 65568 | tf_op jit(solution)/shard_map/ppermute | solution.py:33
  164.2 1.0 fusion.2
  166.1 2.3 %collective-permute-done.12 = bf16[32,1024]{1,0:T(8,128)(2,1)S(1)} collective-permute-done((bf16[32,1024]{1,0:T(8,128)(2,1)S(1)}, bf16[32,1024]{1,0:T(8,128)(2,1)S(1)}, u32[]{:S(2)}, u32[]{:S(2)}) %collective-permute-start.12) | collective-permute-done | bytes 65568 | tf_op jit(solution)/shard_map/ppermute | solution.py:28
  168.8 1.3 collective-permute-done.18
  170.1 1.5 collective-permute-start.19
  172.4 3.5 %collective-permute-start.3 = (bf16[16,4,8,512]{3,2,1,0:T(8,128)(2,1)}, bf16[16,4,8,512]{3,2,1,0:T(8,128)(2,1)}, u32[]{:S(2)}, u32[]{:S(2)}) collective-permute-start(bf16[16,4,8,512]{3,2,1,0:T(8,128)(2,1)} %slice_bitcast_fusion), channel_id=1, source_target_pairs={{0,1},{1,0},{2,3},{3,2},{4,5},{5,4},{6,7},{7,6},{8,9},{9,8},{10,11... | collective-permute-start | bytes 1572872 | tf_op jit(solution)/shard_map/ppermute | solution.py:23
  176.1 3.4 %collective-permute-start.14 = (bf16[32,1024]{1,0:T(8,128)(2,1)S(1)}, bf16[32,1024]{1,0:T(8,128)(2,1)}, u32[]{:S(2)}, u32[]{:S(2)}) collective-permute-start(bf16[32,1024]{1,0:T(8,128)(2,1)S(1)} %add_convert_fusion), channel_id=1, source_target_pairs={{0,16},{8,24},{16,0},{24,8},{1,17},{9,25},{17,1},{25,9},{2,18},{10... | collective-permute-start | bytes 196616 | tf_op jit(solution)/shard_map/ppermute | solution.py:28
  179.5 2.4 %collective-permute-start.21 = (f32[128,128]{1,0:T(8,128)S(1)}, f32[128,128]{1,0:T(8,128)S(1)}, u32[]{:S(2)}, u32[]{:S(2)}) collective-permute-start(f32[128,128]{1,0:T(8,128)S(1)} %add.107), channel_id=1, source_target_pairs={{0,4},{2,6},{4,0},{6,2},{1,5},{3,7},{5,1},{7,3},{8,12},{10,14},{12... | collective-permute-start | bytes 196616 | tf_op jit(solution)/shard_map/ppermute | solution.py:28
  182.0 1.9 slice_bitcast_fusion.1
  183.9 3.1 %collective-permute-start.2 = (bf16[16,4,8,512]{3,2,1,0:T(8,128)(2,1)}, bf16[16,4,8,512]{3,2,1,0:T(8,128)(2,1)}, u32[]{:S(2)}, u32[]{:S(2)}) collective-permute-start(bf16[16,4,8,512]{3,2,1,0:T(8,128)(2,1)} %slice_bitcast_fusion.1), channel_id=1, source_target_pairs={{0,1},{1,0},{2,3},{3,2},{4,5},{5,4},{6,7},{7,6},{8,9},{9,8},{10,11... | collective-permute-start | bytes 1572872 | tf_op jit(solution)/shard_map/ppermute | solution.py:23
  187.0 1.4 collective-permute-start.22
  188.4 0.9 add_multiply_fusion
  189.3 6.4 %collective-permute-start.15 = (f32[32,1024]{1,0:T(8,128)S(1)}, f32[32,1024]{1,0:T(8,128)S(1)}, u32[]{:S(2)}, u32[]{:S(2)}) collective-permute-start(f32[32,1024]{1,0:T(8,128)S(1)} %add_multiply_fusion), channel_id=1, source_target_pairs={{0,0},{1,16},{2,1},{3,17},{4,2},{5,18},{6,3},{7,19},{8,32},{9,48},... | collective-permute-start | bytes 393224 | tf_op jit(solution)/shard_map/ppermute | solution.py:411
  195.7 3.0 %collective-permute-start.23 = (f32[128,128]{1,0:T(8,128)S(1)}, f32[128,128]{1,0:T(8,128)S(1)}, u32[]{:S(2)}, u32[]{:S(2)}) collective-permute-start(f32[128,128]{1,0:T(8,128)S(1)} %add.109), channel_id=1, source_target_pairs={{0,16},{8,24},{16,0},{24,8},{1,17},{9,25},{17,1},{25,9},{2,18},{10... | collective-permute-start | bytes 196616 | tf_op jit(solution)/shard_map/ppermute | solution.py:28
  198.7 1.2 copy-done.6
  200.0 1.2 copy-done.8
  201.2 1.0 copy-done.12
  202.2 1.2 copy-done.16
  203.4 1.0 copy-done.22
  204.5 4.7 %shard_map.115 = (bf16[4,128,1024]{2,1,0:T(8,128)(2,1)}, bf16[4,128,1024]{2,1,0:T(8,128)(2,1)}, bf16[4,128,1024]{2,1,0:T(8,128)(2,1)}) custom-call(s32[1]{0:T(128)} %bitcast.core_ref, bf16[16,2,4,8,512]{4,3,2,1,0:T(8,128)(2,1)S(1)} %all-to-all-done.2.mid_ref, bf16[16,4,8,512]{3,2,1,0:T(8,128)(2,1)} %collective-permute-done.3.got_ref, ...), custom_call_target="tpu_custom_call" | custom-call | flops 1073741824 | bytes 10485760 | tf_op jit(solution)/shard_map/pallas_call | solution.py:59
  209.8 3.4 %shard_map.114 = bf16[4,128,1024]{2,1,0:T(8,128)(2,1)} custom-call(s32[1]{0:T(128)} %bitcast.core_ref, bf16[16,2,4,8,512]{4,3,2,1,0:T(8,128)(2,1)} %all-to-all-done.4.mid_ref, bf16[16,4,8,512]{3,2,1,0:T(8,128)(2,1)} %collective-permute-done.2.got_ref), custom_call_target="tpu_custom_call" | custom-call | bytes 4194304 | tf_op jit(solution)/shard_map/pallas_call | solution.py:59
  (82 shorter events, 9.4 us)
Async XLA Ops:
  0.6 12.6 %copy-start = (bf16[1024,1024]{1,0:T(8,128)(2,1)S(1)}, bf16[1024,1024]{1,0:T(8,128)(2,1)}, u32[]{:S(2)}) copy-start(bf16[1024,1024]{1,0:T(8,128)(2,1)} %ff_ref.3) | copy-start | bytes 6291460
  0.6 1.4 copy-start.19
  2.1 1.0 copy-start.9
  3.1 32.2 %all-to-all-start = ((bf16[16,4,8,1024]{3,2,1,0:T(8,128)(2,1)}), bf16[16,4,8,1024]{3,2,1,0:T(8,128)(2,1)S(1)}, u32[]{:S(2)}, u32[]{:S(2)}) async-start(bf16[16,4,8,1024]{3,2,1,0:T(8,128)(2,1)} %copy-done.9), calls=%async_computation | async-start | bytes 2097152 | tf_op jit(solution)/shard_map/all_to_all | solution.py:37
  13.3 1.2 copy-start.5
  14.5 1.2 copy-start.7
  15.7 1.2 copy-start.20
  20.7 0.8 copy-start.10
  21.5 1.0 copy-start.15
  22.5 1.0 copy-start.17
  23.4 0.8 copy-start.21
  24.2 0.8 copy-start.26
  25.0 0.8 copy-start.27
  25.8 22.6 %copy-start.28 = (bf16[128,128]{1,0:T(8,128)(2,1)S(1)}, bf16[128,128]{1,0:T(8,128)(2,1)}, u32[]{:S(2)}) copy-start(bf16[128,128]{1,0:T(8,128)(2,1)} %sf_ref.1) | copy-start | bytes 98308
  35.2 16.2 %copy-start.1 = (bf16[16,4,8,1024]{3,2,1,0:T(8,128)(2,1)}, bf16[16,4,8,1024]{3,2,1,0:T(8,128)(2,1)S(1)}, u32[]{:S(2)}) copy-start(bf16[16,4,8,1024]{3,2,1,0:T(8,128)(2,1)S(1)} %all-to-all-done.own_ref.up_ref) | copy-start | bytes 3145732
  35.2 28.6 %all-to-all-start.1 = ((bf16[16,4,8,512]{3,2,1,0:T(8,128)(2,1)}), bf16[16,4,8,512]{3,2,1,0:T(8,128)(2,1)}, u32[]{:S(2)}, u32[]{:S(2)}) async-start(bf16[16,4,8,512]{3,2,1,0:T(8,128)(2,1)} %copy-done.26), calls=%async_computation.1 | async-start | bytes 1048576 | tf_op jit(solution)/shard_map/all_to_all | solution.py:37
  46.6 4.8 %collective-permute-start.1 = (bf16[16,4,8,512]{3,2,1,0:T(8,128)(2,1)S(1)}, bf16[16,4,8,512]{3,2,1,0:T(8,128)(2,1)S(1)}, u32[]{:S(2)}, u32[]{:S(2)}) collective-permute-start(bf16[16,4,8,512]{3,2,1,0:T(8,128)(2,1)S(1)} %constant_dynamic-slice_fusion), channel_id=1, source_target_pairs={{0,1},{1,0},{2,3},{3,2},{4,5},{5,4},{6,7},{7,6},{8,9},{9,8},{10,11... | collective-permute-start | bytes 1572872 | tf_op jit(solution)/shard_map/ppermute | solution.py:23
  50.1 1.3 copy-start.13
  53.0 1.0 copy-start.4
  54.0 0.8 copy-start.23
  63.8 31.0 %all-to-all-start.2 = ((bf16[16,2,4,8,512]{4,3,2,1,0:T(8,128)(2,1)}), bf16[16,2,4,8,512]{4,3,2,1,0:T(8,128)(2,1)S(1)}, u32[]{:S(2)}, u32[]{:S(2)}) async-start(bf16[16,2,4,8,512]{4,3,2,1,0:T(8,128)(2,1)} %copy-done.4), calls=%async_computation.2 | async-start | bytes 2097152 | tf_op jit(solution)/shard_map/all_to_all | solution.py:37
  69.1 2.9 %collective-permute-start = (bf16[16,4,8,512]{3,2,1,0:T(8,128)(2,1)}, bf16[16,4,8,512]{3,2,1,0:T(8,128)(2,1)}, u32[]{:S(2)}, u32[]{:S(2)}) collective-permute-start(bf16[16,4,8,512]{3,2,1,0:T(8,128)(2,1)} %copy-done.27), channel_id=1, source_target_pairs={{0,1},{1,0},{2,3},{3,2},{4,5},{5,4},{6,7},{7,6},{8,9},{9,8},{10,11... | collective-permute-start | bytes 1572872 | tf_op jit(solution)/shard_map/ppermute | solution.py:23
  94.8 19.4 %all-to-all-start.3 = ((bf16[16,4,8,512]{3,2,1,0:T(8,128)(2,1)}), bf16[16,4,8,512]{3,2,1,0:T(8,128)(2,1)}, u32[]{:S(2)}, u32[]{:S(2)}) async-start(bf16[16,4,8,512]{3,2,1,0:T(8,128)(2,1)} %collective-permute-done), calls=%async_computation.3 | async-start | bytes 1048576 | tf_op jit(solution)/shard_map/all_to_all | solution.py:37
  101.0 24.9 %collective-permute-start.5 = (bf16[16,4,8,1024]{3,2,1,0:T(8,128)(2,1)}, bf16[16,4,8,1024]{3,2,1,0:T(8,128)(2,1)}, u32[]{:S(2)}, u32[]{:S(2)}) collective-permute-start(bf16[16,4,8,1024]{3,2,1,0:T(8,128)(2,1)} %copy-done.17), channel_id=1, source_target_pairs={{0,1},{1,0},{2,3},{3,2},{4,5},{5,4},{6,7},{7,6},{8,9},{9,8},{10,11... | collective-permute-start | bytes 3145736 | tf_op jit(solution)/shard_map/ppermute | solution.py:23
  102.3 23.6 %collective-permute-start.4 = (bf16[16,4,8,512]{3,2,1,0:T(8,128)(2,1)}, bf16[16,4,8,512]{3,2,1,0:T(8,128)(2,1)}, u32[]{:S(2)}, u32[]{:S(2)}) collective-permute-start(bf16[16,4,8,512]{3,2,1,0:T(8,128)(2,1)} %copy-done.21), channel_id=1, source_target_pairs={{0,1},{1,0},{2,3},{3,2},{4,5},{5,4},{6,7},{7,6},{8,9},{9,8},{10,11... | collective-permute-start | bytes 1572872 | tf_op jit(solution)/shard_map/ppermute | solution.py:23
  114.3 1.6 copy-start.14
  118.4 1.0 copy-start.3
  119.4 62.6 %all-to-all-start.4 = ((bf16[16,2,4,8,512]{4,3,2,1,0:T(8,128)(2,1)}), bf16[16,2,4,8,512]{4,3,2,1,0:T(8,128)(2,1)}, u32[]{:S(2)}, u32[]{:S(2)}) async-start(bf16[16,2,4,8,512]{4,3,2,1,0:T(8,128)(2,1)} %copy-done.3), calls=%async_computation.4 | async-start | bytes 2097152 | tf_op jit(solution)/shard_map/all_to_all | solution.py:37
  125.9 1.0 copy-start.11
  126.9 1.2 copy-start.18
  133.0 0.8 copy-start.25
  133.8 7.6 %collective-permute-start.6 = (bf16[128,1024]{1,0:T(8,128)(2,1)}, bf16[128,1024]{1,0:T(8,128)(2,1)}, u32[]{:S(2)}, u32[]{:S(2)}) collective-permute-start(bf16[128,1024]{1,0:T(8,128)(2,1)} %get-tuple-element.39), channel_id=1, source_target_pairs={{0,32},{32,64},{64,96},{96,0},{1,33},{33,65},{65,97},{97,1},{2,34}... | collective-permute-start | bytes 786440 | tf_op jit(solution)/shard_map/ppermute | solution.py:33
  135.0 6.4 %collective-permute-start.7 = (bf16[128,1024]{1,0:T(8,128)(2,1)}, bf16[128,1024]{1,0:T(8,128)(2,1)}, u32[]{:S(2)}, u32[]{:S(2)}) collective-permute-start(bf16[128,1024]{1,0:T(8,128)(2,1)} %get-tuple-element.40), channel_id=1, source_target_pairs={{0,96},{32,0},{64,32},{96,64},{1,97},{33,1},{65,33},{97,65},{2,98}... | collective-permute-start | bytes 786440 | tf_op jit(solution)/shard_map/ppermute | solution.py:33
  136.5 11.5 %collective-permute-start.8 = (bf16[128,1024]{1,0:T(8,128)(2,1)S(1)}, bf16[128,1024]{1,0:T(8,128)(2,1)}, u32[]{:S(2)}, u32[]{:S(2)}) collective-permute-start(bf16[128,1024]{1,0:T(8,128)(2,1)S(1)} %get-tuple-element.41), channel_id=1, source_target_pairs={{0,64},{32,96},{64,0},{96,32},{1,65},{33,97},{65,1},{97,33},{2,66}... | collective-permute-start | bytes 786440 | tf_op jit(solution)/shard_map/ppermute | solution.py:33
  138.0 12.2 %copy-start.2 = (bf16[16,4,8,1024]{3,2,1,0:T(8,128)(2,1)S(1)}, bf16[16,4,8,1024]{3,2,1,0:T(8,128)(2,1)}, u32[]{:S(2)}) copy-start(bf16[16,4,8,1024]{3,2,1,0:T(8,128)(2,1)} %copy-done.1) | copy-start | bytes 3145732
  138.0 12.2 %copy-start.24 = (bf16[16,4,8,512]{3,2,1,0:T(8,128)(2,1)S(1)}, bf16[16,4,8,512]{3,2,1,0:T(8,128)(2,1)}, u32[]{:S(2)}) copy-start(bf16[16,4,8,512]{3,2,1,0:T(8,128)(2,1)} %copy-done.23) | copy-start | bytes 1572868
  149.4 0.8 copy-start.29
  154.1 6.9 %collective-permute-start.16 = (f32[128,128]{1,0:T(8,128)S(1)}, f32[128,128]{1,0:T(8,128)S(1)}, u32[]{:S(2)}, u32[]{:S(2)}) collective-permute-start(f32[128,128]{1,0:T(8,128)S(1)} %shard_map.117), channel_id=1, source_target_pairs={{0,1},{1,0},{2,3},{3,2},{4,5},{5,4},{6,7},{7,6},{8,9},{9,8},{10,11... | collective-permute-start | bytes 196616 | tf_op jit(solution)/shard_map/ppermute | solution.py:28
  156.8 5.1 %collective-permute-start.10 = (bf16[32,1024]{1,0:T(8,128)(2,1)S(1)}, bf16[32,1024]{1,0:T(8,128)(2,1)S(1)}, u32[]{:S(2)}, u32[]{:S(2)}) collective-permute-start(bf16[32,1024]{1,0:T(8,128)(2,1)S(1)} %get-tuple-element.44), channel_id=1, source_target_pairs={{0,2},{2,4},{4,6},{6,0},{1,3},{3,5},{5,7},{7,1},{8,10},{10,12},{12... | collective-permute-start | bytes 196616 | tf_op jit(solution)/shard_map/ppermute | solution.py:33
  158.0 3.9 %collective-permute-start.11 = (bf16[32,1024]{1,0:T(8,128)(2,1)S(1)}, bf16[32,1024]{1,0:T(8,128)(2,1)}, u32[]{:S(2)}, u32[]{:S(2)}) collective-permute-start(bf16[32,1024]{1,0:T(8,128)(2,1)S(1)} %get-tuple-element.43), channel_id=1, source_target_pairs={{0,6},{2,0},{4,2},{6,4},{1,7},{3,1},{5,3},{7,5},{8,14},{10,8},{12,... | collective-permute-start | bytes 196616 | tf_op jit(solution)/shard_map/ppermute | solution.py:33
  159.5 4.7 %collective-permute-start.9 = (bf16[32,1024]{1,0:T(8,128)(2,1)S(1)}, bf16[32,1024]{1,0:T(8,128)(2,1)}, u32[]{:S(2)}, u32[]{:S(2)}) collective-permute-start(bf16[32,1024]{1,0:T(8,128)(2,1)S(1)} %get-tuple-element.42), channel_id=1, source_target_pairs={{0,4},{2,6},{4,0},{6,2},{1,5},{3,7},{5,1},{7,3},{8,12},{10,14},{12... | collective-permute-start | bytes 196616 | tf_op jit(solution)/shard_map/ppermute | solution.py:33
  161.0 4.3 %collective-permute-start.17 = (f32[128,128]{1,0:T(8,128)S(1)}, f32[128,128]{1,0:T(8,128)S(1)}, u32[]{:S(2)}, u32[]{:S(2)}) collective-permute-start(f32[128,128]{1,0:T(8,128)S(1)} %add.103), channel_id=1, source_target_pairs={{0,32},{32,0},{64,96},{96,64},{1,33},{33,1},{65,97},{97,65},{2,34}... | collective-permute-start | bytes 196616 | tf_op jit(solution)/shard_map/ppermute | solution.py:28
  165.2 3.2 %collective-permute-start.12 = (bf16[32,1024]{1,0:T(8,128)(2,1)S(1)}, bf16[32,1024]{1,0:T(8,128)(2,1)S(1)}, u32[]{:S(2)}, u32[]{:S(2)}) collective-permute-start(bf16[32,1024]{1,0:T(8,128)(2,1)S(1)} %fusion.2), channel_id=1, source_target_pairs={{0,128},{128,0},{1,129},{129,1},{2,130},{130,2},{3,131},{131,3},{4... | collective-permute-start | bytes 196616 | tf_op jit(solution)/shard_map/ppermute | solution.py:28
  165.4 4.7 %collective-permute-start.18 = (f32[128,128]{1,0:T(8,128)S(1)}, f32[128,128]{1,0:T(8,128)S(1)}, u32[]{:S(2)}, u32[]{:S(2)}) collective-permute-start(f32[128,128]{1,0:T(8,128)S(1)} %add.104), channel_id=1, source_target_pairs={{0,64},{32,96},{64,0},{96,32},{1,65},{33,97},{65,1},{97,33},{2,66}... | collective-permute-start | bytes 196616 | tf_op jit(solution)/shard_map/ppermute | solution.py:28
  168.5 7.6 %collective-permute-start.13 = (bf16[32,1024]{1,0:T(8,128)(2,1)S(1)}, bf16[32,1024]{1,0:T(8,128)(2,1)S(1)}, u32[]{:S(2)}, u32[]{:S(2)}) collective-permute-start(bf16[32,1024]{1,0:T(8,128)(2,1)S(1)} %add_convert_fusion.1), channel_id=1, source_target_pairs={{0,8},{8,0},{16,24},{24,16},{1,9},{9,1},{17,25},{25,17},{2,10},{10... | collective-permute-start | bytes 196616 | tf_op jit(solution)/shard_map/ppermute | solution.py:28
  170.1 5.9 %collective-permute-start.19 = (f32[128,128]{1,0:T(8,128)S(1)}, f32[128,128]{1,0:T(8,128)S(1)}, u32[]{:S(2)}, u32[]{:S(2)}) collective-permute-start(f32[128,128]{1,0:T(8,128)S(1)} %add.105), channel_id=1, source_target_pairs={{0,128},{128,0},{1,129},{129,1},{2,130},{130,2},{3,131},{131,3},{4... | collective-permute-start | bytes 196616 | tf_op jit(solution)/shard_map/ppermute | solution.py:28
  172.4 26.3 %collective-permute-start.3 = (bf16[16,4,8,512]{3,2,1,0:T(8,128)(2,1)}, bf16[16,4,8,512]{3,2,1,0:T(8,128)(2,1)}, u32[]{:S(2)}, u32[]{:S(2)}) collective-permute-start(bf16[16,4,8,512]{3,2,1,0:T(8,128)(2,1)} %slice_bitcast_fusion), channel_id=1, source_target_pairs={{0,1},{1,0},{2,3},{3,2},{4,5},{5,4},{6,7},{7,6},{8,9},{9,8},{10,11... | collective-permute-start | bytes 1572872 | tf_op jit(solution)/shard_map/ppermute | solution.py:23
  176.0 3.6 %collective-permute-start.20 = (f32[128,128]{1,0:T(8,128)S(1)}, f32[128,128]{1,0:T(8,128)S(1)}, u32[]{:S(2)}, u32[]{:S(2)}) collective-permute-start(f32[128,128]{1,0:T(8,128)S(1)} %add.106), channel_id=1, source_target_pairs={{0,2},{2,0},{4,6},{6,4},{1,3},{3,1},{5,7},{7,5},{8,10},{10,8},{12,... | collective-permute-start | bytes 196616 | tf_op jit(solution)/shard_map/ppermute | solution.py:28
  176.1 12.3 %collective-permute-start.14 = (bf16[32,1024]{1,0:T(8,128)(2,1)S(1)}, bf16[32,1024]{1,0:T(8,128)(2,1)}, u32[]{:S(2)}, u32[]{:S(2)}) collective-permute-start(bf16[32,1024]{1,0:T(8,128)(2,1)S(1)} %add_convert_fusion), channel_id=1, source_target_pairs={{0,16},{8,24},{16,0},{24,8},{1,17},{9,25},{17,1},{25,9},{2,18},{10... | collective-permute-start | bytes 196616 | tf_op jit(solution)/shard_map/ppermute | solution.py:28
  179.5 7.4 %collective-permute-start.21 = (f32[128,128]{1,0:T(8,128)S(1)}, f32[128,128]{1,0:T(8,128)S(1)}, u32[]{:S(2)}, u32[]{:S(2)}) collective-permute-start(f32[128,128]{1,0:T(8,128)S(1)} %add.107), channel_id=1, source_target_pairs={{0,4},{2,6},{4,0},{6,2},{1,5},{3,7},{5,1},{7,3},{8,12},{10,14},{12... | collective-permute-start | bytes 196616 | tf_op jit(solution)/shard_map/ppermute | solution.py:28
  183.9 26.0 %collective-permute-start.2 = (bf16[16,4,8,512]{3,2,1,0:T(8,128)(2,1)}, bf16[16,4,8,512]{3,2,1,0:T(8,128)(2,1)}, u32[]{:S(2)}, u32[]{:S(2)}) collective-permute-start(bf16[16,4,8,512]{3,2,1,0:T(8,128)(2,1)} %slice_bitcast_fusion.1), channel_id=1, source_target_pairs={{0,1},{1,0},{2,3},{3,2},{4,5},{5,4},{6,7},{7,6},{8,9},{9,8},{10,11... | collective-permute-start | bytes 1572872 | tf_op jit(solution)/shard_map/ppermute | solution.py:23
  187.0 8.7 %collective-permute-start.22 = (f32[128,128]{1,0:T(8,128)S(1)}, f32[128,128]{1,0:T(8,128)S(1)}, u32[]{:S(2)}, u32[]{:S(2)}) collective-permute-start(f32[128,128]{1,0:T(8,128)S(1)} %add.108), channel_id=1, source_target_pairs={{0,8},{8,0},{16,24},{24,16},{1,9},{9,1},{17,25},{25,17},{2,10},{10... | collective-permute-start | bytes 196616 | tf_op jit(solution)/shard_map/ppermute | solution.py:28
  189.3 20.0 %collective-permute-start.15 = (f32[32,1024]{1,0:T(8,128)S(1)}, f32[32,1024]{1,0:T(8,128)S(1)}, u32[]{:S(2)}, u32[]{:S(2)}) collective-permute-start(f32[32,1024]{1,0:T(8,128)S(1)} %add_multiply_fusion), channel_id=1, source_target_pairs={{0,0},{1,16},{2,1},{3,17},{4,2},{5,18},{6,3},{7,19},{8,32},{9,48},... | collective-permute-start | bytes 393224 | tf_op jit(solution)/shard_map/ppermute | solution.py:411
  195.7 13.5 %collective-permute-start.23 = (f32[128,128]{1,0:T(8,128)S(1)}, f32[128,128]{1,0:T(8,128)S(1)}, u32[]{:S(2)}, u32[]{:S(2)}) collective-permute-start(f32[128,128]{1,0:T(8,128)S(1)} %add.109), channel_id=1, source_target_pairs={{0,16},{8,24},{16,0},{24,8},{1,17},{9,25},{17,1},{25,9},{2,18},{10... | collective-permute-start | bytes 196616 | tf_op jit(solution)/shard_map/ppermute | solution.py:28
  198.7 1.2 copy-start.6
  200.0 1.2 copy-start.8
  201.2 1.0 copy-start.12
  202.2 1.2 copy-start.16
  203.4 1.0 copy-start.22

commit v2 on v1

v2 whole, which is shorter than its diff:
```python
import math

import jax
import jax.numpy as jnp
from jax import lax
from jax.experimental import pallas as pl
from jax.experimental.pallas import tpu as pltpu
from jax.sharding import Mesh
from jax.sharding import PartitionSpec as P

AXES = ("zl", "x", "zh", "y", "c")
BF = jnp.bfloat16
F32 = jnp.float32
PEERS, LOCAL, ROWS, HALF = 16, 4, 8, 512
CHANNELS, WIDTH = PEERS * ROWS, 2 * HALF
NB = PEERS * 2 * LOCAL
SIDE = PEERS * LOCAL * ROWS
LIMIT = 60 * 1024 * 1024


def swap(value):
    return lax.ppermute(value, "c", [(0, 1), (1, 0)])


def flip(value, axis, bit):
    size = lax.axis_size(axis)
    return lax.ppermute(value, axis, [(i, i ^ bit) for i in range(size)])


def shift(value, axis, step):
    size = lax.axis_size(axis)
    return lax.ppermute(value, axis, [(i, (i + step) % size) for i in range(size)])


def exchange(value):
    return lax.all_to_all(value, ("y", "zh"), 0, 0, tiled=True)


def to_owner(step):
    perm = []
    for zl in range(2):
        for x in range(4):
            for zh in range(4):
                for y in range(4):
                    for c in range(2):
                        place = 16 * c + 4 * x + y
                        source = (((zl * 4 + x) * 4 + zh) * 4 + y) * 2 + c
                        target = (((zl * 4 + (zh ^ step)) * 4 + place // 8) * 4 + place // 2 % 4) * 2 + place % 2
                        perm.append((source, target))
    return perm


def call(body, scalars, operands, in_specs, out_shapes, out_specs, grid=(1,), scratch=()):
    return pl.pallas_call(
        body,
        out_shape=out_shapes,
        grid_spec=pltpu.PrefetchScalarGridSpec(
            num_scalar_prefetch=len(scalars),
            grid=grid,
            in_specs=in_specs,
            out_specs=out_specs,
            scratch_shapes=list(scratch),
        ),
        compiler_params=pltpu.CompilerParams(vmem_limit_bytes=LIMIT),
        cost_estimate=pl.CostEstimate(flops=1 << 10, bytes_accessed=1 << 10, transcendentals=0),
    )(*scalars, *operands)


def whole(shape):
    return pl.BlockSpec(shape, lambda *_: (0,) * len(shape))


def struct(shape, dtype=BF):
    return jax.ShapeDtypeStruct(shape, dtype)


def sigmoid(gates):
    return jax.nn.sigmoid(gates.astype(F32))


def pack_body(in_ref, out_ref):
    for b in range(LOCAL):
        out_ref[:, b] = in_ref[b].reshape(PEERS, ROWS, WIDTH)


def pack(value):
    return call(
        pack_body,
        (),
        (value,),
        [whole((LOCAL, CHANNELS, WIDTH))],
        struct((PEERS, LOCAL, ROWS, WIDTH)),
        whole((PEERS, LOCAL, ROWS, WIDTH)),
    )


def placed(n, core):
    rel = n // SIDE
    real = rel + core - 2 * rel * core
    peer = (n // (LOCAL * ROWS)) % PEERS
    return (peer % 4 * 4 + peer // 4) * (2 * LOCAL) + real * LOCAL + (n // ROWS) % LOCAL


def widen_body(at_ref, sf_ref, wide_ref, turned_ref):
    core = at_ref[0]
    size = 2 * SIDE
    n = lax.broadcasted_iota(jnp.int32, (size, NB), 0)
    o = lax.broadcasted_iota(jnp.int32, (size, NB), 1)
    pick = jnp.where(placed(n, core) == o, 1.0, 0.0).astype(BF)
    row = lax.broadcasted_iota(jnp.int32, (size, size), 0) % ROWS
    column = lax.broadcasted_iota(jnp.int32, (size, size), 1) % ROWS
    same = row == column
    for ref, dim in ((wide_ref, 0), (turned_ref, 1)):
        tall = lax.dot_general(pick, sf_ref[...], (((1,), (dim,)), ((), ())), preferred_element_type=F32)
        full = lax.dot_general(tall.astype(BF), pick, (((1,), (1,)), ((), ())), preferred_element_type=F32)
        ref[...] = jnp.where(same, full, 0.0).astype(BF)


def widen(at, sf):
    shape = (2 * SIDE, 2 * SIDE)
    return call(
        widen_body,
        (at,),
        (sf,),
        [whole((NB, NB))],
        [struct(shape), struct(shape)],
        [whole(shape), whole(shape)],
    )


GROUP = 4
STEP_ROWS = GROUP * LOCAL * ROWS


def forward_body(
    core_ref, in_ref, gate_ref, kernel_ref, ff_ref, mixed_ref, blocks_ref, own_ref, oth_ref, kown_ref, koth_ref, flat
):
    core = core_ref[0]
    for b in range(LOCAL):
        mixed = (in_ref[b].astype(F32) * sigmoid(gate_ref[b])).astype(BF)
        for g in range(GROUP):
            piece = mixed[g * ROWS : (g + 1) * ROWS]
            mixed_ref[g, b] = piece
            flat[(g * LOCAL + b) * ROWS : (g * LOCAL + b + 1) * ROWS] = piece
    blocks = lax.dot_general(flat[...], ff_ref[...], (((1,), (1,)), ((), ())), preferred_element_type=F32)
    blocks = blocks.astype(BF).reshape(GROUP, LOCAL, ROWS, WIDTH)
    blocks_ref[...] = blocks
    for b in range(LOCAL):
        weight = kernel_ref[b].reshape(GROUP, ROWS, WIDTH)
        kern = (blocks[:, b].astype(F32) * weight.astype(F32)).astype(BF)
        low, high = kern[..., :HALF], kern[..., HALF:]
        own_ref[:, b] = jnp.where(core == 0, low, high)
        oth_ref[:, b] = jnp.where(core == 0, high, low)
        low, high = weight[..., :HALF], weight[..., HALF:]
        kown_ref[:, b] = jnp.where(core == 0, low, high)
        koth_ref[:, b] = jnp.where(core == 0, high, low)


def natural_spec():
    return pl.BlockSpec((LOCAL, GROUP * ROWS, WIDTH), lambda i, *_: (0, i, 0))


def rows_spec(width):
    return pl.BlockSpec((GROUP, LOCAL, ROWS, width), lambda i, *_: (i, 0, 0, 0))


def forward(core, inputs, gates, kernel, ff):
    full, part = struct((PEERS, LOCAL, ROWS, WIDTH)), struct((PEERS, LOCAL, ROWS, HALF))
    return call(
        forward_body,
        (core,),
        (inputs, gates, kernel, ff),
        [natural_spec()] * 3 + [whole((WIDTH, WIDTH))],
        [full, full, part, part, part, part],
        [rows_spec(WIDTH)] * 2 + [rows_spec(HALF)] * 4,
        grid=(PEERS // GROUP,),
        scratch=[pltpu.VMEM((STEP_ROWS, WIDTH), BF)],
    )


CHUNK = 256


STEPS = HALF // CHUNK


def across_body(at_ref, wide_ref, own_ref, oth_ref, out_ref):
    own = own_ref[...].reshape(SIDE, CHUNK)
    oth = oth_ref[...].reshape(SIDE, CHUNK)
    total = jnp.dot(wide_ref[:, :SIDE], own, preferred_element_type=F32)
    total = total + jnp.dot(wide_ref[:, SIDE:], oth, preferred_element_type=F32)
    total = total.astype(BF)
    for rel in range(2):
        out_ref[:, rel] = total[rel * SIDE : (rel + 1) * SIDE].reshape(PEERS, LOCAL, ROWS, CHUNK)


def across(at, wide, own, oth, own_spec, oth_spec):
    return call(
        across_body,
        (at,),
        (wide, own, oth),
        [whole((2 * SIDE, 2 * SIDE)), own_spec, oth_spec],
        struct((PEERS, 2, LOCAL, ROWS, HALF)),
        pl.BlockSpec((PEERS, 2, LOCAL, ROWS, CHUNK), lambda i, at: (0, 0, 0, 0, i)),
        grid=(STEPS,),
    )


def across_up(at, wide, up, up_oth):
    block = (PEERS, LOCAL, ROWS, CHUNK)
    own = pl.BlockSpec(block, lambda i, at: (0, 0, 0, at[0] * STEPS + i))
    return across(at, wide, up, up_oth, own, pl.BlockSpec(block, lambda i, at: (0, 0, 0, i)))


def across_kern(at, wide, kern):
    block = (PEERS, 1, LOCAL, ROWS, CHUNK)
    own = pl.BlockSpec(block, lambda i, at: (0, 0, 0, 0, i))
    return across(at, wide, kern, kern, own, pl.BlockSpec(block, lambda i, at: (0, 1, 0, 0, i)))


def second_body(at_ref, up_ref, up_oth_ref, kern_ref, out_ref):
    core = at_ref[0]
    row = lax.broadcasted_iota(jnp.int32, (SIDE, SIDE), 0) % ROWS
    column = lax.broadcasted_iota(jnp.int32, (SIDE, SIDE), 1) % ROWS
    same = row == column
    tall = []
    for ref in (up_ref, up_oth_ref):
        up = ref[...].reshape(SIDE, HALF)
        wide = []
        for rel in range(2):
            kern = kern_ref[:, rel].reshape(SIDE, HALF)
            full = lax.dot_general(up, kern, (((1,), (1,)), ((), ())), preferred_element_type=F32)
            wide.append(jnp.where(same, full, 0.0).reshape(SIDE // ROWS, ROWS, SIDE).sum(1))
        tall.append(jnp.concatenate(wide, 1))
    tall = jnp.concatenate(tall, 0)
    n = lax.broadcasted_iota(jnp.int32, (2 * SIDE, NB), 0)
    o = lax.broadcasted_iota(jnp.int32, (2 * SIDE, NB), 1)
    pick = jnp.where(placed(n, core) == o, 1.0, 0.0)
    total = jnp.dot(tall, pick, precision=lax.Precision.HIGHEST, preferred_element_type=F32)
    n = lax.broadcasted_iota(jnp.int32, (NB, NB), 1) * ROWS
    o = lax.broadcasted_iota(jnp.int32, (NB, NB), 0)
    pick = jnp.where(placed(n, core) == o, 1.0, 0.0)
    out_ref[...] = jnp.dot(pick, total, precision=lax.Precision.HIGHEST, preferred_element_type=F32)


def second(at, up, up_oth, kern):
    block = (PEERS, LOCAL, ROWS, HALF)
    return call(
        second_body,
        (at,),
        (up, up_oth, kern),
        [pl.BlockSpec(block, lambda i, at: (0, 0, 0, at[0])), whole(block), whole(kern.shape)],
        struct((NB, NB), F32),
        whole((NB, NB)),
    )


SHARE = HALF // 4
PACKED = WIDTH + NB


def first_body(x_ref, core_ref, mid_ref, kown_ref, koth_ref, own_ref, oth_ref, second_ref, *out_refs):
    total = 0.0
    for rel, (weight, mixed) in enumerate(((kown_ref, own_ref), (koth_ref, oth_ref))):
        grad = mid_ref[:, rel].reshape(SIDE, SHARE) * weight[...].reshape(SIDE, SHARE)
        total = total + lax.dot_general(
            grad,
            mixed[...].reshape(SIDE, WIDTH),
            (((0,), (0,)), ((), ())),
            preferred_element_type=F32,
        )
    chunk = lax.rem(x_ref[0] + turn(pl.program_id(0)), 4)
    terms = second_ref[pl.ds(pl.multiple_of(core_ref[0] * (NB // 2) + chunk * (NB // 8), NB // 8), NB // 8), :]
    blank = jnp.zeros((SHARE // 4 - LOCAL, NB), F32)
    terms = [piece for y in range(4) for piece in (terms[y * LOCAL : (y + 1) * LOCAL], blank)]
    terms = jnp.concatenate(terms, 0)
    for step, ref in enumerate(out_refs):

        @pl.when(pl.program_id(0) == step)
        def _():
            ref[:, :WIDTH] = total.astype(ref.dtype)
            ref[:, WIDTH:] = terms.astype(ref.dtype)


def turn(i):
    return jnp.where(i == 0, 2, jnp.where(i == 2, 3, jnp.where(i == 1, 1, 0)))


def first_terms(x, core, mid, kown, koth, own, oth, terms):
    def chunk(i, x):
        return lax.rem(x[0] + turn(i), 4)

    weight = pl.BlockSpec((PEERS, LOCAL, ROWS, SHARE), lambda i, x, core: (0, 0, 0, chunk(i, x)))
    mixed = whole((PEERS, LOCAL, ROWS, WIDTH))
    out = (SHARE, PACKED)
    return call(
        first_body,
        (x, core),
        (mid, kown, koth, own, oth, terms),
        [pl.BlockSpec((PEERS, 2, LOCAL, ROWS, SHARE), lambda i, x, core: (0, 0, 0, 0, chunk(i, x))), weight, weight]
        + [mixed, mixed, whole((NB, NB))],
        [struct(out), struct(out), struct(out), struct(out, F32)],
        [whole(out)] * 4,
        grid=(4,),
    )


def grads_body(
    core_ref, mid_ref, got_ref, blocks_ref, kown_ref, koth_ref, in_ref, gate_ref, ff_ref, gin_ref, ggate_ref, gkern_ref
):
    core = core_ref[0]
    own = pl.ds(pl.multiple_of(core * HALF, HALF), HALF)
    oth = pl.ds(pl.multiple_of((1 - core) * HALF, HALF), HALF)
    total = 0.0
    for at, mid, weight in ((own, mid_ref[:, 0], kown_ref), (oth, got_ref[...], koth_ref)):
        grad = mid * blocks_ref[:, :, :, at]
        for b in range(LOCAL):
            gkern_ref[b, :, at] = grad[:, b].reshape(GROUP * ROWS, HALF)
        grad = (mid * weight[...]).reshape(STEP_ROWS, HALF)
        total = total + jnp.dot(grad, ff_ref[at, :], preferred_element_type=F32)
    total = total.reshape(GROUP, LOCAL, ROWS, WIDTH)
    for b in range(LOCAL):
        grad = total[:, b].reshape(GROUP * ROWS, WIDTH)
        sig = sigmoid(gate_ref[b])
        gin_ref[b] = (grad * sig).astype(BF)
        ggate_ref[b] = (grad * in_ref[b].astype(F32) * sig * (1.0 - sig)).astype(BF)


def grads(core, mid, got, blocks, kown, koth, inputs, gates, ff):
    out = struct((LOCAL, CHANNELS, WIDTH))
    return call(
        grads_body,
        (core,),
        (mid, got, blocks, kown, koth, inputs, gates, ff),
        [
            pl.BlockSpec((GROUP, 1, LOCAL, ROWS, HALF), lambda i, *_: (i, 0, 0, 0, 0)),
            rows_spec(HALF),
            rows_spec(WIDTH),
            rows_spec(HALF),
            rows_spec(HALF),
            natural_spec(),
            natural_spec(),
            whole((WIDTH, WIDTH)),
        ],
        [out, out, out],
        [natural_spec()] * 3,
        grid=(PEERS // GROUP,),
    )


def join_body(core_ref, mid_ref, got_ref, out_ref):
    core = core_ref[0]
    own = pl.ds(pl.multiple_of(core * HALF, HALF), HALF)
    oth = pl.ds(pl.multiple_of((1 - core) * HALF, HALF), HALF)
    for b in range(LOCAL):
        out_ref[b, :, own] = mid_ref[:, 0, b].reshape(GROUP * ROWS, HALF)
        out_ref[b, :, oth] = got_ref[:, b].reshape(GROUP * ROWS, HALF)


def join(core, mid, got):
    return call(
        join_body,
        (core,),
        (mid, got),
        [pl.BlockSpec((GROUP, 1, LOCAL, ROWS, HALF), lambda i, *_: (i, 0, 0, 0, 0)), rows_spec(HALF)],
        struct((LOCAL, CHANNELS, WIDTH)),
        natural_spec(),
        grid=(PEERS // GROUP,),
    )


def on_device(inputs, gates, kernel, first_factor, second_factor, upstream):
    core, x, y = (lax.axis_index(axis).astype(jnp.int32) for axis in ("c", "x", "y"))
    x_at, at = x.reshape(1), core.reshape(1)
    all_channels = CHANNELS * lax.axis_size("zl") * lax.axis_size("x")

    up = exchange(pack(upstream))
    mixed, blocks, kern_own, kern_oth, kown, koth = forward(at, inputs, gates, kernel, first_factor)
    kern = jnp.stack([kern_own, swap(kern_oth)], 1)
    wide, turned = widen(at, second_factor)
    up, kern, wide, turned = lax.optimization_barrier((up, kern, wide, turned))

    kern = exchange(kern)
    up_oth = swap(lax.dynamic_slice_in_dim(up, (1 - core) * HALF, HALF, 3))
    mid = across_up(at, turned, up, up_oth)
    koth_got = swap(koth)
    mixed_got = swap(mixed)
    mid, kern, koth_got, mixed_got = lax.optimization_barrier((mid, kern, koth_got, mixed_got))

    mid = exchange(mid)
    out = across_kern(at, wide, kern)

    terms = second(at, up, up_oth, kern)
    terms = terms + swap(terms)
    mid, out, terms = lax.optimization_barrier((mid, out, terms))
    out = exchange(out)

    sent2, sent1, sent3, total = first_terms(x_at, at, mid, kown, koth_got, mixed, mixed_got, terms)
    got = [shift(sent2, "x", 2), shift(sent1, "x", 1), shift(sent3, "x", 3)]
    mid_got = swap(mid[:, 1])
    others = grads(at, mid, mid_got, blocks, kown, koth, inputs, gates, first_factor)
    total, *others = lax.optimization_barrier((total, *others))

    total = total + got[1].astype(F32) + got[2].astype(F32) + got[0].astype(F32)
    total = total.reshape(4, SHARE // 4, PACKED)
    parts = total.astype(BF)
    got = [shift(lax.dynamic_index_in_dim(parts, lax.rem(y + step, 4), 0, False), "y", step) for step in (2, 1, 3)]
    total = lax.dynamic_index_in_dim(total, y, 0, False)
    for part in got:
        total = total + part.astype(F32)
    part = total.astype(BF)
    near = flip(part, "zl", 1)
    output = join(at, out, swap(out[:, 1]))
    part, output = lax.optimization_barrier((part, output))
    part = (part.astype(F32) + near.astype(F32)).astype(BF)
    got = [lax.ppermute(part, AXES, to_owner(step)).astype(F32) for step in range(4)]
    total = (got[0] + got[1]) + (got[2] + got[3])
    grad_first = total[:, :WIDTH] * (1.0 / math.sqrt(NB * all_channels))
    grad_second = total[:LOCAL, WIDTH:] * (1.0 / math.sqrt(all_channels * WIDTH))
    return (output, *others, grad_first, grad_second)


def solution(mesh):
    fine = Mesh(mesh.devices.reshape(2, 4, 4, 4, 2), AXES)
    seq, dp = ("zh", "y", "c"), ("zl", "x")
    big = P(seq, dp, None)
    return jax.shard_map(
        on_device,
        mesh=fine,
        in_specs=(big, big, big, P(), P(), big),
        out_specs=(big, big, big, big, P(seq, None), P(seq, None)),
        check_vma=False,
    )
```

time: 217 us -> 180 us (0.83)
  local copies, waits for them, and re-layouts: 29.8 us -> 4.04 us
  waiting for transfers between devices: 70.9 us -> 51.2 us
  Pallas kernels: 26.4 us -> 41.7 us
  starting transfers between devices: 81.9 us -> 73.9 us
    unnamed x61 -> x24, local copies, waits for them, and re-layouts: 27 us -> 3.9 us
    all_to_all x5 -> x4, waiting for transfers between devices: 53.1 us -> 31.7 us  [exchange(): return lax.all_to_all(value, ('y', 'zh'), 0, 0, tiled=True)]
    pallas_call x9, Pallas kernels: 26.4 us -> 41.7 us  [call(): pl.pallas_call(body, out_shape=out_shapes, grid_spec=pltpu.PrefetchScalar...]
    ppermute x11 -> x1, starting transfers between devices: 16.8 us -> 3.08 us  [flip(): return lax.ppermute(value, axis, [(i, i ^ bit) for i in range(size)])]
    ppermute x1 -> x4, waiting for transfers between devices: 0.01 us -> 10.7 us  [on_device(): lax.ppermute(part, AXES, to_owner(step)).astype(F32)]
    ppermute x1 -> x4, starting transfers between devices: 6.39 us -> 15.8 us  [on_device(): lax.ppermute(part, AXES, to_owner(step)).astype(F32)]
    ppermute x6, waiting for transfers between devices: 12.3 us -> 5.73 us  [shift(): lax.ppermute(value, axis, [(i, (i + step) % size) for i in range(size)])]
    all_to_all x5 -> x4, starting transfers between devices: 39.4 us -> 35.2 us  [exchange(): return lax.all_to_all(value, ('y', 'zh'), 0, 0, tiled=True)]
  transfers between devices with their start and end apart: 29 -> 22, of which waited for: 10 -> 8; matrix products, arithmetic and copies ran while one was open for 3% -> 2% of each run, Pallas kernels for 11% -> 22%
where the time goes in v2:
time: 180 us; the launch traced here: 177 us
  starting transfers between devices  73.9 us (41%)
  waiting for transfers between devices  51.2 us (28%)
  Pallas kernels  41.7 us (23%)
  other arithmetic  5.48 us (3%)
  local copies, waits for them, and re-layouts  4.04 us (2%)
    pallas_call x9, Pallas kernels, call(): pl.pallas_call(body, out_shape=out_shapes, grid_spec=pltpu.PrefetchScalar...  41.7 us
    all_to_all x4, starting transfers between devices, exchange(): return lax.all_to_all(value, ('y', 'zh'), 0, 0, tiled=True)  35.2 us
    all_to_all x4, waiting for transfers between devices, exchange(): return lax.all_to_all(value, ('y', 'zh'), 0, 0, tiled=True)  31.7 us
    ppermute x4, starting transfers between devices, on_device(): lax.ppermute(part, AXES, to_owner(step)).astype(F32)  15.8 us
    ppermute x7, starting transfers between devices, swap(): return lax.ppermute(value, 'c', [(0, 1), (1, 0)])  11.4 us
    ppermute x4, waiting for transfers between devices, on_device(): lax.ppermute(part, AXES, to_owner(step)).astype(F32)  10.7 us
    ppermute x6, starting transfers between devices, shift(): lax.ppermute(value, axis, [(i, (i + step) % size) for i in range(size)])  8.43 us
    ppermute x6, waiting for transfers between devices, shift(): lax.ppermute(value, axis, [(i, (i + step) % size) for i in range(size)])  5.73 us
  transfers between devices with their start and end apart: 22, of which 8 were waited for; matrix products, arithmetic and copies ran while one was open for 2% of the time, Pallas kernels for 22%

profile of v2, /device:TPU:65, one launch (start us, length us, event | category | flops | bytes accessed | tf_op | source)
XLA Modules:
  0.0 177.1 jit_solution(14051900029701866650)
XLA Ops:
  0.6 2.3 %shard_map.109 = bf16[16,4,8,1024]{3,2,1,0:T(8,128)(2,1)} custom-call(bf16[4,128,1024]{2,1,0:T(8,128)(2,1)} %in_ref.3), custom_call_target="tpu_custom_call" | custom-call | flops 1024 | bytes 1024 | tf_op jit(solution)/shard_map/pallas_call | solution.py:54
  2.9 10.2 %all-to-all-start = ((bf16[16,4,8,1024]{3,2,1,0:T(8,128)(2,1)}), bf16[16,4,8,1024]{3,2,1,0:T(8,128)(2,1)S(1)}, u32[]{:S(2)}, u32[]{:S(2)}) async-start(bf16[16,4,8,1024]{3,2,1,0:T(8,128)(2,1)} %shard_map.109), calls=%async_computation | async-start | bytes 2097152 | tf_op jit(solution)/shard_map/all_to_all | solution.py:36
  13.1 6.8 %shard_map.110 = (bf16[16,4,8,1024]{3,2,1,0:T(8,128)(2,1)}, bf16[16,4,8,1024]{3,2,1,0:T(8,128)(2,1)}, bf16[16,4,8,512]{3,2,1,0:T(8,128)(2,1)}, bf16[16,4,8,512]{...) custom-call(s32[1]{0:T(128)} %bitcast.1.core_ref.at_ref, ...), custom_call_target="tpu_custom_call" | custom-call | flops 1024 | bytes 1024 | tf_op jit(solution)/shard_map/pallas_call | solution.py:54
  19.9 1.3 collective-permute-start
  21.2 3.9 %shard_map.111 = (bf16[1024,1024]{1,0:T(8,128)(2,1)}, bf16[1024,1024]{1,0:T(8,128)(2,1)}) custom-call(s32[1]{0:T(128)} %bitcast.1.core_ref.at_ref, bf16[128,128]{1,0:T(8,128)(2,1)} %sf_ref.1), custom_call_target="tpu_custom_call" | custom-call | flops 1024 | bytes 1024 | tf_op jit(solution)/shard_map/pallas_call | solution.py:54
  25.1 0.0 collective-permute-done
  25.1 2.2 %pad_maximum_fusion = bf16[16,2,4,8,512]{4,3,2,1,0:T(8,128)(2,1)} fusion(bf16[16,1,4,8,512]{4,3,2,1,0:T(8,128)(2,1)S(1)} %bitcast.28, bf16[16,1,4,8,512]{4,3,2,1,0:T(8,128)(2,1)} %bitcast.27), kind=kLoop, calls=%fused_computation | loop fusion | flops 524288 | bytes 2097152 | tf_op jit(solution)/shard_map/stack | solution.py:379
  27.3 12.3 %all-to-all-done.own_ref.up_ref = bf16[16,4,8,1024]{3,2,1,0:T(8,128)(2,1)S(1)} async-done(((bf16[16,4,8,1024]{3,2,1,0:T(8,128)(2,1)}), bf16[16,4,8,1024]{3,2,1,0:T(8,128)(2,1)S(1)}, u32[]{:S(2)}, u32[]{:S(2)}) %all-to-all-start) | async-done | bytes 1048608 | tf_op jit(solution)/shard_map/all_to_all | solution.py:36
  39.5 6.3 %all-to-all-start.1 = ((bf16[16,2,4,8,512]{4,3,2,1,0:T(8,128)(2,1)}), bf16[16,2,4,8,512]{4,3,2,1,0:T(8,128)(2,1)S(1)}, u32[]{:S(2)}, u32[]{:S(2)}) async-start(bf16[16,2,4,8,512]{4,3,2,1,0:T(8,128)(2,1)} %pad_maximum_fusion), calls=%async_computation.1 | async-start | bytes 2097152 | tf_op jit(solution)/shard_map/all_to_all | solution.py:36
  45.8 2.5 %collective-permute-start.3 = (bf16[16,4,8,1024]{3,2,1,0:T(8,128)(2,1)S(1)}, bf16[16,4,8,1024]{3,2,1,0:T(8,128)(2,1)}, u32[]{:S(2)}, u32[]{:S(2)}) collective-permute-start(bf16[16,4,8,1024]{3,2,1,0:T(8,128)(2,1)S(1)} %copy-done.5), channel_id=1, source_target_pairs={{0,1},{1,0},{2,3},{3,2},{4,5},{5,4},{6,7},{7,6},{8,9},{9,8},{10,11... | collective-permute-start | bytes 3145736 | tf_op jit(solution)/shard_map/ppermute | solution.py:22
  48.4 0.1 collective-permute-start.1
  48.5 0.5 collective-permute-start.2
  49.0 3.1 %collective-permute-done.1.oth_ref.up_oth_ref = bf16[16,4,8,512]{3,2,1,0:T(8,128)(2,1)S(1)} collective-permute-done((bf16[16,4,8,512]{3,2,1,0:T(8,128)(2,1)S(1)}, bf16[16,4,8,512]{3,2,1,0:T(8,128)(2,1)S(1)}, u32[]{:S(2)}, u32[]{:S(2)}) %collective-permute-start.1) | collective-permute-done | bytes 524320 | tf_op jit(solution)/shard_map/ppermute | solution.py:22
  52.1 0.0 copy-done.2
  52.1 0.8 copy-done.4
  52.9 4.0 %shard_map.112 = bf16[16,2,4,8,512]{4,3,2,1,0:T(8,128)(2,1)} custom-call(s32[1]{0:T(128)} %bitcast.1.core_ref.at_ref, bf16[1024,1024]{1,0:T(8,128)(2,1)} %get-tuple-element.42.wide_ref, bf16[16,4,8,1024]{3,2,1,0:T(8,128)(2,1)} %copy-done.2, bf16[16,4,8,512]{3,2,1,0:T(8,128)(2,1)} %copy-done.4), custom_call_target="tpu_custom_call" | custom-call | flops 1024 | bytes 1024 | tf_op jit(solution)/shard_map/pallas_call | solution.py:54
  57.0 0.0 collective-permute-done.2.koth_ref
  57.0 0.0 collective-permute-done.3.oth_ref
  57.0 10.5 %all-to-all-done.1.own_ref.oth_ref.kern_ref = bf16[16,2,4,8,512]{4,3,2,1,0:T(8,128)(2,1)S(1)} async-done(((bf16[16,2,4,8,512]{4,3,2,1,0:T(8,128)(2,1)}), bf16[16,2,4,8,512]{4,3,2,1,0:T(8,128)(2,1)S(1)}, u32[]{:S(2)}, u32[]{:S(2)}) %all-to-all-start.1) | async-done | bytes 1048608 | tf_op jit(solution)/shard_map/all_to_all | solution.py:36
  67.5 8.9 %all-to-all-start.2 = ((bf16[16,2,4,8,512]{4,3,2,1,0:T(8,128)(2,1)}), bf16[16,2,4,8,512]{4,3,2,1,0:T(8,128)(2,1)S(1)}, u32[]{:S(2)}, u32[]{:S(2)}) async-start(bf16[16,2,4,8,512]{4,3,2,1,0:T(8,128)(2,1)} %shard_map.112), calls=%async_computation.2 | async-start | bytes 2097152 | tf_op jit(solution)/shard_map/all_to_all | solution.py:36
  76.4 4.9 %shard_map.114 = f32[128,128]{1,0:T(8,128)} custom-call(s32[1]{0:T(128)} %bitcast.1.core_ref.at_ref, bf16[16,4,8,1024]{3,2,1,0:T(8,128)(2,1)} %copy-done.2, bf16[16,4,8,512]{3,2,1,0:T(8,128)(2,1)} %copy-done.4, bf16[16,2,4,8,512]{4,3,2,1,0:T(8,128)(2,1)} %copy-done), custom_call_target="tpu_custom_call" | custom-call | flops 1024 | bytes 1024 | tf_op jit(solution)/shard_map/pallas_call | solution.py:54
  81.3 2.2 %collective-permute-start.4 = (f32[128,128]{1,0:T(8,128)}, f32[128,128]{1,0:T(8,128)S(1)}, u32[]{:S(2)}, u32[]{:S(2)}) collective-permute-start(f32[128,128]{1,0:T(8,128)} %shard_map.114), channel_id=1, source_target_pairs={{0,1},{1,0},{2,3},{3,2},{4,5},{5,4},{6,7},{7,6},{8,9},{9,8},{10,11... | collective-permute-start | bytes 196616 | tf_op jit(solution)/shard_map/ppermute | solution.py:22
  83.5 4.0 %shard_map.113 = bf16[16,2,4,8,512]{4,3,2,1,0:T(8,128)(2,1)} custom-call(s32[1]{0:T(128)} %bitcast.1.core_ref.at_ref, bf16[1024,1024]{1,0:T(8,128)(2,1)} %get-tuple-element.48.wide_ref, bf16[16,2,4,8,512]{4,3,2,1,0:T(8,128)(2,1)} %copy-done, bf16[16,2,4,8,512]{4,3,2,1,0:T(8,128)(2,1)} %copy-done), custom_call_target="tpu_custom_call" | custom-call | flops 1024 | bytes 1024 | tf_op jit(solution)/shard_map/pallas_call | solution.py:54
  87.5 0.0 collective-permute-done.4
  87.5 0.6 add.60.second_ref
  88.1 9.0 %all-to-all-done.2.mid_ref = bf16[16,2,4,8,512]{4,3,2,1,0:T(8,128)(2,1)S(1)} async-done(((bf16[16,2,4,8,512]{4,3,2,1,0:T(8,128)(2,1)}), bf16[16,2,4,8,512]{4,3,2,1,0:T(8,128)(2,1)S(1)}, u32[]{:S(2)}, u32[]{:S(2)}) %all-to-all-start.2) | async-done | bytes 1048608 | tf_op jit(solution)/shard_map/all_to_all | solution.py:36
  97.1 9.8 %all-to-all-start.3 = ((bf16[16,2,4,8,512]{4,3,2,1,0:T(8,128)(2,1)}), bf16[16,2,4,8,512]{4,3,2,1,0:T(8,128)(2,1)S(1)}, u32[]{:S(2)}, u32[]{:S(2)}) async-start(bf16[16,2,4,8,512]{4,3,2,1,0:T(8,128)(2,1)} %shard_map.113), calls=%async_computation.3 | async-start | bytes 2097152 | tf_op jit(solution)/shard_map/all_to_all | solution.py:36
  107.0 3.1 %collective-permute-start.5 = (bf16[16,4,8,512]{3,2,1,0:T(8,128)(2,1)S(1)}, bf16[16,4,8,512]{3,2,1,0:T(8,128)(2,1)S(1)}, u32[]{:S(2)}, u32[]{:S(2)}) collective-permute-start(bf16[16,4,8,512]{3,2,1,0:T(8,128)(2,1)S(1)} %slice_bitcast_fusion.1), channel_id=1, source_target_pairs={{0,1},{1,0},{2,3},{3,2},{4,5},{5,4},{6,7},{7,6},{8,9},{9,8},{10,11... | collective-permute-start | bytes 1572872 | tf_op jit(solution)/shard_map/ppermute | solution.py:22
  110.0 5.7 %shard_map.115 = (bf16[128,1152]{1,0:T(8,128)(2,1)}, bf16[128,1152]{1,0:T(8,128)(2,1)}, bf16[128,1152]{1,0:T(8,128)(2,1)}, f32[128,1152]{1,0:T(8,128)}) custom-call(s32[1]{0:T(128)} %bitcast.x_ref, s32[1]{0:T(128)} %bitcast.1.core_ref.at_ref, bf16[16,2,4,8,512]{4,3,2,1,0:T(8,128)(2,1)} %copy-done.1, bf16[16,4,8,512]{3,2,1,0:T(8,128)(2,1)} %get-tuple-element.51.kown_ref, ...), custom_call_target="tpu_custom_call" | custom-call | flops 1024 | bytes 1024 | tf_op jit(solution)/shard_map/pallas_call | solution.py:54
  115.7 1.2 collective-permute-start.6
  116.9 1.5 collective-permute-start.7
  118.4 1.5 collective-permute-start.8
  119.9 0.0 collective-permute-done.5.got_ref
  119.9 0.8 copy-done.7
  120.8 6.7 %shard_map.116 = (bf16[4,128,1024]{2,1,0:T(8,128)(2,1)}, bf16[4,128,1024]{2,1,0:T(8,128)(2,1)}, bf16[4,128,1024]{2,1,0:T(8,128)(2,1)}) custom-call(s32[1]{0:T(128)} %bitcast.1.core_ref.at_ref, bf16[16,2,4,8,512]{4,3,2,1,0:T(8,128)(2,1)} %copy-done.1, bf16[16,4,8,512]{3,2,1,0:T(8,128)(2,1)} %copy-done.7, ...), custom_call_target="tpu_custom_call" | custom-call | flops 1024 | bytes 1024 | tf_op jit(solution)/shard_map/pallas_call | solution.py:54
  127.4 0.0 collective-permute-done.6
  127.5 0.0 collective-permute-done.7
  127.5 0.7 copy-done.9
  128.2 0.7 copy-done.10
  128.9 4.3 %collective-permute-done.8 = bf16[128,1152]{1,0:T(8,128)(2,1)} collective-permute-done((bf16[128,1152]{1,0:T(8,128)(2,1)}, bf16[128,1152]{1,0:T(8,128)(2,1)}, u32[]{:S(2)}, u32[]{:S(2)}) %collective-permute-start.8) | collective-permute-done | bytes 294944 | tf_op jit(solution)/shard_map/ppermute | solution.py:32
  133.2 1.3 convert_add_fusion
  134.5 1.3 collective-permute-start.10
  135.7 1.5 collective-permute-start.11
  137.2 1.5 collective-permute-start.9
  138.7 0.0 all-to-all-done.3.mid_ref
  138.8 1.8 %collective-permute-start.12 = (bf16[16,4,8,512]{3,2,1,0:T(8,128)(2,1)S(1)}, bf16[16,4,8,512]{3,2,1,0:T(8,128)(2,1)S(1)}, u32[]{:S(2)}, u32[]{:S(2)}) collective-permute-start(bf16[16,4,8,512]{3,2,1,0:T(8,128)(2,1)S(1)} %slice_bitcast_fusion), channel_id=1, source_target_pairs={{0,1},{1,0},{2,3},{3,2},{4,5},{5,4},{6,7},{7,6},{8,9},{9,8},{10,11... | collective-permute-start | bytes 1572872 | tf_op jit(solution)/shard_map/ppermute | solution.py:22
  140.5 0.0 collective-permute-done.10
  140.5 0.0 collective-permute-done.11
  140.5 1.4 collective-permute-done.9
  142.0 3.1 %collective-permute-start.13 = (bf16[32,1152]{1,0:T(8,128)(2,1)S(1)}, bf16[32,1152]{1,0:T(8,128)(2,1)S(1)}, u32[]{:S(2)}, u32[]{:S(2)}) collective-permute-start(bf16[32,1152]{1,0:T(8,128)(2,1)S(1)} %fusion.2), channel_id=1, source_target_pairs={{0,128},{128,0},{1,129},{129,1},{2,130},{130,2},{3,131},{131,3},{4... | collective-permute-start | bytes 221192 | tf_op jit(solution)/shard_map/ppermute | solution.py:27
  145.1 0.0 collective-permute-done.12.got_ref
  145.1 0.8 copy-done.8
  145.9 3.4 %shard_map.117 = bf16[4,128,1024]{2,1,0:T(8,128)(2,1)} custom-call(s32[1]{0:T(128)} %bitcast.1.core_ref.at_ref, bf16[16,2,4,8,512]{4,3,2,1,0:T(8,128)(2,1)} %copy-done.3, bf16[16,4,8,512]{3,2,1,0:T(8,128)(2,1)} %copy-done.8), custom_call_target="tpu_custom_call" | custom-call | flops 1024 | bytes 1024 | tf_op jit(solution)/shard_map/pallas_call | solution.py:54
  149.3 0.0 collective-permute-done.13
  149.3 8.5 %collective-permute-start.14 = (bf16[32,1152]{1,0:T(8,128)(2,1)S(1)}, bf16[32,1152]{1,0:T(8,128)(2,1)S(1)}, u32[]{:S(2)}, u32[]{:S(2)}) collective-permute-start(bf16[32,1152]{1,0:T(8,128)(2,1)S(1)} %add_convert_fusion), channel_id=1, source_target_pairs={{0,0},{1,16},{2,1},{3,17},{4,2},{5,18},{6,3},{7,19},{8,32},{9,48},... | collective-permute-start | bytes 221192 | tf_op jit(solution)/shard_map/ppermute | solution.py:416
  157.8 0.1 collective-permute-start.15
  157.9 5.0 %collective-permute-start.16 = (bf16[32,1152]{1,0:T(8,128)(2,1)S(1)}, bf16[32,1152]{1,0:T(8,128)(2,1)S(1)}, u32[]{:S(2)}, u32[]{:S(2)}) collective-permute-start(bf16[32,1152]{1,0:T(8,128)(2,1)S(1)} %add_convert_fusion), channel_id=1, source_target_pairs={{0,64},{1,80},{2,65},{3,81},{4,66},{5,82},{6,67},{7,83},{8,96},{9,... | collective-permute-start | bytes 221192 | tf_op jit(solution)/shard_map/ppermute | solution.py:416
  162.9 2.2 %collective-permute-start.17 = (bf16[32,1152]{1,0:T(8,128)(2,1)S(1)}, bf16[32,1152]{1,0:T(8,128)(2,1)S(1)}, u32[]{:S(2)}, u32[]{:S(2)}) collective-permute-start(bf16[32,1152]{1,0:T(8,128)(2,1)S(1)} %add_convert_fusion), channel_id=1, source_target_pairs={{0,96},{1,112},{2,97},{3,113},{4,98},{5,114},{6,99},{7,115},{8,64}... | collective-permute-start | bytes 221192 | tf_op jit(solution)/shard_map/ppermute | solution.py:416
  165.1 0.0 collective-permute-done.14
  165.2 0.0 collective-permute-done.15
  165.2 7.5 %collective-permute-done.16 = bf16[32,1152]{1,0:T(8,128)(2,1)S(1)} collective-permute-done((bf16[32,1152]{1,0:T(8,128)(2,1)S(1)}, bf16[32,1152]{1,0:T(8,128)(2,1)S(1)}, u32[]{:S(2)}, u32[]{:S(2)}) %collective-permute-start.16) | collective-permute-done | bytes 73760 | tf_op jit(solution)/shard_map/ppermute | solution.py:416
  172.6 3.2 %collective-permute-done.17 = bf16[32,1152]{1,0:T(8,128)(2,1)S(1)} collective-permute-done((bf16[32,1152]{1,0:T(8,128)(2,1)S(1)}, bf16[32,1152]{1,0:T(8,128)(2,1)S(1)}, u32[]{:S(2)}, u32[]{:S(2)}) %collective-permute-start.17) | collective-permute-done | bytes 73760 | tf_op jit(solution)/shard_map/ppermute | solution.py:416
  175.9 0.7 slice_multiply_fusion
  176.5 0.6 slice_multiply_fusion.1
  (26 shorter events, 0.3 us)
Async XLA Ops:
  2.9 36.6 %all-to-all-start = ((bf16[16,4,8,1024]{3,2,1,0:T(8,128)(2,1)}), bf16[16,4,8,1024]{3,2,1,0:T(8,128)(2,1)S(1)}, u32[]{:S(2)}, u32[]{:S(2)}) async-start(bf16[16,4,8,1024]{3,2,1,0:T(8,128)(2,1)} %shard_map.109), calls=%async_computation | async-start | bytes 2097152 | tf_op jit(solution)/shard_map/all_to_all | solution.py:36
  19.9 5.2 %collective-permute-start = (bf16[16,4,8,512]{3,2,1,0:T(8,128)(2,1)}, bf16[16,4,8,512]{3,2,1,0:T(8,128)(2,1)S(1)}, u32[]{:S(2)}, u32[]{:S(2)}) collective-permute-start(bf16[16,4,8,512]{3,2,1,0:T(8,128)(2,1)} %get-tuple-element.39), channel_id=1, source_target_pairs={{0,1},{1,0},{2,3},{3,2},{4,5},{5,4},{6,7},{7,6},{8,9},{9,8},{10,11... | collective-permute-start | bytes 1572872 | tf_op jit(solution)/shard_map/ppermute | solution.py:22
  25.1 20.8 %copy-start.5 = (bf16[16,4,8,1024]{3,2,1,0:T(8,128)(2,1)S(1)}, bf16[16,4,8,1024]{3,2,1,0:T(8,128)(2,1)}, u32[]{:S(2)}) copy-start(bf16[16,4,8,1024]{3,2,1,0:T(8,128)(2,1)} %get-tuple-element.46.own_ref) | copy-start | bytes 3145732
  39.5 12.6 %copy-start.2 = (bf16[16,4,8,1024]{3,2,1,0:T(8,128)(2,1)}, bf16[16,4,8,1024]{3,2,1,0:T(8,128)(2,1)S(1)}, u32[]{:S(2)}) copy-start(bf16[16,4,8,1024]{3,2,1,0:T(8,128)(2,1)S(1)} %all-to-all-done.own_ref.up_ref) | copy-start | bytes 3145732
  39.5 27.9 %all-to-all-start.1 = ((bf16[16,2,4,8,512]{4,3,2,1,0:T(8,128)(2,1)}), bf16[16,2,4,8,512]{4,3,2,1,0:T(8,128)(2,1)S(1)}, u32[]{:S(2)}, u32[]{:S(2)}) async-start(bf16[16,2,4,8,512]{4,3,2,1,0:T(8,128)(2,1)} %pad_maximum_fusion), calls=%async_computation.1 | async-start | bytes 2097152 | tf_op jit(solution)/shard_map/all_to_all | solution.py:36
  45.8 11.2 %collective-permute-start.3 = (bf16[16,4,8,1024]{3,2,1,0:T(8,128)(2,1)S(1)}, bf16[16,4,8,1024]{3,2,1,0:T(8,128)(2,1)}, u32[]{:S(2)}, u32[]{:S(2)}) collective-permute-start(bf16[16,4,8,1024]{3,2,1,0:T(8,128)(2,1)S(1)} %copy-done.5), channel_id=1, source_target_pairs={{0,1},{1,0},{2,3},{3,2},{4,5},{5,4},{6,7},{7,6},{8,9},{9,8},{10,11... | collective-permute-start | bytes 3145736 | tf_op jit(solution)/shard_map/ppermute | solution.py:22
  48.4 3.7 %collective-permute-start.1 = (bf16[16,4,8,512]{3,2,1,0:T(8,128)(2,1)S(1)}, bf16[16,4,8,512]{3,2,1,0:T(8,128)(2,1)S(1)}, u32[]{:S(2)}, u32[]{:S(2)}) collective-permute-start(bf16[16,4,8,512]{3,2,1,0:T(8,128)(2,1)S(1)} %constant_dynamic-slice_fusion), channel_id=1, source_target_pairs={{0,1},{1,0},{2,3},{3,2},{4,5},{5,4},{6,7},{7,6},{8,9},{9,8},{10,11... | collective-permute-start | bytes 1572872 | tf_op jit(solution)/shard_map/ppermute | solution.py:22
  48.5 8.5 %collective-permute-start.2 = (bf16[16,4,8,512]{3,2,1,0:T(8,128)(2,1)}, bf16[16,4,8,512]{3,2,1,0:T(8,128)(2,1)}, u32[]{:S(2)}, u32[]{:S(2)}) collective-permute-start(bf16[16,4,8,512]{3,2,1,0:T(8,128)(2,1)} %get-tuple-element.45.koth_ref), channel_id=1, source_target_pairs={{0,1},{1,0},{2,3},{3,2},{4,5},{5,4},{6,7},{7,6},{8,9},{9,8},{10,11... | collective-permute-start | bytes 1572872 | tf_op jit(solution)/shard_map/ppermute | solution.py:22
  52.1 0.8 copy-start.4
  67.5 8.9 %copy-start = (bf16[16,2,4,8,512]{4,3,2,1,0:T(8,128)(2,1)}, bf16[16,2,4,8,512]{4,3,2,1,0:T(8,128)(2,1)S(1)}, u32[]{:S(2)}) copy-start(bf16[16,2,4,8,512]{4,3,2,1,0:T(8,128)(2,1)S(1)} %all-to-all-done.1.own_ref.oth_ref.kern_ref) | copy-start | bytes 3145732
  67.5 29.6 %all-to-all-start.2 = ((bf16[16,2,4,8,512]{4,3,2,1,0:T(8,128)(2,1)}), bf16[16,2,4,8,512]{4,3,2,1,0:T(8,128)(2,1)S(1)}, u32[]{:S(2)}, u32[]{:S(2)}) async-start(bf16[16,2,4,8,512]{4,3,2,1,0:T(8,128)(2,1)} %shard_map.112), calls=%async_computation.2 | async-start | bytes 2097152 | tf_op jit(solution)/shard_map/all_to_all | solution.py:36
  81.3 6.2 %copy-start.11 = (f32[128,128]{1,0:T(8,128)S(1)}, f32[128,128]{1,0:T(8,128)}, u32[]{:S(2)}) copy-start(f32[128,128]{1,0:T(8,128)} %shard_map.114) | copy-start | bytes 196612
  81.3 6.2 %collective-permute-start.4 = (f32[128,128]{1,0:T(8,128)}, f32[128,128]{1,0:T(8,128)S(1)}, u32[]{:S(2)}, u32[]{:S(2)}) collective-permute-start(f32[128,128]{1,0:T(8,128)} %shard_map.114), channel_id=1, source_target_pairs={{0,1},{1,0},{2,3},{3,2},{4,5},{5,4},{6,7},{7,6},{8,9},{9,8},{10,11... | collective-permute-start | bytes 196616 | tf_op jit(solution)/shard_map/ppermute | solution.py:22
  97.1 12.9 %copy-start.1 = (bf16[16,2,4,8,512]{4,3,2,1,0:T(8,128)(2,1)}, bf16[16,2,4,8,512]{4,3,2,1,0:T(8,128)(2,1)S(1)}, u32[]{:S(2)}) copy-start(bf16[16,2,4,8,512]{4,3,2,1,0:T(8,128)(2,1)S(1)} %all-to-all-done.2.mid_ref) | copy-start | bytes 3145732
  97.1 41.6 %all-to-all-start.3 = ((bf16[16,2,4,8,512]{4,3,2,1,0:T(8,128)(2,1)}), bf16[16,2,4,8,512]{4,3,2,1,0:T(8,128)(2,1)S(1)}, u32[]{:S(2)}, u32[]{:S(2)}) async-start(bf16[16,2,4,8,512]{4,3,2,1,0:T(8,128)(2,1)} %shard_map.113), calls=%async_computation.3 | async-start | bytes 2097152 | tf_op jit(solution)/shard_map/all_to_all | solution.py:36
  107.0 13.0 %collective-permute-start.5 = (bf16[16,4,8,512]{3,2,1,0:T(8,128)(2,1)S(1)}, bf16[16,4,8,512]{3,2,1,0:T(8,128)(2,1)S(1)}, u32[]{:S(2)}, u32[]{:S(2)}) collective-permute-start(bf16[16,4,8,512]{3,2,1,0:T(8,128)(2,1)S(1)} %slice_bitcast_fusion.1), channel_id=1, source_target_pairs={{0,1},{1,0},{2,3},{3,2},{4,5},{5,4},{6,7},{7,6},{8,9},{9,8},{10,11... | collective-permute-start | bytes 1572872 | tf_op jit(solution)/shard_map/ppermute | solution.py:22
  115.7 11.7 %collective-permute-start.6 = (bf16[128,1152]{1,0:T(8,128)(2,1)}, bf16[128,1152]{1,0:T(8,128)(2,1)S(1)}, u32[]{:S(2)}, u32[]{:S(2)}) collective-permute-start(bf16[128,1152]{1,0:T(8,128)(2,1)} %get-tuple-element.61), channel_id=1, source_target_pairs={{0,32},{32,64},{64,96},{96,0},{1,33},{33,65},{65,97},{97,1},{2,34}... | collective-permute-start | bytes 884744 | tf_op jit(solution)/shard_map/ppermute | solution.py:32
  116.9 10.5 %collective-permute-start.7 = (bf16[128,1152]{1,0:T(8,128)(2,1)}, bf16[128,1152]{1,0:T(8,128)(2,1)S(1)}, u32[]{:S(2)}, u32[]{:S(2)}) collective-permute-start(bf16[128,1152]{1,0:T(8,128)(2,1)} %get-tuple-element.62), channel_id=1, source_target_pairs={{0,96},{32,0},{64,32},{96,64},{1,97},{33,1},{65,33},{97,65},{2,98}... | collective-permute-start | bytes 884744 | tf_op jit(solution)/shard_map/ppermute | solution.py:32
  118.4 14.7 %collective-permute-start.8 = (bf16[128,1152]{1,0:T(8,128)(2,1)}, bf16[128,1152]{1,0:T(8,128)(2,1)}, u32[]{:S(2)}, u32[]{:S(2)}) collective-permute-start(bf16[128,1152]{1,0:T(8,128)(2,1)} %get-tuple-element.63), channel_id=1, source_target_pairs={{0,64},{32,96},{64,0},{96,32},{1,65},{33,97},{65,1},{97,33},{2,66}... | collective-permute-start | bytes 884744 | tf_op jit(solution)/shard_map/ppermute | solution.py:32
  119.9 0.8 copy-start.7
  120.8 12.4 %copy-start.6 = (f32[128,1152]{1,0:T(8,128)S(1)}, f32[128,1152]{1,0:T(8,128)}, u32[]{:S(2)}) copy-start(f32[128,1152]{1,0:T(8,128)} %get-tuple-element.60) | copy-start | bytes 1769476
  127.4 0.7 copy-start.9
  128.2 0.7 copy-start.10
  134.5 6.0 %collective-permute-start.10 = (bf16[32,1152]{1,0:T(8,128)(2,1)S(1)}, bf16[32,1152]{1,0:T(8,128)(2,1)S(1)}, u32[]{:S(2)}, u32[]{:S(2)}) collective-permute-start(bf16[32,1152]{1,0:T(8,128)(2,1)S(1)} %get-tuple-element.72), channel_id=1, source_target_pairs={{0,2},{2,4},{4,6},{6,0},{1,3},{3,5},{5,7},{7,1},{8,10},{10,12},{12... | collective-permute-start | bytes 221192 | tf_op jit(solution)/shard_map/ppermute | solution.py:32
  135.7 4.8 %collective-permute-start.11 = (bf16[32,1152]{1,0:T(8,128)(2,1)S(1)}, bf16[32,1152]{1,0:T(8,128)(2,1)S(1)}, u32[]{:S(2)}, u32[]{:S(2)}) collective-permute-start(bf16[32,1152]{1,0:T(8,128)(2,1)S(1)} %get-tuple-element.71), channel_id=1, source_target_pairs={{0,6},{2,0},{4,2},{6,4},{1,7},{3,1},{5,3},{7,5},{8,14},{10,8},{12,... | collective-permute-start | bytes 221192 | tf_op jit(solution)/shard_map/ppermute | solution.py:32
  137.2 4.7 %collective-permute-start.9 = (bf16[32,1152]{1,0:T(8,128)(2,1)S(1)}, bf16[32,1152]{1,0:T(8,128)(2,1)S(1)}, u32[]{:S(2)}, u32[]{:S(2)}) collective-permute-start(bf16[32,1152]{1,0:T(8,128)(2,1)S(1)} %get-tuple-element.70), channel_id=1, source_target_pairs={{0,4},{2,6},{4,0},{6,2},{1,5},{3,7},{5,1},{7,3},{8,12},{10,14},{12... | collective-permute-start | bytes 221192 | tf_op jit(solution)/shard_map/ppermute | solution.py:32
  138.7 6.4 %copy-start.3 = (bf16[16,2,4,8,512]{4,3,2,1,0:T(8,128)(2,1)}, bf16[16,2,4,8,512]{4,3,2,1,0:T(8,128)(2,1)S(1)}, u32[]{:S(2)}) copy-start(bf16[16,2,4,8,512]{4,3,2,1,0:T(8,128)(2,1)S(1)} %all-to-all-done.3.mid_ref) | copy-start | bytes 3145732
  138.8 6.3 %collective-permute-start.12 = (bf16[16,4,8,512]{3,2,1,0:T(8,128)(2,1)S(1)}, bf16[16,4,8,512]{3,2,1,0:T(8,128)(2,1)S(1)}, u32[]{:S(2)}, u32[]{:S(2)}) collective-permute-start(bf16[16,4,8,512]{3,2,1,0:T(8,128)(2,1)S(1)} %slice_bitcast_fusion), channel_id=1, source_target_pairs={{0,1},{1,0},{2,3},{3,2},{4,5},{5,4},{6,7},{7,6},{8,9},{9,8},{10,11... | collective-permute-start | bytes 1572872 | tf_op jit(solution)/shard_map/ppermute | solution.py:22
  142.0 7.3 %collective-permute-start.13 = (bf16[32,1152]{1,0:T(8,128)(2,1)S(1)}, bf16[32,1152]{1,0:T(8,128)(2,1)S(1)}, u32[]{:S(2)}, u32[]{:S(2)}) collective-permute-start(bf16[32,1152]{1,0:T(8,128)(2,1)S(1)} %fusion.2), channel_id=1, source_target_pairs={{0,128},{128,0},{1,129},{129,1},{2,130},{130,2},{3,131},{131,3},{4... | collective-permute-start | bytes 221192 | tf_op jit(solution)/shard_map/ppermute | solution.py:27
  145.1 0.8 copy-start.8
  149.3 15.8 %collective-permute-start.14 = (bf16[32,1152]{1,0:T(8,128)(2,1)S(1)}, bf16[32,1152]{1,0:T(8,128)(2,1)S(1)}, u32[]{:S(2)}, u32[]{:S(2)}) collective-permute-start(bf16[32,1152]{1,0:T(8,128)(2,1)S(1)} %add_convert_fusion), channel_id=1, source_target_pairs={{0,0},{1,16},{2,1},{3,17},{4,2},{5,18},{6,3},{7,19},{8,32},{9,48},... | collective-permute-start | bytes 221192 | tf_op jit(solution)/shard_map/ppermute | solution.py:416
  157.8 7.3 %collective-permute-start.15 = (bf16[32,1152]{1,0:T(8,128)(2,1)S(1)}, bf16[32,1152]{1,0:T(8,128)(2,1)S(1)}, u32[]{:S(2)}, u32[]{:S(2)}) collective-permute-start(bf16[32,1152]{1,0:T(8,128)(2,1)S(1)} %add_convert_fusion), channel_id=1, source_target_pairs={{0,32},{1,48},{2,33},{3,49},{4,34},{5,50},{6,35},{7,51},{8,0},{9,1... | collective-permute-start | bytes 221192 | tf_op jit(solution)/shard_map/ppermute | solution.py:416
  157.9 14.7 %collective-permute-start.16 = (bf16[32,1152]{1,0:T(8,128)(2,1)S(1)}, bf16[32,1152]{1,0:T(8,128)(2,1)S(1)}, u32[]{:S(2)}, u32[]{:S(2)}) collective-permute-start(bf16[32,1152]{1,0:T(8,128)(2,1)S(1)} %add_convert_fusion), channel_id=1, source_target_pairs={{0,64},{1,80},{2,65},{3,81},{4,66},{5,82},{6,67},{7,83},{8,96},{9,... | collective-permute-start | bytes 221192 | tf_op jit(solution)/shard_map/ppermute | solution.py:416
  162.9 12.9 %collective-permute-start.17 = (bf16[32,1152]{1,0:T(8,128)(2,1)S(1)}, bf16[32,1152]{1,0:T(8,128)(2,1)S(1)}, u32[]{:S(2)}, u32[]{:S(2)}) collective-permute-start(bf16[32,1152]{1,0:T(8,128)(2,1)S(1)} %add_convert_fusion), channel_id=1, source_target_pairs={{0,96},{1,112},{2,97},{3,113},{4,98},{5,114},{6,99},{7,115},{8,64}... | collective-permute-start | bytes 221192 | tf_op jit(solution)/shard_map/ppermute | solution.py:416

commit v3 on v2

--- a/solution.py
+++ b/solution.py
@@ -43,7 +43,7 @@
             for zh in range(4):
                 for y in range(4):
                     for c in range(2):
-                        place = 16 * c + 4 * x + y
+                        place = (2 * c + x // 2) * 8 + 2 * y + x % 2
                         source = (((zl * 4 + x) * 4 + zh) * 4 + y) * 2 + c
                         target = (((zl * 4 + (zh ^ step)) * 4 + place // 8) * 4 + place // 2 % 4) * 2 + place % 2
                         perm.append((source, target))
@@ -128,7 +128,7 @@
     )
 
 
-GROUP = 4
+GROUP = 8
 STEP_ROWS = GROUP * LOCAL * ROWS
 
 
@@ -259,49 +259,40 @@
 PACKED = WIDTH + NB
 
 
-def first_body(x_ref, core_ref, mid_ref, kown_ref, koth_ref, own_ref, oth_ref, second_ref, *out_refs):
+def first_body(x_ref, at_ref, mid_ref, kown_ref, koth_ref, own_ref, oth_ref, second_ref, *refs):
     total = 0.0
     for rel, (weight, mixed) in enumerate(((kown_ref, own_ref), (koth_ref, oth_ref))):
-        grad = mid_ref[:, rel].reshape(SIDE, SHARE) * weight[...].reshape(SIDE, SHARE)
+        grad = mid_ref[:, rel].reshape(SIDE, HALF) * weight[...].reshape(SIDE, HALF)
         total = total + lax.dot_general(
-            grad,
-            mixed[...].reshape(SIDE, WIDTH),
-            (((0,), (0,)), ((), ())),
-            preferred_element_type=F32,
+            grad, mixed[...].reshape(SIDE, WIDTH), (((0,), (0,)), ((), ())), preferred_element_type=F32
         )
-    chunk = lax.rem(x_ref[0] + turn(pl.program_id(0)), 4)
-    terms = second_ref[pl.ds(pl.multiple_of(core_ref[0] * (NB // 2) + chunk * (NB // 8), NB // 8), NB // 8), :]
-    blank = jnp.zeros((SHARE // 4 - LOCAL, NB), F32)
-    terms = [piece for y in range(4) for piece in (terms[y * LOCAL : (y + 1) * LOCAL], blank)]
-    terms = jnp.concatenate(terms, 0)
-    for step, ref in enumerate(out_refs):
-
-        @pl.when(pl.program_id(0) == step)
-        def _():
-            ref[:, :WIDTH] = total.astype(ref.dtype)
-            ref[:, WIDTH:] = terms.astype(ref.dtype)
-
-
-def turn(i):
-    return jnp.where(i == 0, 2, jnp.where(i == 2, 3, jnp.where(i == 1, 1, 0)))
-
-
-def first_terms(x, core, mid, kown, koth, own, oth, terms):
-    def chunk(i, x):
-        return lax.rem(x[0] + turn(i), 4)
-
-    weight = pl.BlockSpec((PEERS, LOCAL, ROWS, SHARE), lambda i, x, core: (0, 0, 0, chunk(i, x)))
-    mixed = whole((PEERS, LOCAL, ROWS, WIDTH))
+    full_ref = refs[4]
+    full_ref[...] = total
+    row = lax.broadcasted_iota(jnp.int32, (SHARE, NB), 0)
+    column = lax.broadcasted_iota(jnp.int32, (SHARE, NB), 1)
+    for step, ref in zip((2, 1, 3, 0), refs):
+        x = lax.rem(x_ref[0] + step, 4)
+        high, low = x // 2, lax.rem(x, 2)
+        for y in range(4):
+            rows = pl.ds(pl.multiple_of((high * 8 + 2 * y + low) * 32, 32), 32)
+            ref[y * 32 : (y + 1) * 32, :WIDTH] = full_ref[rows, :].astype(ref.dtype)
+        place = (2 * at_ref[0] + high) * 8 + row // 32 * 2 + low
+        pick = jnp.where((place * LOCAL + row % 32 == column) & (row % 32 < LOCAL), 1.0, 0.0)
+        terms = jnp.dot(pick, second_ref[...], precision=lax.Precision.HIGHEST, preferred_element_type=F32)
+        ref[:, WIDTH:] = terms.astype(ref.dtype)
+
+
+def first_terms(x, at, mid, kown, koth, own, oth, terms):
     out = (SHARE, PACKED)
+    operands = (mid, kown, koth, own, oth, terms)
     return call(
         first_body,
-        (x, core),
-        (mid, kown, koth, own, oth, terms),
-        [pl.BlockSpec((PEERS, 2, LOCAL, ROWS, SHARE), lambda i, x, core: (0, 0, 0, 0, chunk(i, x))), weight, weight]
-        + [mixed, mixed, whole((NB, NB))],
+        (x, at),
+        operands,
+        [whole(operand.shape) for operand in operands],
         [struct(out), struct(out), struct(out), struct(out, F32)],
         [whole(out)] * 4,
-        grid=(4,),
+        scratch=[pltpu.VMEM((HALF, WIDTH), F32)],
     )
 
 

time: 180 us -> 174 us (0.967)
  Pallas kernels: 41.7 us -> 36.3 us
  waiting for transfers between devices: 51.2 us -> 54.1 us
  starting transfers between devices: 73.9 us -> 72 us
    pallas_call x9, Pallas kernels: 41.7 us -> 36.3 us  [call(): pl.pallas_call(body, out_shape=out_shapes, grid_spec=pltpu.PrefetchScalar...]
    ppermute x4, starting transfers between devices: 15.8 us -> 13.7 us  [on_device(): lax.ppermute(part, AXES, to_owner(step)).astype(F32)]
    all_to_all x4, waiting for transfers between devices: 31.7 us -> 33.5 us  [exchange(): return lax.all_to_all(value, ('y', 'zh'), 0, 0, tiled=True)]
  transfers between devices with their start and end apart: 22 -> 22, of which waited for: 8 -> 9; matrix products, arithmetic and copies ran while one was open for 2% -> 2% of each run, Pallas kernels for 22% -> 20%
where the time goes in v3:
time: 174 us; the launch traced here: 173 us
  starting transfers between devices  72 us (41%)
  waiting for transfers between devices  54.1 us (31%)
  Pallas kernels  36.3 us (21%)
  other arithmetic  5.48 us (3%)
  local copies, waits for them, and re-layouts  4.04 us (2%)
    pallas_call x9, Pallas kernels, call(): pl.pallas_call(body, out_shape=out_shapes, grid_spec=pltpu.PrefetchScalar...  36.3 us
    all_to_all x4, starting transfers between devices, exchange(): return lax.all_to_all(value, ('y', 'zh'), 0, 0, tiled=True)  35.2 us
    all_to_all x4, waiting for transfers between devices, exchange(): return lax.all_to_all(value, ('y', 'zh'), 0, 0, tiled=True)  33.5 us
    ppermute x4, starting transfers between devices, on_device(): lax.ppermute(part, AXES, to_owner(step)).astype(F32)  13.7 us
    ppermute x7, starting transfers between devices, swap(): return lax.ppermute(value, 'c', [(0, 1), (1, 0)])  11.5 us
    ppermute x4, waiting for transfers between devices, on_device(): lax.ppermute(part, AXES, to_owner(step)).astype(F32)  10.5 us
    ppermute x6, starting transfers between devices, shift(): lax.ppermute(value, axis, [(i, (i + step) % size) for i in range(size)])  8.44 us
    ppermute x6, waiting for transfers between devices, shift(): lax.ppermute(value, axis, [(i, (i + step) % size) for i in range(size)])  6.93 us
  transfers between devices with their start and end apart: 22, of which 9 were waited for; matrix products, arithmetic and copies ran while one was open for 2% of the time, Pallas kernels for 20%

profile of v3, /device:TPU:65, one launch (start us, length us, event | category | flops | bytes accessed | tf_op | source)
XLA Modules:
  0.0 172.7 jit_solution(11499992637178046994)
XLA Ops:
  0.6 2.3 %shard_map.109 = bf16[16,4,8,1024]{3,2,1,0:T(8,128)(2,1)} custom-call(bf16[4,128,1024]{2,1,0:T(8,128)(2,1)} %in_ref.3), custom_call_target="tpu_custom_call" | custom-call | flops 1024 | bytes 1024 | tf_op jit(solution)/shard_map/pallas_call | solution.py:54
  2.9 10.2 %all-to-all-start = ((bf16[16,4,8,1024]{3,2,1,0:T(8,128)(2,1)}), bf16[16,4,8,1024]{3,2,1,0:T(8,128)(2,1)S(1)}, u32[]{:S(2)}, u32[]{:S(2)}) async-start(bf16[16,4,8,1024]{3,2,1,0:T(8,128)(2,1)} %shard_map.109), calls=%async_computation | async-start | bytes 2097152 | tf_op jit(solution)/shard_map/all_to_all | solution.py:36
  13.1 5.0 %shard_map.110 = (bf16[16,4,8,1024]{3,2,1,0:T(8,128)(2,1)}, bf16[16,4,8,1024]{3,2,1,0:T(8,128)(2,1)}, bf16[16,4,8,512]{3,2,1,0:T(8,128)(2,1)}, bf16[16,4,8,512]{...) custom-call(s32[1]{0:T(128)} %bitcast.1.core_ref.at_ref, ...), custom_call_target="tpu_custom_call" | custom-call | flops 1024 | bytes 1024 | tf_op jit(solution)/shard_map/pallas_call | solution.py:54
  18.1 1.3 collective-permute-start
  19.3 3.9 %shard_map.111 = (bf16[1024,1024]{1,0:T(8,128)(2,1)}, bf16[1024,1024]{1,0:T(8,128)(2,1)}) custom-call(s32[1]{0:T(128)} %bitcast.1.core_ref.at_ref, bf16[128,128]{1,0:T(8,128)(2,1)} %sf_ref.1), custom_call_target="tpu_custom_call" | custom-call | flops 1024 | bytes 1024 | tf_op jit(solution)/shard_map/pallas_call | solution.py:54
  23.2 0.0 collective-permute-done
  23.2 2.2 %pad_maximum_fusion = bf16[16,2,4,8,512]{4,3,2,1,0:T(8,128)(2,1)} fusion(bf16[16,1,4,8,512]{4,3,2,1,0:T(8,128)(2,1)S(1)} %bitcast.28, bf16[16,1,4,8,512]{4,3,2,1,0:T(8,128)(2,1)} %bitcast.27), kind=kLoop, calls=%fused_computation | loop fusion | flops 524288 | bytes 2097152 | tf_op jit(solution)/shard_map/stack | solution.py:370
  25.4 14.1 %all-to-all-done.own_ref.up_ref = bf16[16,4,8,1024]{3,2,1,0:T(8,128)(2,1)S(1)} async-done(((bf16[16,4,8,1024]{3,2,1,0:T(8,128)(2,1)}), bf16[16,4,8,1024]{3,2,1,0:T(8,128)(2,1)S(1)}, u32[]{:S(2)}, u32[]{:S(2)}) %all-to-all-start) | async-done | bytes 1048608 | tf_op jit(solution)/shard_map/all_to_all | solution.py:36
  39.5 6.3 %all-to-all-start.1 = ((bf16[16,2,4,8,512]{4,3,2,1,0:T(8,128)(2,1)}), bf16[16,2,4,8,512]{4,3,2,1,0:T(8,128)(2,1)S(1)}, u32[]{:S(2)}, u32[]{:S(2)}) async-start(bf16[16,2,4,8,512]{4,3,2,1,0:T(8,128)(2,1)} %pad_maximum_fusion), calls=%async_computation.1 | async-start | bytes 2097152 | tf_op jit(solution)/shard_map/all_to_all | solution.py:36
  45.8 2.5 %collective-permute-start.3 = (bf16[16,4,8,1024]{3,2,1,0:T(8,128)(2,1)S(1)}, bf16[16,4,8,1024]{3,2,1,0:T(8,128)(2,1)}, u32[]{:S(2)}, u32[]{:S(2)}) collective-permute-start(bf16[16,4,8,1024]{3,2,1,0:T(8,128)(2,1)S(1)} %copy-done.5), channel_id=1, source_target_pairs={{0,1},{1,0},{2,3},{3,2},{4,5},{5,4},{6,7},{7,6},{8,9},{9,8},{10,11... | collective-permute-start | bytes 3145736 | tf_op jit(solution)/shard_map/ppermute | solution.py:22
  48.4 0.1 collective-permute-start.1
  48.5 0.5 collective-permute-start.2
  49.0 3.1 %collective-permute-done.1.oth_ref.up_oth_ref = bf16[16,4,8,512]{3,2,1,0:T(8,128)(2,1)S(1)} collective-permute-done((bf16[16,4,8,512]{3,2,1,0:T(8,128)(2,1)S(1)}, bf16[16,4,8,512]{3,2,1,0:T(8,128)(2,1)S(1)}, u32[]{:S(2)}, u32[]{:S(2)}) %collective-permute-start.1) | collective-permute-done | bytes 524320 | tf_op jit(solution)/shard_map/ppermute | solution.py:22
  52.1 0.0 copy-done.2
  52.1 0.8 copy-done.4
  52.9 4.0 %shard_map.112 = bf16[16,2,4,8,512]{4,3,2,1,0:T(8,128)(2,1)} custom-call(s32[1]{0:T(128)} %bitcast.1.core_ref.at_ref, bf16[1024,1024]{1,0:T(8,128)(2,1)} %get-tuple-element.42.wide_ref, bf16[16,4,8,1024]{3,2,1,0:T(8,128)(2,1)} %copy-done.2, bf16[16,4,8,512]{3,2,1,0:T(8,128)(2,1)} %copy-done.4), custom_call_target="tpu_custom_call" | custom-call | flops 1024 | bytes 1024 | tf_op jit(solution)/shard_map/pallas_call | solution.py:54
  57.0 0.0 collective-permute-done.2.koth_ref
  57.0 0.0 collective-permute-done.3.oth_ref
  57.0 10.5 %all-to-all-done.1.own_ref.oth_ref.kern_ref = bf16[16,2,4,8,512]{4,3,2,1,0:T(8,128)(2,1)S(1)} async-done(((bf16[16,2,4,8,512]{4,3,2,1,0:T(8,128)(2,1)}), bf16[16,2,4,8,512]{4,3,2,1,0:T(8,128)(2,1)S(1)}, u32[]{:S(2)}, u32[]{:S(2)}) %all-to-all-start.1) | async-done | bytes 1048608 | tf_op jit(solution)/shard_map/all_to_all | solution.py:36
  67.5 8.9 %all-to-all-start.2 = ((bf16[16,2,4,8,512]{4,3,2,1,0:T(8,128)(2,1)}), bf16[16,2,4,8,512]{4,3,2,1,0:T(8,128)(2,1)S(1)}, u32[]{:S(2)}, u32[]{:S(2)}) async-start(bf16[16,2,4,8,512]{4,3,2,1,0:T(8,128)(2,1)} %shard_map.112), calls=%async_computation.2 | async-start | bytes 2097152 | tf_op jit(solution)/shard_map/all_to_all | solution.py:36
  76.4 4.9 %shard_map.114 = f32[128,128]{1,0:T(8,128)} custom-call(s32[1]{0:T(128)} %bitcast.1.core_ref.at_ref, bf16[16,4,8,1024]{3,2,1,0:T(8,128)(2,1)} %copy-done.2, bf16[16,4,8,512]{3,2,1,0:T(8,128)(2,1)} %copy-done.4, bf16[16,2,4,8,512]{4,3,2,1,0:T(8,128)(2,1)} %copy-done), custom_call_target="tpu_custom_call" | custom-call | flops 1024 | bytes 1024 | tf_op jit(solution)/shard_map/pallas_call | solution.py:54
  81.3 2.2 %collective-permute-start.4 = (f32[128,128]{1,0:T(8,128)}, f32[128,128]{1,0:T(8,128)S(1)}, u32[]{:S(2)}, u32[]{:S(2)}) collective-permute-start(f32[128,128]{1,0:T(8,128)} %shard_map.114), channel_id=1, source_target_pairs={{0,1},{1,0},{2,3},{3,2},{4,5},{5,4},{6,7},{7,6},{8,9},{9,8},{10,11... | collective-permute-start | bytes 196616 | tf_op jit(solution)/shard_map/ppermute | solution.py:22
  83.5 4.0 %shard_map.113 = bf16[16,2,4,8,512]{4,3,2,1,0:T(8,128)(2,1)} custom-call(s32[1]{0:T(128)} %bitcast.1.core_ref.at_ref, bf16[1024,1024]{1,0:T(8,128)(2,1)} %get-tuple-element.48.wide_ref, bf16[16,2,4,8,512]{4,3,2,1,0:T(8,128)(2,1)} %copy-done, bf16[16,2,4,8,512]{4,3,2,1,0:T(8,128)(2,1)} %copy-done), custom_call_target="tpu_custom_call" | custom-call | flops 1024 | bytes 1024 | tf_op jit(solution)/shard_map/pallas_call | solution.py:54
  87.5 0.0 collective-permute-done.4
  87.5 0.6 add.60.second_ref
  88.1 9.0 %all-to-all-done.2.mid_ref = bf16[16,2,4,8,512]{4,3,2,1,0:T(8,128)(2,1)S(1)} async-done(((bf16[16,2,4,8,512]{4,3,2,1,0:T(8,128)(2,1)}), bf16[16,2,4,8,512]{4,3,2,1,0:T(8,128)(2,1)S(1)}, u32[]{:S(2)}, u32[]{:S(2)}) %all-to-all-start.2) | async-done | bytes 1048608 | tf_op jit(solution)/shard_map/all_to_all | solution.py:36
  97.1 9.8 %all-to-all-start.3 = ((bf16[16,2,4,8,512]{4,3,2,1,0:T(8,128)(2,1)}), bf16[16,2,4,8,512]{4,3,2,1,0:T(8,128)(2,1)S(1)}, u32[]{:S(2)}, u32[]{:S(2)}) async-start(bf16[16,2,4,8,512]{4,3,2,1,0:T(8,128)(2,1)} %shard_map.113), calls=%async_computation.3 | async-start | bytes 2097152 | tf_op jit(solution)/shard_map/all_to_all | solution.py:36
  107.0 3.3 %collective-permute-start.5 = (bf16[16,4,8,512]{3,2,1,0:T(8,128)(2,1)S(1)}, bf16[16,4,8,512]{3,2,1,0:T(8,128)(2,1)S(1)}, u32[]{:S(2)}, u32[]{:S(2)}) collective-permute-start(bf16[16,4,8,512]{3,2,1,0:T(8,128)(2,1)S(1)} %slice_bitcast_fusion.1), channel_id=1, source_target_pairs={{0,1},{1,0},{2,3},{3,2},{4,5},{5,4},{6,7},{7,6},{8,9},{9,8},{10,11... | collective-permute-start | bytes 1572872 | tf_op jit(solution)/shard_map/ppermute | solution.py:22
  110.2 4.7 %shard_map.115 = (bf16[128,1152]{1,0:T(8,128)(2,1)}, bf16[128,1152]{1,0:T(8,128)(2,1)}, bf16[128,1152]{1,0:T(8,128)(2,1)}, f32[128,1152]{1,0:T(8,128)}) custom-call(s32[1]{0:T(128)} %bitcast.x_ref, s32[1]{0:T(128)} %bitcast.1.core_ref.at_ref, bf16[16,2,4,8,512]{4,3,2,1,0:T(8,128)(2,1)} %copy-done.1, bf16[16,4,8,512]{3,2,1,0:T(8,128)(2,1)} %get-tuple-element.51.kown_ref, ...), custom_call_target="tpu_custom_call" | custom-call | flops 1024 | bytes 1024 | tf_op jit(solution)/shard_map/pallas_call | solution.py:54
  114.9 1.2 collective-permute-start.6
  116.1 1.5 collective-permute-start.7
  117.6 1.5 collective-permute-start.8
  119.1 0.0 collective-permute-done.5.got_ref
  119.2 0.8 copy-done.7
  120.0 5.5 %shard_map.116 = (bf16[4,128,1024]{2,1,0:T(8,128)(2,1)}, bf16[4,128,1024]{2,1,0:T(8,128)(2,1)}, bf16[4,128,1024]{2,1,0:T(8,128)(2,1)}) custom-call(s32[1]{0:T(128)} %bitcast.1.core_ref.at_ref, bf16[16,2,4,8,512]{4,3,2,1,0:T(8,128)(2,1)} %copy-done.1, bf16[16,4,8,512]{3,2,1,0:T(8,128)(2,1)} %copy-done.7, ...), custom_call_target="tpu_custom_call" | custom-call | flops 1024 | bytes 1024 | tf_op jit(solution)/shard_map/pallas_call | solution.py:54
  125.5 0.0 collective-permute-done.6
  125.5 0.0 collective-permute-done.7
  125.5 0.7 copy-done.9
  126.2 0.7 copy-done.10
  126.9 5.5 %collective-permute-done.8 = bf16[128,1152]{1,0:T(8,128)(2,1)} collective-permute-done((bf16[128,1152]{1,0:T(8,128)(2,1)}, bf16[128,1152]{1,0:T(8,128)(2,1)}, u32[]{:S(2)}, u32[]{:S(2)}) %collective-permute-start.8) | collective-permute-done | bytes 294944 | tf_op jit(solution)/shard_map/ppermute | solution.py:32
  132.4 1.3 convert_add_fusion
  133.7 1.3 collective-permute-start.10
  135.0 1.5 collective-permute-start.11
  136.5 1.5 collective-permute-start.9
  137.9 0.0 all-to-all-done.3.mid_ref
  138.0 1.7 %collective-permute-start.12 = (bf16[16,4,8,512]{3,2,1,0:T(8,128)(2,1)S(1)}, bf16[16,4,8,512]{3,2,1,0:T(8,128)(2,1)S(1)}, u32[]{:S(2)}, u32[]{:S(2)}) collective-permute-start(bf16[16,4,8,512]{3,2,1,0:T(8,128)(2,1)S(1)} %slice_bitcast_fusion), channel_id=1, source_target_pairs={{0,1},{1,0},{2,3},{3,2},{4,5},{5,4},{6,7},{7,6},{8,9},{9,8},{10,11... | collective-permute-start | bytes 1572872 | tf_op jit(solution)/shard_map/ppermute | solution.py:22
  139.7 0.0 collective-permute-done.10
  139.7 0.0 collective-permute-done.11
  139.7 1.4 collective-permute-done.9
  141.2 3.1 %collective-permute-start.13 = (bf16[32,1152]{1,0:T(8,128)(2,1)S(1)}, bf16[32,1152]{1,0:T(8,128)(2,1)S(1)}, u32[]{:S(2)}, u32[]{:S(2)}) collective-permute-start(bf16[32,1152]{1,0:T(8,128)(2,1)S(1)} %fusion.2), channel_id=1, source_target_pairs={{0,128},{128,0},{1,129},{129,1},{2,130},{130,2},{3,131},{131,3},{4... | collective-permute-start | bytes 221192 | tf_op jit(solution)/shard_map/ppermute | solution.py:27
  144.3 0.0 collective-permute-done.12.got_ref
  144.3 0.8 copy-done.8
  145.1 2.0 %shard_map.117 = bf16[4,128,1024]{2,1,0:T(8,128)(2,1)} custom-call(s32[1]{0:T(128)} %bitcast.1.core_ref.at_ref, bf16[16,2,4,8,512]{4,3,2,1,0:T(8,128)(2,1)} %copy-done.3, bf16[16,4,8,512]{3,2,1,0:T(8,128)(2,1)} %copy-done.8), custom_call_target="tpu_custom_call" | custom-call | flops 1024 | bytes 1024 | tf_op jit(solution)/shard_map/pallas_call | solution.py:54
  147.1 0.0 collective-permute-done.13
  147.2 8.5 %collective-permute-start.14 = (bf16[32,1152]{1,0:T(8,128)(2,1)S(1)}, bf16[32,1152]{1,0:T(8,128)(2,1)S(1)}, u32[]{:S(2)}, u32[]{:S(2)}) collective-permute-start(bf16[32,1152]{1,0:T(8,128)(2,1)S(1)} %add_convert_fusion), channel_id=1, source_target_pairs={{0,0},{1,16},{2,2},{3,18},{4,4},{5,20},{6,6},{7,22},{8,32},{9,48},... | collective-permute-start | bytes 221192 | tf_op jit(solution)/shard_map/ppermute | solution.py:407
  155.6 0.1 collective-permute-start.15
  155.7 3.3 %collective-permute-start.16 = (bf16[32,1152]{1,0:T(8,128)(2,1)S(1)}, bf16[32,1152]{1,0:T(8,128)(2,1)S(1)}, u32[]{:S(2)}, u32[]{:S(2)}) collective-permute-start(bf16[32,1152]{1,0:T(8,128)(2,1)S(1)} %add_convert_fusion), channel_id=1, source_target_pairs={{0,64},{1,80},{2,66},{3,82},{4,68},{5,84},{6,70},{7,86},{8,96},{9,... | collective-permute-start | bytes 221192 | tf_op jit(solution)/shard_map/ppermute | solution.py:407
  159.0 1.9 %collective-permute-start.17 = (bf16[32,1152]{1,0:T(8,128)(2,1)S(1)}, bf16[32,1152]{1,0:T(8,128)(2,1)S(1)}, u32[]{:S(2)}, u32[]{:S(2)}) collective-permute-start(bf16[32,1152]{1,0:T(8,128)(2,1)S(1)} %add_convert_fusion), channel_id=1, source_target_pairs={{0,96},{1,112},{2,98},{3,114},{4,100},{5,116},{6,102},{7,118},{8,6... | collective-permute-start | bytes 221192 | tf_op jit(solution)/shard_map/ppermute | solution.py:407
  160.9 0.0 collective-permute-done.14
  160.9 0.1 collective-permute-done.15
  161.0 3.1 %collective-permute-done.16 = bf16[32,1152]{1,0:T(8,128)(2,1)S(1)} collective-permute-done((bf16[32,1152]{1,0:T(8,128)(2,1)S(1)}, bf16[32,1152]{1,0:T(8,128)(2,1)S(1)}, u32[]{:S(2)}, u32[]{:S(2)}) %collective-permute-start.16) | collective-permute-done | bytes 73760 | tf_op jit(solution)/shard_map/ppermute | solution.py:407
  164.1 7.3 %collective-permute-done.17 = bf16[32,1152]{1,0:T(8,128)(2,1)S(1)} collective-permute-done((bf16[32,1152]{1,0:T(8,128)(2,1)S(1)}, bf16[32,1152]{1,0:T(8,128)(2,1)S(1)}, u32[]{:S(2)}, u32[]{:S(2)}) %collective-permute-start.17) | collective-permute-done | bytes 73760 | tf_op jit(solution)/shard_map/ppermute | solution.py:407
  171.5 0.7 slice_multiply_fusion
  172.1 0.6 slice_multiply_fusion.1
  (26 shorter events, 0.3 us)
Async XLA Ops:
  2.9 36.6 %all-to-all-start = ((bf16[16,4,8,1024]{3,2,1,0:T(8,128)(2,1)}), bf16[16,4,8,1024]{3,2,1,0:T(8,128)(2,1)S(1)}, u32[]{:S(2)}, u32[]{:S(2)}) async-start(bf16[16,4,8,1024]{3,2,1,0:T(8,128)(2,1)} %shard_map.109), calls=%async_computation | async-start | bytes 2097152 | tf_op jit(solution)/shard_map/all_to_all | solution.py:36
  18.1 5.2 %collective-permute-start = (bf16[16,4,8,512]{3,2,1,0:T(8,128)(2,1)}, bf16[16,4,8,512]{3,2,1,0:T(8,128)(2,1)S(1)}, u32[]{:S(2)}, u32[]{:S(2)}) collective-permute-start(bf16[16,4,8,512]{3,2,1,0:T(8,128)(2,1)} %get-tuple-element.39), channel_id=1, source_target_pairs={{0,1},{1,0},{2,3},{3,2},{4,5},{5,4},{6,7},{7,6},{8,9},{9,8},{10,11... | collective-permute-start | bytes 1572872 | tf_op jit(solution)/shard_map/ppermute | solution.py:22
  23.2 22.6 %copy-start.5 = (bf16[16,4,8,1024]{3,2,1,0:T(8,128)(2,1)S(1)}, bf16[16,4,8,1024]{3,2,1,0:T(8,128)(2,1)}, u32[]{:S(2)}) copy-start(bf16[16,4,8,1024]{3,2,1,0:T(8,128)(2,1)} %get-tuple-element.46.own_ref) | copy-start | bytes 3145732
  39.5 12.6 %copy-start.2 = (bf16[16,4,8,1024]{3,2,1,0:T(8,128)(2,1)}, bf16[16,4,8,1024]{3,2,1,0:T(8,128)(2,1)S(1)}, u32[]{:S(2)}) copy-start(bf16[16,4,8,1024]{3,2,1,0:T(8,128)(2,1)S(1)} %all-to-all-done.own_ref.up_ref) | copy-start | bytes 3145732
  39.5 27.9 %all-to-all-start.1 = ((bf16[16,2,4,8,512]{4,3,2,1,0:T(8,128)(2,1)}), bf16[16,2,4,8,512]{4,3,2,1,0:T(8,128)(2,1)S(1)}, u32[]{:S(2)}, u32[]{:S(2)}) async-start(bf16[16,2,4,8,512]{4,3,2,1,0:T(8,128)(2,1)} %pad_maximum_fusion), calls=%async_computation.1 | async-start | bytes 2097152 | tf_op jit(solution)/shard_map/all_to_all | solution.py:36
  45.8 11.2 %collective-permute-start.3 = (bf16[16,4,8,1024]{3,2,1,0:T(8,128)(2,1)S(1)}, bf16[16,4,8,1024]{3,2,1,0:T(8,128)(2,1)}, u32[]{:S(2)}, u32[]{:S(2)}) collective-permute-start(bf16[16,4,8,1024]{3,2,1,0:T(8,128)(2,1)S(1)} %copy-done.5), channel_id=1, source_target_pairs={{0,1},{1,0},{2,3},{3,2},{4,5},{5,4},{6,7},{7,6},{8,9},{9,8},{10,11... | collective-permute-start | bytes 3145736 | tf_op jit(solution)/shard_map/ppermute | solution.py:22
  48.4 3.7 %collective-permute-start.1 = (bf16[16,4,8,512]{3,2,1,0:T(8,128)(2,1)S(1)}, bf16[16,4,8,512]{3,2,1,0:T(8,128)(2,1)S(1)}, u32[]{:S(2)}, u32[]{:S(2)}) collective-permute-start(bf16[16,4,8,512]{3,2,1,0:T(8,128)(2,1)S(1)} %constant_dynamic-slice_fusion), channel_id=1, source_target_pairs={{0,1},{1,0},{2,3},{3,2},{4,5},{5,4},{6,7},{7,6},{8,9},{9,8},{10,11... | collective-permute-start | bytes 1572872 | tf_op jit(solution)/shard_map/ppermute | solution.py:22
  48.5 8.5 %collective-permute-start.2 = (bf16[16,4,8,512]{3,2,1,0:T(8,128)(2,1)}, bf16[16,4,8,512]{3,2,1,0:T(8,128)(2,1)}, u32[]{:S(2)}, u32[]{:S(2)}) collective-permute-start(bf16[16,4,8,512]{3,2,1,0:T(8,128)(2,1)} %get-tuple-element.45.koth_ref), channel_id=1, source_target_pairs={{0,1},{1,0},{2,3},{3,2},{4,5},{5,4},{6,7},{7,6},{8,9},{9,8},{10,11... | collective-permute-start | bytes 1572872 | tf_op jit(solution)/shard_map/ppermute | solution.py:22
  52.1 0.8 copy-start.4
  67.5 8.9 %copy-start = (bf16[16,2,4,8,512]{4,3,2,1,0:T(8,128)(2,1)}, bf16[16,2,4,8,512]{4,3,2,1,0:T(8,128)(2,1)S(1)}, u32[]{:S(2)}) copy-start(bf16[16,2,4,8,512]{4,3,2,1,0:T(8,128)(2,1)S(1)} %all-to-all-done.1.own_ref.oth_ref.kern_ref) | copy-start | bytes 3145732
  67.5 29.6 %all-to-all-start.2 = ((bf16[16,2,4,8,512]{4,3,2,1,0:T(8,128)(2,1)}), bf16[16,2,4,8,512]{4,3,2,1,0:T(8,128)(2,1)S(1)}, u32[]{:S(2)}, u32[]{:S(2)}) async-start(bf16[16,2,4,8,512]{4,3,2,1,0:T(8,128)(2,1)} %shard_map.112), calls=%async_computation.2 | async-start | bytes 2097152 | tf_op jit(solution)/shard_map/all_to_all | solution.py:36
  81.3 6.2 %copy-start.11 = (f32[128,128]{1,0:T(8,128)S(1)}, f32[128,128]{1,0:T(8,128)}, u32[]{:S(2)}) copy-start(f32[128,128]{1,0:T(8,128)} %shard_map.114) | copy-start | bytes 196612
  81.3 6.2 %collective-permute-start.4 = (f32[128,128]{1,0:T(8,128)}, f32[128,128]{1,0:T(8,128)S(1)}, u32[]{:S(2)}, u32[]{:S(2)}) collective-permute-start(f32[128,128]{1,0:T(8,128)} %shard_map.114), channel_id=1, source_target_pairs={{0,1},{1,0},{2,3},{3,2},{4,5},{5,4},{6,7},{7,6},{8,9},{9,8},{10,11... | collective-permute-start | bytes 196616 | tf_op jit(solution)/shard_map/ppermute | solution.py:22
  97.1 13.1 %copy-start.1 = (bf16[16,2,4,8,512]{4,3,2,1,0:T(8,128)(2,1)}, bf16[16,2,4,8,512]{4,3,2,1,0:T(8,128)(2,1)S(1)}, u32[]{:S(2)}) copy-start(bf16[16,2,4,8,512]{4,3,2,1,0:T(8,128)(2,1)S(1)} %all-to-all-done.2.mid_ref) | copy-start | bytes 3145732
  97.1 40.9 %all-to-all-start.3 = ((bf16[16,2,4,8,512]{4,3,2,1,0:T(8,128)(2,1)}), bf16[16,2,4,8,512]{4,3,2,1,0:T(8,128)(2,1)S(1)}, u32[]{:S(2)}, u32[]{:S(2)}) async-start(bf16[16,2,4,8,512]{4,3,2,1,0:T(8,128)(2,1)} %shard_map.113), calls=%async_computation.3 | async-start | bytes 2097152 | tf_op jit(solution)/shard_map/all_to_all | solution.py:36
  107.0 12.2 %collective-permute-start.5 = (bf16[16,4,8,512]{3,2,1,0:T(8,128)(2,1)S(1)}, bf16[16,4,8,512]{3,2,1,0:T(8,128)(2,1)S(1)}, u32[]{:S(2)}, u32[]{:S(2)}) collective-permute-start(bf16[16,4,8,512]{3,2,1,0:T(8,128)(2,1)S(1)} %slice_bitcast_fusion.1), channel_id=1, source_target_pairs={{0,1},{1,0},{2,3},{3,2},{4,5},{5,4},{6,7},{7,6},{8,9},{9,8},{10,11... | collective-permute-start | bytes 1572872 | tf_op jit(solution)/shard_map/ppermute | solution.py:22
  114.9 10.5 %collective-permute-start.6 = (bf16[128,1152]{1,0:T(8,128)(2,1)}, bf16[128,1152]{1,0:T(8,128)(2,1)S(1)}, u32[]{:S(2)}, u32[]{:S(2)}) collective-permute-start(bf16[128,1152]{1,0:T(8,128)(2,1)} %get-tuple-element.61), channel_id=1, source_target_pairs={{0,32},{32,64},{64,96},{96,0},{1,33},{33,65},{65,97},{97,1},{2,34}... | collective-permute-start | bytes 884744 | tf_op jit(solution)/shard_map/ppermute | solution.py:32
  116.1 9.3 %collective-permute-start.7 = (bf16[128,1152]{1,0:T(8,128)(2,1)}, bf16[128,1152]{1,0:T(8,128)(2,1)S(1)}, u32[]{:S(2)}, u32[]{:S(2)}) collective-permute-start(bf16[128,1152]{1,0:T(8,128)(2,1)} %get-tuple-element.62), channel_id=1, source_target_pairs={{0,96},{32,0},{64,32},{96,64},{1,97},{33,1},{65,33},{97,65},{2,98}... | collective-permute-start | bytes 884744 | tf_op jit(solution)/shard_map/ppermute | solution.py:32
  117.6 14.8 %collective-permute-start.8 = (bf16[128,1152]{1,0:T(8,128)(2,1)}, bf16[128,1152]{1,0:T(8,128)(2,1)}, u32[]{:S(2)}, u32[]{:S(2)}) collective-permute-start(bf16[128,1152]{1,0:T(8,128)(2,1)} %get-tuple-element.63), channel_id=1, source_target_pairs={{0,64},{32,96},{64,0},{96,32},{1,65},{33,97},{65,1},{97,33},{2,66}... | collective-permute-start | bytes 884744 | tf_op jit(solution)/shard_map/ppermute | solution.py:32
  119.1 0.8 copy-start.7
  120.0 12.4 %copy-start.6 = (f32[128,1152]{1,0:T(8,128)S(1)}, f32[128,1152]{1,0:T(8,128)}, u32[]{:S(2)}) copy-start(f32[128,1152]{1,0:T(8,128)} %get-tuple-element.60) | copy-start | bytes 1769476
  125.5 0.7 copy-start.9
  126.2 0.7 copy-start.10
  133.7 6.0 %collective-permute-start.10 = (bf16[32,1152]{1,0:T(8,128)(2,1)S(1)}, bf16[32,1152]{1,0:T(8,128)(2,1)S(1)}, u32[]{:S(2)}, u32[]{:S(2)}) collective-permute-start(bf16[32,1152]{1,0:T(8,128)(2,1)S(1)} %get-tuple-element.72), channel_id=1, source_target_pairs={{0,2},{2,4},{4,6},{6,0},{1,3},{3,5},{5,7},{7,1},{8,10},{10,12},{12... | collective-permute-start | bytes 221192 | tf_op jit(solution)/shard_map/ppermute | solution.py:32
  135.0 4.8 %collective-permute-start.11 = (bf16[32,1152]{1,0:T(8,128)(2,1)S(1)}, bf16[32,1152]{1,0:T(8,128)(2,1)S(1)}, u32[]{:S(2)}, u32[]{:S(2)}) collective-permute-start(bf16[32,1152]{1,0:T(8,128)(2,1)S(1)} %get-tuple-element.71), channel_id=1, source_target_pairs={{0,6},{2,0},{4,2},{6,4},{1,7},{3,1},{5,3},{7,5},{8,14},{10,8},{12,... | collective-permute-start | bytes 221192 | tf_op jit(solution)/shard_map/ppermute | solution.py:32
  136.5 4.7 %collective-permute-start.9 = (bf16[32,1152]{1,0:T(8,128)(2,1)S(1)}, bf16[32,1152]{1,0:T(8,128)(2,1)S(1)}, u32[]{:S(2)}, u32[]{:S(2)}) collective-permute-start(bf16[32,1152]{1,0:T(8,128)(2,1)S(1)} %get-tuple-element.70), channel_id=1, source_target_pairs={{0,4},{2,6},{4,0},{6,2},{1,5},{3,7},{5,1},{7,3},{8,12},{10,14},{12... | collective-permute-start | bytes 221192 | tf_op jit(solution)/shard_map/ppermute | solution.py:32
  138.0 6.4 %copy-start.3 = (bf16[16,2,4,8,512]{4,3,2,1,0:T(8,128)(2,1)}, bf16[16,2,4,8,512]{4,3,2,1,0:T(8,128)(2,1)S(1)}, u32[]{:S(2)}) copy-start(bf16[16,2,4,8,512]{4,3,2,1,0:T(8,128)(2,1)S(1)} %all-to-all-done.3.mid_ref) | copy-start | bytes 3145732
  138.0 6.3 %collective-permute-start.12 = (bf16[16,4,8,512]{3,2,1,0:T(8,128)(2,1)S(1)}, bf16[16,4,8,512]{3,2,1,0:T(8,128)(2,1)S(1)}, u32[]{:S(2)}, u32[]{:S(2)}) collective-permute-start(bf16[16,4,8,512]{3,2,1,0:T(8,128)(2,1)S(1)} %slice_bitcast_fusion), channel_id=1, source_target_pairs={{0,1},{1,0},{2,3},{3,2},{4,5},{5,4},{6,7},{7,6},{8,9},{9,8},{10,11... | collective-permute-start | bytes 1572872 | tf_op jit(solution)/shard_map/ppermute | solution.py:22
  141.2 5.9 %collective-permute-start.13 = (bf16[32,1152]{1,0:T(8,128)(2,1)S(1)}, bf16[32,1152]{1,0:T(8,128)(2,1)S(1)}, u32[]{:S(2)}, u32[]{:S(2)}) collective-permute-start(bf16[32,1152]{1,0:T(8,128)(2,1)S(1)} %fusion.2), channel_id=1, source_target_pairs={{0,128},{128,0},{1,129},{129,1},{2,130},{130,2},{3,131},{131,3},{4... | collective-permute-start | bytes 221192 | tf_op jit(solution)/shard_map/ppermute | solution.py:27
  144.3 0.8 copy-start.8
  147.2 13.8 %collective-permute-start.14 = (bf16[32,1152]{1,0:T(8,128)(2,1)S(1)}, bf16[32,1152]{1,0:T(8,128)(2,1)S(1)}, u32[]{:S(2)}, u32[]{:S(2)}) collective-permute-start(bf16[32,1152]{1,0:T(8,128)(2,1)S(1)} %add_convert_fusion), channel_id=1, source_target_pairs={{0,0},{1,16},{2,2},{3,18},{4,4},{5,20},{6,6},{7,22},{8,32},{9,48},... | collective-permute-start | bytes 221192 | tf_op jit(solution)/shard_map/ppermute | solution.py:407
  155.6 5.4 %collective-permute-start.15 = (bf16[32,1152]{1,0:T(8,128)(2,1)S(1)}, bf16[32,1152]{1,0:T(8,128)(2,1)S(1)}, u32[]{:S(2)}, u32[]{:S(2)}) collective-permute-start(bf16[32,1152]{1,0:T(8,128)(2,1)S(1)} %add_convert_fusion), channel_id=1, source_target_pairs={{0,32},{1,48},{2,34},{3,50},{4,36},{5,52},{6,38},{7,54},{8,0},{9,1... | collective-permute-start | bytes 221192 | tf_op jit(solution)/shard_map/ppermute | solution.py:407
  155.7 8.4 %collective-permute-start.16 = (bf16[32,1152]{1,0:T(8,128)(2,1)S(1)}, bf16[32,1152]{1,0:T(8,128)(2,1)S(1)}, u32[]{:S(2)}, u32[]{:S(2)}) collective-permute-start(bf16[32,1152]{1,0:T(8,128)(2,1)S(1)} %add_convert_fusion), channel_id=1, source_target_pairs={{0,64},{1,80},{2,66},{3,82},{4,68},{5,84},{6,70},{7,86},{8,96},{9,... | collective-permute-start | bytes 221192 | tf_op jit(solution)/shard_map/ppermute | solution.py:407
  159.0 12.4 %collective-permute-start.17 = (bf16[32,1152]{1,0:T(8,128)(2,1)S(1)}, bf16[32,1152]{1,0:T(8,128)(2,1)S(1)}, u32[]{:S(2)}, u32[]{:S(2)}) collective-permute-start(bf16[32,1152]{1,0:T(8,128)(2,1)S(1)} %add_convert_fusion), channel_id=1, source_target_pairs={{0,96},{1,112},{2,98},{3,114},{4,100},{5,116},{6,102},{7,118},{8,6... | collective-permute-start | bytes 221192 | tf_op jit(solution)/shard_map/ppermute | solution.py:407

commit v4 on v3

--- a/solution.py
+++ b/solution.py
@@ -50,7 +50,7 @@
     return perm
 
 
-def call(body, scalars, operands, in_specs, out_shapes, out_specs, grid=(1,), scratch=()):
+def call(body, scalars, operands, in_specs, out_shapes, out_specs, grid=(1,), scratch=(), limit=LIMIT):
     return pl.pallas_call(
         body,
         out_shape=out_shapes,
@@ -61,7 +61,7 @@
             out_specs=out_specs,
             scratch_shapes=list(scratch),
         ),
-        compiler_params=pltpu.CompilerParams(vmem_limit_bytes=LIMIT),
+        compiler_params=pltpu.CompilerParams(vmem_limit_bytes=limit),
         cost_estimate=pl.CostEstimate(flops=1 << 10, bytes_accessed=1 << 10, transcendentals=0),
     )(*scalars, *operands)
 
@@ -292,6 +292,7 @@
         [whole(operand.shape) for operand in operands],
         [struct(out), struct(out), struct(out), struct(out, F32)],
         [whole(out)] * 4,
+        limit=40 * 1024 * 1024,
         scratch=[pltpu.VMEM((HALF, WIDTH), F32)],
     )
 

time: 174 us -> 172 us (0.989)
  waiting for transfers between devices: 54.1 us -> 47.2 us
  starting transfers between devices: 72 us -> 77.3 us
  local copies, waits for them, and re-layouts: 4.04 us -> 8.7 us
  Pallas kernels: 36.3 us -> 33.9 us
  other arithmetic: 5.48 us -> 3.71 us
    ppermute x7, starting transfers between devices: 11.5 us -> 20.2 us  [swap(): return lax.ppermute(value, 'c', [(0, 1), (1, 0)])]
    all_to_all x4, waiting for transfers between devices: 33.5 us -> 27.3 us  [exchange(): return lax.all_to_all(value, ('y', 'zh'), 0, 0, tiled=True)]
    all_to_all x4, starting transfers between devices: 35.2 us -> 29.5 us  [exchange(): return lax.all_to_all(value, ('y', 'zh'), 0, 0, tiled=True)]
    pallas_call x9, Pallas kernels: 36.3 us -> 33.9 us  [call(): pl.pallas_call(body, out_shape=out_shapes, grid_spec=pltpu.PrefetchScalar...]
    ppermute x1, starting transfers between devices: 3.08 us -> 5.53 us  [flip(): return lax.ppermute(value, axis, [(i, i ^ bit) for i in range(size)])]
    unnamed x24, local copies, waits for them, and re-layouts: 3.9 us -> 5.68 us
    ppermute x7, waiting for transfers between devices: 3.16 us -> 1.41 us  [swap(): return lax.ppermute(value, 'c', [(0, 1), (1, 0)])]
  transfers between devices with their start and end apart: 22 -> 22, of which waited for: 9 -> 9; matrix products, arithmetic and copies ran while one was open for 2% -> 3% of each run, Pallas kernels for 20% -> 18%
where the time goes in v4:
time: 172 us
  starting transfers between devices  77.3 us (45%)
  waiting for transfers between devices  47.2 us (27%)
  Pallas kernels  33.9 us (20%)
  local copies, waits for them, and re-layouts  8.7 us (5%)
  other arithmetic  3.71 us (2%)
    pallas_call x9, Pallas kernels, call(): pl.pallas_call(body, out_shape=out_shapes, grid_spec=pltpu.PrefetchScalar...  33.9 us
    all_to_all x4, starting transfers between devices, exchange(): return lax.all_to_all(value, ('y', 'zh'), 0, 0, tiled=True)  29.5 us
    all_to_all x4, waiting for transfers between devices, exchange(): return lax.all_to_all(value, ('y', 'zh'), 0, 0, tiled=True)  27.3 us
    ppermute x7, starting transfers between devices, swap(): return lax.ppermute(value, 'c', [(0, 1), (1, 0)])  20.2 us
    ppermute x4, starting transfers between devices, on_device(): lax.ppermute(part, AXES, to_owner(step)).astype(F32)  13.7 us
    ppermute x4, waiting for transfers between devices, on_device(): lax.ppermute(part, AXES, to_owner(step)).astype(F32)  10.3 us
    ppermute x6, starting transfers between devices, shift(): lax.ppermute(value, axis, [(i, (i + step) % size) for i in range(size)])  8.43 us
    ppermute x6, waiting for transfers between devices, shift(): lax.ppermute(value, axis, [(i, (i + step) % size) for i in range(size)])  8.17 us
  transfers between devices with their start and end apart: 22, of which 9 were waited for; matrix products, arithmetic and copies ran while one was open for 3% of the time, Pallas kernels for 18%

profile of v4, /device:TPU:65, one launch (start us, length us, event | category | flops | bytes accessed | tf_op | source)
XLA Modules:
  0.0 171.5 jit_solution(9882986295269128563)
XLA Ops:
  0.6 2.3 %shard_map.109 = bf16[16,4,8,1024]{3,2,1,0:T(8,128)(2,1)} custom-call(bf16[4,128,1024]{2,1,0:T(8,128)(2,1)} %in_ref.3), custom_call_target="tpu_custom_call" | custom-call | flops 1024 | bytes 1024 | tf_op jit(solution)/shard_map/pallas_call | solution.py:54
  2.9 10.2 %all-to-all-start = ((bf16[16,4,8,1024]{3,2,1,0:T(8,128)(2,1)}), bf16[16,4,8,1024]{3,2,1,0:T(8,128)(2,1)S(1)}, u32[]{:S(2)}, u32[]{:S(2)}) async-start(bf16[16,4,8,1024]{3,2,1,0:T(8,128)(2,1)} %shard_map.109), calls=%async_computation | async-start | bytes 2097152 | tf_op jit(solution)/shard_map/all_to_all | solution.py:36
  13.1 4.9 %shard_map.110 = (bf16[16,4,8,1024]{3,2,1,0:T(8,128)(2,1)}, bf16[16,4,8,1024]{3,2,1,0:T(8,128)(2,1)}, bf16[16,4,8,512]{3,2,1,0:T(8,128)(2,1)}, bf16[16,4,8,512]{...) custom-call(s32[1]{0:T(128)} %bitcast.1.core_ref.at_ref, ...), custom_call_target="tpu_custom_call" | custom-call | flops 1024 | bytes 1024 | tf_op jit(solution)/shard_map/pallas_call | solution.py:54
  18.0 1.3 collective-permute-start
  19.3 3.9 %shard_map.111 = (bf16[1024,1024]{1,0:T(8,128)(2,1)}, bf16[1024,1024]{1,0:T(8,128)(2,1)}) custom-call(s32[1]{0:T(128)} %bitcast.1.core_ref.at_ref, bf16[128,128]{1,0:T(8,128)(2,1)} %sf_ref.1), custom_call_target="tpu_custom_call" | custom-call | flops 1024 | bytes 1024 | tf_op jit(solution)/shard_map/pallas_call | solution.py:54
  23.2 0.0 collective-permute-done
  23.2 2.2 %pad_maximum_fusion = bf16[16,2,4,8,512]{4,3,2,1,0:T(8,128)(2,1)} fusion(bf16[16,1,4,8,512]{4,3,2,1,0:T(8,128)(2,1)S(1)} %bitcast.28, bf16[16,1,4,8,512]{4,3,2,1,0:T(8,128)(2,1)} %bitcast.27), kind=kLoop, calls=%fused_computation | loop fusion | flops 524288 | bytes 2097152 | tf_op jit(solution)/shard_map/stack | solution.py:371
  25.4 14.1 %all-to-all-done.own_ref.up_ref = bf16[16,4,8,1024]{3,2,1,0:T(8,128)(2,1)S(1)} async-done(((bf16[16,4,8,1024]{3,2,1,0:T(8,128)(2,1)}), bf16[16,4,8,1024]{3,2,1,0:T(8,128)(2,1)S(1)}, u32[]{:S(2)}, u32[]{:S(2)}) %all-to-all-start) | async-done | bytes 1048608 | tf_op jit(solution)/shard_map/all_to_all | solution.py:36
  39.5 6.3 %all-to-all-start.1 = ((bf16[16,2,4,8,512]{4,3,2,1,0:T(8,128)(2,1)}), bf16[16,2,4,8,512]{4,3,2,1,0:T(8,128)(2,1)}, u32[]{:S(2)}, u32[]{:S(2)}) async-start(bf16[16,2,4,8,512]{4,3,2,1,0:T(8,128)(2,1)} %pad_maximum_fusion), calls=%async_computation.1 | async-start | bytes 2097152 | tf_op jit(solution)/shard_map/all_to_all | solution.py:36
  45.8 3.1 %collective-permute-start.3 = (bf16[16,4,8,1024]{3,2,1,0:T(8,128)(2,1)S(1)}, bf16[16,4,8,1024]{3,2,1,0:T(8,128)(2,1)S(1)}, u32[]{:S(2)}, u32[]{:S(2)}) collective-permute-start(bf16[16,4,8,1024]{3,2,1,0:T(8,128)(2,1)S(1)} %copy-done.2), channel_id=1, source_target_pairs={{0,1},{1,0},{2,3},{3,2},{4,5},{5,4},{6,7},{7,6},{8,9},{9,8},{10,11... | collective-permute-start | bytes 3145736 | tf_op jit(solution)/shard_map/ppermute | solution.py:22
  49.0 1.1 constant_dynamic-slice_fusion
  50.0 0.1 collective-permute-start.1
  50.1 0.5 collective-permute-start.2
  50.6 1.4 collective-permute-done.1.oth_ref.up_oth_ref
  52.0 0.8 copy-done.8
  52.8 4.0 %shard_map.112 = bf16[16,2,4,8,512]{4,3,2,1,0:T(8,128)(2,1)} custom-call(s32[1]{0:T(128)} %bitcast.1.core_ref.at_ref, bf16[1024,1024]{1,0:T(8,128)(2,1)} %get-tuple-element.42.wide_ref, bf16[16,4,8,1024]{3,2,1,0:T(8,128)(2,1)} %copy-done.7, bf16[16,4,8,512]{3,2,1,0:T(8,128)(2,1)} %copy-done.8), custom_call_target="tpu_custom_call" | custom-call | flops 1024 | bytes 1024 | tf_op jit(solution)/shard_map/pallas_call | solution.py:54
  56.9 0.0 collective-permute-done.2.koth_ref
  56.9 0.8 copy-done.5
  57.7 0.0 collective-permute-done.3.oth_ref
  57.7 1.0 copy-done.3
  58.7 8.9 %all-to-all-done.1.own_ref.oth_ref.kern_ref = bf16[16,2,4,8,512]{4,3,2,1,0:T(8,128)(2,1)} async-done(((bf16[16,2,4,8,512]{4,3,2,1,0:T(8,128)(2,1)}), bf16[16,2,4,8,512]{4,3,2,1,0:T(8,128)(2,1)}, u32[]{:S(2)}, u32[]{:S(2)}) %all-to-all-start.1) | async-done | bytes 1048608 | tf_op jit(solution)/shard_map/all_to_all | solution.py:36
  67.6 5.9 %all-to-all-start.2 = ((bf16[16,2,4,8,512]{4,3,2,1,0:T(8,128)(2,1)}), bf16[16,2,4,8,512]{4,3,2,1,0:T(8,128)(2,1)S(1)}, u32[]{:S(2)}, u32[]{:S(2)}) async-start(bf16[16,2,4,8,512]{4,3,2,1,0:T(8,128)(2,1)} %shard_map.112), calls=%async_computation.2 | async-start | bytes 2097152 | tf_op jit(solution)/shard_map/all_to_all | solution.py:36
  73.4 4.9 %shard_map.114 = f32[128,128]{1,0:T(8,128)} custom-call(s32[1]{0:T(128)} %bitcast.1.core_ref.at_ref, bf16[16,4,8,1024]{3,2,1,0:T(8,128)(2,1)} %copy-done.7, bf16[16,4,8,512]{3,2,1,0:T(8,128)(2,1)} %copy-done.8, bf16[16,2,4,8,512]{4,3,2,1,0:T(8,128)(2,1)} %all-to-all-done.1.own_ref.oth_ref.kern_ref), custom_call_target="tpu_custom_call" | custom-call | flops 1024 | bytes 1024 | tf_op jit(solution)/shard_map/pallas_call | solution.py:54
  78.3 5.2 %collective-permute-start.4 = (f32[128,128]{1,0:T(8,128)}, f32[128,128]{1,0:T(8,128)S(1)}, u32[]{:S(2)}, u32[]{:S(2)}) collective-permute-start(f32[128,128]{1,0:T(8,128)} %shard_map.114), channel_id=1, source_target_pairs={{0,1},{1,0},{2,3},{3,2},{4,5},{5,4},{6,7},{7,6},{8,9},{9,8},{10,11... | collective-permute-start | bytes 196616 | tf_op jit(solution)/shard_map/ppermute | solution.py:22
  83.6 4.0 %shard_map.113 = bf16[16,2,4,8,512]{4,3,2,1,0:T(8,128)(2,1)} custom-call(s32[1]{0:T(128)} %bitcast.1.core_ref.at_ref, bf16[1024,1024]{1,0:T(8,128)(2,1)} %get-tuple-element.48.wide_ref, bf16[16,2,4,8,512]{4,3,2,1,0:T(8,128)(2,1)} %all-to-all-done.1.own_ref.oth_ref.kern_ref, bf16[16,2,4,8,512]{4,3,2,1,0:T(8,128)(2,1)} %all-to-all-done.1.own_ref.oth_ref.kern_ref), custom_call_target="tpu_custom_call" | custom-call | flops 1024 | bytes 1024 | tf_op jit(solution)/shard_map/pallas_call | solution.py:54
  87.6 0.0 collective-permute-done.4
  87.6 4.3 %all-to-all-done.2.mid_ref = bf16[16,2,4,8,512]{4,3,2,1,0:T(8,128)(2,1)S(1)} async-done(((bf16[16,2,4,8,512]{4,3,2,1,0:T(8,128)(2,1)}), bf16[16,2,4,8,512]{4,3,2,1,0:T(8,128)(2,1)S(1)}, u32[]{:S(2)}, u32[]{:S(2)}) %all-to-all-start.2) | async-done | bytes 1048608 | tf_op jit(solution)/shard_map/all_to_all | solution.py:36
  91.9 7.2 %all-to-all-start.3 = ((bf16[16,2,4,8,512]{4,3,2,1,0:T(8,128)(2,1)}), bf16[16,2,4,8,512]{4,3,2,1,0:T(8,128)(2,1)}, u32[]{:S(2)}, u32[]{:S(2)}) async-start(bf16[16,2,4,8,512]{4,3,2,1,0:T(8,128)(2,1)} %shard_map.113), calls=%async_computation.3 | async-start | bytes 2097152 | tf_op jit(solution)/shard_map/all_to_all | solution.py:36
  99.1 0.8 slice_bitcast_fusion.1
  99.9 8.2 %collective-permute-start.5 = (bf16[16,4,8,512]{3,2,1,0:T(8,128)(2,1)}, bf16[16,4,8,512]{3,2,1,0:T(8,128)(2,1)}, u32[]{:S(2)}, u32[]{:S(2)}) collective-permute-start(bf16[16,4,8,512]{3,2,1,0:T(8,128)(2,1)} %slice_bitcast_fusion.1), channel_id=1, source_target_pairs={{0,1},{1,0},{2,3},{3,2},{4,5},{5,4},{6,7},{7,6},{8,9},{9,8},{10,11... | collective-permute-start | bytes 1572872 | tf_op jit(solution)/shard_map/ppermute | solution.py:22
  108.2 1.2 copy-done.4
  109.4 1.0 copy-done.6
  110.4 2.3 %shard_map.115 = (bf16[128,1152]{1,0:T(8,128)(2,1)}, bf16[128,1152]{1,0:T(8,128)(2,1)}, bf16[128,1152]{1,0:T(8,128)(2,1)}, f32[128,1152]{1,0:T(8,128)S(1)}) custom-call(s32[1]{0:T(128)} %bitcast.x_ref, s32[1]{0:T(128)} %bitcast.1.core_ref.at_ref, bf16[16,2,4,8,512]{4,3,2,1,0:T(8,128)(2,1)S(1)} %all-to-all-done.2.mid_ref, ...), custom_call_target="tpu_custom_call" | custom-call | flops 1024 | bytes 1024 | tf_op jit(solution)/shard_map/pallas_call | solution.py:54
  112.8 1.2 collective-permute-start.6
  114.0 1.5 collective-permute-start.7
  115.4 1.5 collective-permute-start.8
  117.0 0.0 collective-permute-done.5.got_ref
  117.0 5.4 %shard_map.116 = (bf16[4,128,1024]{2,1,0:T(8,128)(2,1)}, bf16[4,128,1024]{2,1,0:T(8,128)(2,1)}, bf16[4,128,1024]{2,1,0:T(8,128)(2,1)}) custom-call(s32[1]{0:T(128)} %bitcast.1.core_ref.at_ref, bf16[16,2,4,8,512]{4,3,2,1,0:T(8,128)(2,1)} %copy-done, bf16[16,4,8,512]{3,2,1,0:T(8,128)(2,1)} %collective-permute-done.5.got_ref, ...), custom_call_target="tpu_custom_call" | custom-call | flops 1024 | bytes 1024 | tf_op jit(solution)/shard_map/pallas_call | solution.py:54
  122.4 0.5 collective-permute-done.6
  122.9 0.0 collective-permute-done.7
  122.9 7.2 %collective-permute-done.8 = bf16[128,1152]{1,0:T(8,128)(2,1)S(1)} collective-permute-done((bf16[128,1152]{1,0:T(8,128)(2,1)}, bf16[128,1152]{1,0:T(8,128)(2,1)S(1)}, u32[]{:S(2)}, u32[]{:S(2)}) %collective-permute-start.8) | collective-permute-done | bytes 294944 | tf_op jit(solution)/shard_map/ppermute | solution.py:32
  130.1 0.1 convert_add_fusion
  130.3 1.3 collective-permute-start.10
  131.6 1.5 collective-permute-start.11
  133.1 1.5 collective-permute-start.9
  134.6 0.0 all-to-all-done.3.mid_ref
  134.6 1.1 slice_bitcast_fusion
  135.6 1.7 collective-permute-start.12
  137.4 0.0 collective-permute-done.11
  137.4 0.4 collective-permute-done.9
  137.8 5.5 %collective-permute-start.13 = (bf16[32,1152]{1,0:T(8,128)(2,1)S(1)}, bf16[32,1152]{1,0:T(8,128)(2,1)S(1)}, u32[]{:S(2)}, u32[]{:S(2)}) collective-permute-start(bf16[32,1152]{1,0:T(8,128)(2,1)S(1)} %fusion.2), channel_id=1, source_target_pairs={{0,128},{128,0},{1,129},{129,1},{2,130},{130,2},{3,131},{131,3},{4... | collective-permute-start | bytes 221192 | tf_op jit(solution)/shard_map/ppermute | solution.py:27
  143.4 0.8 copy-done.10
  144.2 2.0 %shard_map.117 = bf16[4,128,1024]{2,1,0:T(8,128)(2,1)} custom-call(s32[1]{0:T(128)} %bitcast.1.core_ref.at_ref, bf16[16,2,4,8,512]{4,3,2,1,0:T(8,128)(2,1)} %all-to-all-done.3.mid_ref, bf16[16,4,8,512]{3,2,1,0:T(8,128)(2,1)} %copy-done.10), custom_call_target="tpu_custom_call" | custom-call | flops 1024 | bytes 1024 | tf_op jit(solution)/shard_map/pallas_call | solution.py:54
  146.2 0.0 collective-permute-done.13
  146.2 8.3 %collective-permute-start.14 = (bf16[32,1152]{1,0:T(8,128)(2,1)S(1)}, bf16[32,1152]{1,0:T(8,128)(2,1)S(1)}, u32[]{:S(2)}, u32[]{:S(2)}) collective-permute-start(bf16[32,1152]{1,0:T(8,128)(2,1)S(1)} %add_convert_fusion), channel_id=1, source_target_pairs={{0,0},{1,16},{2,2},{3,18},{4,4},{5,20},{6,6},{7,22},{8,32},{9,48},... | collective-permute-start | bytes 221192 | tf_op jit(solution)/shard_map/ppermute | solution.py:408
  154.6 0.1 collective-permute-start.15
  154.7 3.3 %collective-permute-start.16 = (bf16[32,1152]{1,0:T(8,128)(2,1)S(1)}, bf16[32,1152]{1,0:T(8,128)(2,1)S(1)}, u32[]{:S(2)}, u32[]{:S(2)}) collective-permute-start(bf16[32,1152]{1,0:T(8,128)(2,1)S(1)} %add_convert_fusion), channel_id=1, source_target_pairs={{0,64},{1,80},{2,66},{3,82},{4,68},{5,84},{6,70},{7,86},{8,96},{9,... | collective-permute-start | bytes 221192 | tf_op jit(solution)/shard_map/ppermute | solution.py:408
  158.0 1.9 %collective-permute-start.17 = (bf16[32,1152]{1,0:T(8,128)(2,1)S(1)}, bf16[32,1152]{1,0:T(8,128)(2,1)S(1)}, u32[]{:S(2)}, u32[]{:S(2)}) collective-permute-start(bf16[32,1152]{1,0:T(8,128)(2,1)S(1)} %add_convert_fusion), channel_id=1, source_target_pairs={{0,96},{1,112},{2,98},{3,114},{4,100},{5,116},{6,102},{7,118},{8,6... | collective-permute-start | bytes 221192 | tf_op jit(solution)/shard_map/ppermute | solution.py:408
  159.9 0.0 collective-permute-done.14
  160.0 0.0 collective-permute-done.15
  160.0 2.9 %collective-permute-done.16 = bf16[32,1152]{1,0:T(8,128)(2,1)S(1)} collective-permute-done((bf16[32,1152]{1,0:T(8,128)(2,1)S(1)}, bf16[32,1152]{1,0:T(8,128)(2,1)S(1)}, u32[]{:S(2)}, u32[]{:S(2)}) %collective-permute-start.16) | collective-permute-done | bytes 73760 | tf_op jit(solution)/shard_map/ppermute | solution.py:408
  162.9 7.4 %collective-permute-done.17 = bf16[32,1152]{1,0:T(8,128)(2,1)S(1)} collective-permute-done((bf16[32,1152]{1,0:T(8,128)(2,1)S(1)}, bf16[32,1152]{1,0:T(8,128)(2,1)S(1)}, u32[]{:S(2)}, u32[]{:S(2)}) %collective-permute-start.17) | collective-permute-done | bytes 73760 | tf_op jit(solution)/shard_map/ppermute | solution.py:408
  170.3 0.7 slice_multiply_fusion
  171.0 0.6 slice_multiply_fusion.1
  (26 shorter events, 0.2 us)
Async XLA Ops:
  2.9 36.6 %all-to-all-start = ((bf16[16,4,8,1024]{3,2,1,0:T(8,128)(2,1)}), bf16[16,4,8,1024]{3,2,1,0:T(8,128)(2,1)S(1)}, u32[]{:S(2)}, u32[]{:S(2)}) async-start(bf16[16,4,8,1024]{3,2,1,0:T(8,128)(2,1)} %shard_map.109), calls=%async_computation | async-start | bytes 2097152 | tf_op jit(solution)/shard_map/all_to_all | solution.py:36
  18.0 5.2 %collective-permute-start = (bf16[16,4,8,512]{3,2,1,0:T(8,128)(2,1)}, bf16[16,4,8,512]{3,2,1,0:T(8,128)(2,1)S(1)}, u32[]{:S(2)}, u32[]{:S(2)}) collective-permute-start(bf16[16,4,8,512]{3,2,1,0:T(8,128)(2,1)} %get-tuple-element.39), channel_id=1, source_target_pairs={{0,1},{1,0},{2,3},{3,2},{4,5},{5,4},{6,7},{7,6},{8,9},{9,8},{10,11... | collective-permute-start | bytes 1572872 | tf_op jit(solution)/shard_map/ppermute | solution.py:22
  23.2 22.6 %copy-start.2 = (bf16[16,4,8,1024]{3,2,1,0:T(8,128)(2,1)S(1)}, bf16[16,4,8,1024]{3,2,1,0:T(8,128)(2,1)}, u32[]{:S(2)}) copy-start(bf16[16,4,8,1024]{3,2,1,0:T(8,128)(2,1)} %get-tuple-element.46.own_ref) | copy-start | bytes 3145732
  25.4 24.7 %copy-start.9 = (bf16[16,4,8,512]{3,2,1,0:T(8,128)(2,1)S(1)}, bf16[16,4,8,512]{3,2,1,0:T(8,128)(2,1)}, u32[]{:S(2)}) copy-start(bf16[16,4,8,512]{3,2,1,0:T(8,128)(2,1)} %get-tuple-element.45.koth_ref) | copy-start | bytes 1572868
  39.5 6.3 %copy-start.7 = (bf16[16,4,8,1024]{3,2,1,0:T(8,128)(2,1)}, bf16[16,4,8,1024]{3,2,1,0:T(8,128)(2,1)S(1)}, u32[]{:S(2)}) copy-start(bf16[16,4,8,1024]{3,2,1,0:T(8,128)(2,1)S(1)} %all-to-all-done.own_ref.up_ref) | copy-start | bytes 3145732
  39.5 28.0 %all-to-all-start.1 = ((bf16[16,2,4,8,512]{4,3,2,1,0:T(8,128)(2,1)}), bf16[16,2,4,8,512]{4,3,2,1,0:T(8,128)(2,1)}, u32[]{:S(2)}, u32[]{:S(2)}) async-start(bf16[16,2,4,8,512]{4,3,2,1,0:T(8,128)(2,1)} %pad_maximum_fusion), calls=%async_computation.1 | async-start | bytes 2097152 | tf_op jit(solution)/shard_map/all_to_all | solution.py:36
  45.8 11.8 %collective-permute-start.3 = (bf16[16,4,8,1024]{3,2,1,0:T(8,128)(2,1)S(1)}, bf16[16,4,8,1024]{3,2,1,0:T(8,128)(2,1)S(1)}, u32[]{:S(2)}, u32[]{:S(2)}) collective-permute-start(bf16[16,4,8,1024]{3,2,1,0:T(8,128)(2,1)S(1)} %copy-done.2), channel_id=1, source_target_pairs={{0,1},{1,0},{2,3},{3,2},{4,5},{5,4},{6,7},{7,6},{8,9},{9,8},{10,11... | collective-permute-start | bytes 3145736 | tf_op jit(solution)/shard_map/ppermute | solution.py:22
  50.0 2.0 %collective-permute-start.1 = (bf16[16,4,8,512]{3,2,1,0:T(8,128)(2,1)S(1)}, bf16[16,4,8,512]{3,2,1,0:T(8,128)(2,1)S(1)}, u32[]{:S(2)}, u32[]{:S(2)}) collective-permute-start(bf16[16,4,8,512]{3,2,1,0:T(8,128)(2,1)S(1)} %constant_dynamic-slice_fusion), channel_id=1, source_target_pairs={{0,1},{1,0},{2,3},{3,2},{4,5},{5,4},{6,7},{7,6},{8,9},{9,8},{10,11... | collective-permute-start | bytes 1572872 | tf_op jit(solution)/shard_map/ppermute | solution.py:22
  50.1 6.7 %collective-permute-start.2 = (bf16[16,4,8,512]{3,2,1,0:T(8,128)(2,1)S(1)}, bf16[16,4,8,512]{3,2,1,0:T(8,128)(2,1)S(1)}, u32[]{:S(2)}, u32[]{:S(2)}) collective-permute-start(bf16[16,4,8,512]{3,2,1,0:T(8,128)(2,1)S(1)} %copy-done.9), channel_id=1, source_target_pairs={{0,1},{1,0},{2,3},{3,2},{4,5},{5,4},{6,7},{7,6},{8,9},{9,8},{10,11... | collective-permute-start | bytes 1572872 | tf_op jit(solution)/shard_map/ppermute | solution.py:22
  52.0 0.8 copy-start.8
  56.9 0.8 copy-start.5
  57.7 1.0 copy-start.3
  67.6 24.4 %all-to-all-start.2 = ((bf16[16,2,4,8,512]{4,3,2,1,0:T(8,128)(2,1)}), bf16[16,2,4,8,512]{4,3,2,1,0:T(8,128)(2,1)S(1)}, u32[]{:S(2)}, u32[]{:S(2)}) async-start(bf16[16,2,4,8,512]{4,3,2,1,0:T(8,128)(2,1)} %shard_map.112), calls=%async_computation.2 | async-start | bytes 2097152 | tf_op jit(solution)/shard_map/all_to_all | solution.py:36
  78.3 9.3 %copy-start.11 = (f32[128,128]{1,0:T(8,128)S(1)}, f32[128,128]{1,0:T(8,128)}, u32[]{:S(2)}) copy-start(f32[128,128]{1,0:T(8,128)} %shard_map.114) | copy-start | bytes 196612
  78.3 9.3 %collective-permute-start.4 = (f32[128,128]{1,0:T(8,128)}, f32[128,128]{1,0:T(8,128)S(1)}, u32[]{:S(2)}, u32[]{:S(2)}) collective-permute-start(f32[128,128]{1,0:T(8,128)} %shard_map.114), channel_id=1, source_target_pairs={{0,1},{1,0},{2,3},{3,2},{4,5},{5,4},{6,7},{7,6},{8,9},{9,8},{10,11... | collective-permute-start | bytes 196616 | tf_op jit(solution)/shard_map/ppermute | solution.py:22
  87.6 20.6 %copy-start.1 = (bf16[16,4,8,512]{3,2,1,0:T(8,128)(2,1)S(1)}, bf16[16,4,8,512]{3,2,1,0:T(8,128)(2,1)}, u32[]{:S(2)}) copy-start(bf16[16,4,8,512]{3,2,1,0:T(8,128)(2,1)} %get-tuple-element.51.kown_ref) | copy-start | bytes 1572868
  91.9 20.8 %copy-start = (bf16[16,2,4,8,512]{4,3,2,1,0:T(8,128)(2,1)}, bf16[16,2,4,8,512]{4,3,2,1,0:T(8,128)(2,1)S(1)}, u32[]{:S(2)}) copy-start(bf16[16,2,4,8,512]{4,3,2,1,0:T(8,128)(2,1)S(1)} %all-to-all-done.2.mid_ref) | copy-start | bytes 3145732
  91.9 42.6 %all-to-all-start.3 = ((bf16[16,2,4,8,512]{4,3,2,1,0:T(8,128)(2,1)}), bf16[16,2,4,8,512]{4,3,2,1,0:T(8,128)(2,1)}, u32[]{:S(2)}, u32[]{:S(2)}) async-start(bf16[16,2,4,8,512]{4,3,2,1,0:T(8,128)(2,1)} %shard_map.113), calls=%async_computation.3 | async-start | bytes 2097152 | tf_op jit(solution)/shard_map/all_to_all | solution.py:36
  99.9 17.1 %collective-permute-start.5 = (bf16[16,4,8,512]{3,2,1,0:T(8,128)(2,1)}, bf16[16,4,8,512]{3,2,1,0:T(8,128)(2,1)}, u32[]{:S(2)}, u32[]{:S(2)}) collective-permute-start(bf16[16,4,8,512]{3,2,1,0:T(8,128)(2,1)} %slice_bitcast_fusion.1), channel_id=1, source_target_pairs={{0,1},{1,0},{2,3},{3,2},{4,5},{5,4},{6,7},{7,6},{8,9},{9,8},{10,11... | collective-permute-start | bytes 1572872 | tf_op jit(solution)/shard_map/ppermute | solution.py:22
  108.2 1.2 copy-start.4
  109.4 1.0 copy-start.6
  112.8 10.2 %collective-permute-start.6 = (bf16[128,1152]{1,0:T(8,128)(2,1)}, bf16[128,1152]{1,0:T(8,128)(2,1)S(1)}, u32[]{:S(2)}, u32[]{:S(2)}) collective-permute-start(bf16[128,1152]{1,0:T(8,128)(2,1)} %get-tuple-element.61), channel_id=1, source_target_pairs={{0,32},{32,64},{64,96},{96,0},{1,33},{33,65},{65,97},{97,1},{2,34}... | collective-permute-start | bytes 884744 | tf_op jit(solution)/shard_map/ppermute | solution.py:32
  114.0 9.0 %collective-permute-start.7 = (bf16[128,1152]{1,0:T(8,128)(2,1)}, bf16[128,1152]{1,0:T(8,128)(2,1)S(1)}, u32[]{:S(2)}, u32[]{:S(2)}) collective-permute-start(bf16[128,1152]{1,0:T(8,128)(2,1)} %get-tuple-element.62), channel_id=1, source_target_pairs={{0,96},{32,0},{64,32},{96,64},{1,97},{33,1},{65,33},{97,65},{2,98}... | collective-permute-start | bytes 884744 | tf_op jit(solution)/shard_map/ppermute | solution.py:32
  115.4 14.7 %collective-permute-start.8 = (bf16[128,1152]{1,0:T(8,128)(2,1)}, bf16[128,1152]{1,0:T(8,128)(2,1)S(1)}, u32[]{:S(2)}, u32[]{:S(2)}) collective-permute-start(bf16[128,1152]{1,0:T(8,128)(2,1)} %get-tuple-element.63), channel_id=1, source_target_pairs={{0,64},{32,96},{64,0},{96,32},{1,65},{33,97},{65,1},{97,33},{2,66}... | collective-permute-start | bytes 884744 | tf_op jit(solution)/shard_map/ppermute | solution.py:32
  130.3 7.0 %collective-permute-start.10 = (bf16[32,1152]{1,0:T(8,128)(2,1)S(1)}, bf16[32,1152]{1,0:T(8,128)(2,1)S(1)}, u32[]{:S(2)}, u32[]{:S(2)}) collective-permute-start(bf16[32,1152]{1,0:T(8,128)(2,1)S(1)} %get-tuple-element.72), channel_id=1, source_target_pairs={{0,2},{2,4},{4,6},{6,0},{1,3},{3,5},{5,7},{7,1},{8,10},{10,12},{12... | collective-permute-start | bytes 221192 | tf_op jit(solution)/shard_map/ppermute | solution.py:32
  131.6 5.8 %collective-permute-start.11 = (bf16[32,1152]{1,0:T(8,128)(2,1)S(1)}, bf16[32,1152]{1,0:T(8,128)(2,1)S(1)}, u32[]{:S(2)}, u32[]{:S(2)}) collective-permute-start(bf16[32,1152]{1,0:T(8,128)(2,1)S(1)} %get-tuple-element.71), channel_id=1, source_target_pairs={{0,6},{2,0},{4,2},{6,4},{1,7},{3,1},{5,3},{7,5},{8,14},{10,8},{12,... | collective-permute-start | bytes 221192 | tf_op jit(solution)/shard_map/ppermute | solution.py:32
  133.1 4.7 %collective-permute-start.9 = (bf16[32,1152]{1,0:T(8,128)(2,1)S(1)}, bf16[32,1152]{1,0:T(8,128)(2,1)S(1)}, u32[]{:S(2)}, u32[]{:S(2)}) collective-permute-start(bf16[32,1152]{1,0:T(8,128)(2,1)S(1)} %get-tuple-element.70), channel_id=1, source_target_pairs={{0,4},{2,6},{4,0},{6,2},{1,5},{3,7},{5,1},{7,3},{8,12},{10,14},{12... | collective-permute-start | bytes 221192 | tf_op jit(solution)/shard_map/ppermute | solution.py:32
  135.6 7.7 %collective-permute-start.12 = (bf16[16,4,8,512]{3,2,1,0:T(8,128)(2,1)S(1)}, bf16[16,4,8,512]{3,2,1,0:T(8,128)(2,1)S(1)}, u32[]{:S(2)}, u32[]{:S(2)}) collective-permute-start(bf16[16,4,8,512]{3,2,1,0:T(8,128)(2,1)S(1)} %slice_bitcast_fusion), channel_id=1, source_target_pairs={{0,1},{1,0},{2,3},{3,2},{4,5},{5,4},{6,7},{7,6},{8,9},{9,8},{10,11... | collective-permute-start | bytes 1572872 | tf_op jit(solution)/shard_map/ppermute | solution.py:22
  137.8 8.4 %collective-permute-start.13 = (bf16[32,1152]{1,0:T(8,128)(2,1)S(1)}, bf16[32,1152]{1,0:T(8,128)(2,1)S(1)}, u32[]{:S(2)}, u32[]{:S(2)}) collective-permute-start(bf16[32,1152]{1,0:T(8,128)(2,1)S(1)} %fusion.2), channel_id=1, source_target_pairs={{0,128},{128,0},{1,129},{129,1},{2,130},{130,2},{3,131},{131,3},{4... | collective-permute-start | bytes 221192 | tf_op jit(solution)/shard_map/ppermute | solution.py:27
  143.4 0.8 copy-start.10
  146.2 13.7 %collective-permute-start.14 = (bf16[32,1152]{1,0:T(8,128)(2,1)S(1)}, bf16[32,1152]{1,0:T(8,128)(2,1)S(1)}, u32[]{:S(2)}, u32[]{:S(2)}) collective-permute-start(bf16[32,1152]{1,0:T(8,128)(2,1)S(1)} %add_convert_fusion), channel_id=1, source_target_pairs={{0,0},{1,16},{2,2},{3,18},{4,4},{5,20},{6,6},{7,22},{8,32},{9,48},... | collective-permute-start | bytes 221192 | tf_op jit(solution)/shard_map/ppermute | solution.py:408
  154.6 5.4 %collective-permute-start.15 = (bf16[32,1152]{1,0:T(8,128)(2,1)S(1)}, bf16[32,1152]{1,0:T(8,128)(2,1)S(1)}, u32[]{:S(2)}, u32[]{:S(2)}) collective-permute-start(bf16[32,1152]{1,0:T(8,128)(2,1)S(1)} %add_convert_fusion), channel_id=1, source_target_pairs={{0,32},{1,48},{2,34},{3,50},{4,36},{5,52},{6,38},{7,54},{8,0},{9,1... | collective-permute-start | bytes 221192 | tf_op jit(solution)/shard_map/ppermute | solution.py:408
  154.7 8.2 %collective-permute-start.16 = (bf16[32,1152]{1,0:T(8,128)(2,1)S(1)}, bf16[32,1152]{1,0:T(8,128)(2,1)S(1)}, u32[]{:S(2)}, u32[]{:S(2)}) collective-permute-start(bf16[32,1152]{1,0:T(8,128)(2,1)S(1)} %add_convert_fusion), channel_id=1, source_target_pairs={{0,64},{1,80},{2,66},{3,82},{4,68},{5,84},{6,70},{7,86},{8,96},{9,... | collective-permute-start | bytes 221192 | tf_op jit(solution)/shard_map/ppermute | solution.py:408
  158.0 12.2 %collective-permute-start.17 = (bf16[32,1152]{1,0:T(8,128)(2,1)S(1)}, bf16[32,1152]{1,0:T(8,128)(2,1)S(1)}, u32[]{:S(2)}, u32[]{:S(2)}) collective-permute-start(bf16[32,1152]{1,0:T(8,128)(2,1)S(1)} %add_convert_fusion), channel_id=1, source_target_pairs={{0,96},{1,112},{2,98},{3,114},{4,100},{5,116},{6,102},{7,118},{8,6... | collective-permute-start | bytes 221192 | tf_op jit(solution)/shard_map/ppermute | solution.py:408

commit v5 on v4

--- a/solution.py
+++ b/solution.py
@@ -91,6 +91,7 @@
         [whole((LOCAL, CHANNELS, WIDTH))],
         struct((PEERS, LOCAL, ROWS, WIDTH)),
         whole((PEERS, LOCAL, ROWS, WIDTH)),
+        limit=16 * 1024 * 1024,
     )
 
 

time: 172 us -> 172 us (level)
    unnamed x24 -> x26, local copies, waits for them, and re-layouts: 5.68 us -> 6.88 us
where the time goes in v5:
time: 172 us
  starting transfers between devices  77.3 us (45%)
  waiting for transfers between devices  47.2 us (27%)
  Pallas kernels  32.6 us (19%)
  local copies, waits for them, and re-layouts  9.9 us (6%)
  other arithmetic  3.71 us (2%)
    pallas_call x9, Pallas kernels, call(): pl.pallas_call(body, out_shape=out_shapes, grid_spec=pltpu.PrefetchScalar...  32.6 us
    all_to_all x4, starting transfers between devices, exchange(): return lax.all_to_all(value, ('y', 'zh'), 0, 0, tiled=True)  29.5 us
    all_to_all x4, waiting for transfers between devices, exchange(): return lax.all_to_all(value, ('y', 'zh'), 0, 0, tiled=True)  27.3 us
    ppermute x7, starting transfers between devices, swap(): return lax.ppermute(value, 'c', [(0, 1), (1, 0)])  20.2 us
    ppermute x4, starting transfers between devices, on_device(): lax.ppermute(part, AXES, to_owner(step)).astype(F32)  13.7 us
    ppermute x4, waiting for transfers between devices, on_device(): lax.ppermute(part, AXES, to_owner(step)).astype(F32)  10.3 us
    ppermute x6, starting transfers between devices, shift(): lax.ppermute(value, axis, [(i, (i + step) % size) for i in range(size)])  8.44 us
    ppermute x6, waiting for transfers between devices, shift(): lax.ppermute(value, axis, [(i, (i + step) % size) for i in range(size)])  8.15 us
  transfers between devices with their start and end apart: 22, of which 9 were waited for; matrix products, arithmetic and copies ran while one was open for 3% of the time, Pallas kernels for 18%

profile of v5, /device:TPU:65, one launch (start us, length us, event | category | flops | bytes accessed | tf_op | source)
XLA Modules:
  0.0 171.5 jit_solution(5612139701749809543)
XLA Ops:
  0.6 1.2 copy-done.5
  1.9 1.0 shard_map.109
  2.9 10.2 %all-to-all-start = ((bf16[16,4,8,1024]{3,2,1,0:T(8,128)(2,1)}), bf16[16,4,8,1024]{3,2,1,0:T(8,128)(2,1)S(1)}, u32[]{:S(2)}, u32[]{:S(2)}) async-start(bf16[16,4,8,1024]{3,2,1,0:T(8,128)(2,1)} %shard_map.109), calls=%async_computation | async-start | bytes 2097152 | tf_op jit(solution)/shard_map/all_to_all | solution.py:36
  13.1 4.9 %shard_map.110 = (bf16[16,4,8,1024]{3,2,1,0:T(8,128)(2,1)}, bf16[16,4,8,1024]{3,2,1,0:T(8,128)(2,1)}, bf16[16,4,8,512]{3,2,1,0:T(8,128)(2,1)}, bf16[16,4,8,512]{...) custom-call(s32[1]{0:T(128)} %bitcast.1.core_ref.at_ref, ...), custom_call_target="tpu_custom_call" | custom-call | flops 1024 | bytes 1024 | tf_op jit(solution)/shard_map/pallas_call | solution.py:54
  18.0 1.3 collective-permute-start
  19.3 3.9 %shard_map.111 = (bf16[1024,1024]{1,0:T(8,128)(2,1)}, bf16[1024,1024]{1,0:T(8,128)(2,1)}) custom-call(s32[1]{0:T(128)} %bitcast.1.core_ref.at_ref, bf16[128,128]{1,0:T(8,128)(2,1)} %sf_ref.1), custom_call_target="tpu_custom_call" | custom-call | flops 1024 | bytes 1024 | tf_op jit(solution)/shard_map/pallas_call | solution.py:54
  23.2 0.0 collective-permute-done
  23.2 2.2 %pad_maximum_fusion = bf16[16,2,4,8,512]{4,3,2,1,0:T(8,128)(2,1)} fusion(bf16[16,1,4,8,512]{4,3,2,1,0:T(8,128)(2,1)S(1)} %bitcast.28, bf16[16,1,4,8,512]{4,3,2,1,0:T(8,128)(2,1)} %bitcast.27), kind=kLoop, calls=%fused_computation | loop fusion | flops 524288 | bytes 2097152 | tf_op jit(solution)/shard_map/stack | solution.py:372
  25.4 14.1 %all-to-all-done.own_ref.up_ref = bf16[16,4,8,1024]{3,2,1,0:T(8,128)(2,1)S(1)} async-done(((bf16[16,4,8,1024]{3,2,1,0:T(8,128)(2,1)}), bf16[16,4,8,1024]{3,2,1,0:T(8,128)(2,1)S(1)}, u32[]{:S(2)}, u32[]{:S(2)}) %all-to-all-start) | async-done | bytes 1048608 | tf_op jit(solution)/shard_map/all_to_all | solution.py:36
  39.5 6.3 %all-to-all-start.1 = ((bf16[16,2,4,8,512]{4,3,2,1,0:T(8,128)(2,1)}), bf16[16,2,4,8,512]{4,3,2,1,0:T(8,128)(2,1)}, u32[]{:S(2)}, u32[]{:S(2)}) async-start(bf16[16,2,4,8,512]{4,3,2,1,0:T(8,128)(2,1)} %pad_maximum_fusion), calls=%async_computation.1 | async-start | bytes 2097152 | tf_op jit(solution)/shard_map/all_to_all | solution.py:36
  45.8 3.1 %collective-permute-start.3 = (bf16[16,4,8,1024]{3,2,1,0:T(8,128)(2,1)S(1)}, bf16[16,4,8,1024]{3,2,1,0:T(8,128)(2,1)S(1)}, u32[]{:S(2)}, u32[]{:S(2)}) collective-permute-start(bf16[16,4,8,1024]{3,2,1,0:T(8,128)(2,1)S(1)} %copy-done.2), channel_id=1, source_target_pairs={{0,1},{1,0},{2,3},{3,2},{4,5},{5,4},{6,7},{7,6},{8,9},{9,8},{10,11... | collective-permute-start | bytes 3145736 | tf_op jit(solution)/shard_map/ppermute | solution.py:22
  49.0 1.1 constant_dynamic-slice_fusion
  50.0 0.1 collective-permute-start.1
  50.1 0.5 collective-permute-start.2
  50.6 1.4 collective-permute-done.1.oth_ref.up_oth_ref
  52.0 0.8 copy-done.9
  52.8 4.0 %shard_map.112 = bf16[16,2,4,8,512]{4,3,2,1,0:T(8,128)(2,1)} custom-call(s32[1]{0:T(128)} %bitcast.1.core_ref.at_ref, bf16[1024,1024]{1,0:T(8,128)(2,1)} %get-tuple-element.42.wide_ref, bf16[16,4,8,1024]{3,2,1,0:T(8,128)(2,1)} %copy-done.8, bf16[16,4,8,512]{3,2,1,0:T(8,128)(2,1)} %copy-done.9), custom_call_target="tpu_custom_call" | custom-call | flops 1024 | bytes 1024 | tf_op jit(solution)/shard_map/pallas_call | solution.py:54
  56.8 0.0 collective-permute-done.2.koth_ref
  56.9 0.8 copy-done.6
  57.6 0.0 collective-permute-done.3.oth_ref
  57.7 1.0 copy-done.3
  58.6 8.9 %all-to-all-done.1.own_ref.oth_ref.kern_ref = bf16[16,2,4,8,512]{4,3,2,1,0:T(8,128)(2,1)} async-done(((bf16[16,2,4,8,512]{4,3,2,1,0:T(8,128)(2,1)}), bf16[16,2,4,8,512]{4,3,2,1,0:T(8,128)(2,1)}, u32[]{:S(2)}, u32[]{:S(2)}) %all-to-all-start.1) | async-done | bytes 1048608 | tf_op jit(solution)/shard_map/all_to_all | solution.py:36
  67.6 5.9 %all-to-all-start.2 = ((bf16[16,2,4,8,512]{4,3,2,1,0:T(8,128)(2,1)}), bf16[16,2,4,8,512]{4,3,2,1,0:T(8,128)(2,1)S(1)}, u32[]{:S(2)}, u32[]{:S(2)}) async-start(bf16[16,2,4,8,512]{4,3,2,1,0:T(8,128)(2,1)} %shard_map.112), calls=%async_computation.2 | async-start | bytes 2097152 | tf_op jit(solution)/shard_map/all_to_all | solution.py:36
  73.4 4.9 %shard_map.114 = f32[128,128]{1,0:T(8,128)} custom-call(s32[1]{0:T(128)} %bitcast.1.core_ref.at_ref, bf16[16,4,8,1024]{3,2,1,0:T(8,128)(2,1)} %copy-done.8, bf16[16,4,8,512]{3,2,1,0:T(8,128)(2,1)} %copy-done.9, bf16[16,2,4,8,512]{4,3,2,1,0:T(8,128)(2,1)} %all-to-all-done.1.own_ref.oth_ref.kern_ref), custom_call_target="tpu_custom_call" | custom-call | flops 1024 | bytes 1024 | tf_op jit(solution)/shard_map/pallas_call | solution.py:54
  78.3 5.2 %collective-permute-start.4 = (f32[128,128]{1,0:T(8,128)}, f32[128,128]{1,0:T(8,128)S(1)}, u32[]{:S(2)}, u32[]{:S(2)}) collective-permute-start(f32[128,128]{1,0:T(8,128)} %shard_map.114), channel_id=1, source_target_pairs={{0,1},{1,0},{2,3},{3,2},{4,5},{5,4},{6,7},{7,6},{8,9},{9,8},{10,11... | collective-permute-start | bytes 196616 | tf_op jit(solution)/shard_map/ppermute | solution.py:22
  83.6 4.0 %shard_map.113 = bf16[16,2,4,8,512]{4,3,2,1,0:T(8,128)(2,1)} custom-call(s32[1]{0:T(128)} %bitcast.1.core_ref.at_ref, bf16[1024,1024]{1,0:T(8,128)(2,1)} %get-tuple-element.48.wide_ref, bf16[16,2,4,8,512]{4,3,2,1,0:T(8,128)(2,1)} %all-to-all-done.1.own_ref.oth_ref.kern_ref, bf16[16,2,4,8,512]{4,3,2,1,0:T(8,128)(2,1)} %all-to-all-done.1.own_ref.oth_ref.kern_ref), custom_call_target="tpu_custom_call" | custom-call | flops 1024 | bytes 1024 | tf_op jit(solution)/shard_map/pallas_call | solution.py:54
  87.6 0.0 collective-permute-done.4
  87.6 4.3 %all-to-all-done.2.mid_ref = bf16[16,2,4,8,512]{4,3,2,1,0:T(8,128)(2,1)S(1)} async-done(((bf16[16,2,4,8,512]{4,3,2,1,0:T(8,128)(2,1)}), bf16[16,2,4,8,512]{4,3,2,1,0:T(8,128)(2,1)S(1)}, u32[]{:S(2)}, u32[]{:S(2)}) %all-to-all-start.2) | async-done | bytes 1048608 | tf_op jit(solution)/shard_map/all_to_all | solution.py:36
  91.9 7.2 %all-to-all-start.3 = ((bf16[16,2,4,8,512]{4,3,2,1,0:T(8,128)(2,1)}), bf16[16,2,4,8,512]{4,3,2,1,0:T(8,128)(2,1)}, u32[]{:S(2)}, u32[]{:S(2)}) async-start(bf16[16,2,4,8,512]{4,3,2,1,0:T(8,128)(2,1)} %shard_map.113), calls=%async_computation.3 | async-start | bytes 2097152 | tf_op jit(solution)/shard_map/all_to_all | solution.py:36
  99.1 0.8 slice_bitcast_fusion.1
  99.9 8.2 %collective-permute-start.5 = (bf16[16,4,8,512]{3,2,1,0:T(8,128)(2,1)}, bf16[16,4,8,512]{3,2,1,0:T(8,128)(2,1)}, u32[]{:S(2)}, u32[]{:S(2)}) collective-permute-start(bf16[16,4,8,512]{3,2,1,0:T(8,128)(2,1)} %slice_bitcast_fusion.1), channel_id=1, source_target_pairs={{0,1},{1,0},{2,3},{3,2},{4,5},{5,4},{6,7},{7,6},{8,9},{9,8},{10,11... | collective-permute-start | bytes 1572872 | tf_op jit(solution)/shard_map/ppermute | solution.py:22
  108.2 1.2 copy-done.4
  109.4 1.0 copy-done.7
  110.4 2.3 %shard_map.115 = (bf16[128,1152]{1,0:T(8,128)(2,1)}, bf16[128,1152]{1,0:T(8,128)(2,1)}, bf16[128,1152]{1,0:T(8,128)(2,1)}, f32[128,1152]{1,0:T(8,128)S(1)}) custom-call(s32[1]{0:T(128)} %bitcast.x_ref, s32[1]{0:T(128)} %bitcast.1.core_ref.at_ref, bf16[16,2,4,8,512]{4,3,2,1,0:T(8,128)(2,1)S(1)} %all-to-all-done.2.mid_ref, ...), custom_call_target="tpu_custom_call" | custom-call | flops 1024 | bytes 1024 | tf_op jit(solution)/shard_map/pallas_call | solution.py:54
  112.8 1.2 collective-permute-start.6
  114.0 1.5 collective-permute-start.7
  115.4 1.5 collective-permute-start.8
  117.0 5.4 %shard_map.116 = (bf16[4,128,1024]{2,1,0:T(8,128)(2,1)}, bf16[4,128,1024]{2,1,0:T(8,128)(2,1)}, bf16[4,128,1024]{2,1,0:T(8,128)(2,1)}) custom-call(s32[1]{0:T(128)} %bitcast.1.core_ref.at_ref, bf16[16,2,4,8,512]{4,3,2,1,0:T(8,128)(2,1)} %copy-done, bf16[16,4,8,512]{3,2,1,0:T(8,128)(2,1)} %collective-permute-done.5.got_ref, ...), custom_call_target="tpu_custom_call" | custom-call | flops 1024 | bytes 1024 | tf_op jit(solution)/shard_map/pallas_call | solution.py:54
  122.4 0.5 collective-permute-done.6
  122.9 0.0 collective-permute-done.7
  122.9 7.2 %collective-permute-done.8 = bf16[128,1152]{1,0:T(8,128)(2,1)S(1)} collective-permute-done((bf16[128,1152]{1,0:T(8,128)(2,1)}, bf16[128,1152]{1,0:T(8,128)(2,1)S(1)}, u32[]{:S(2)}, u32[]{:S(2)}) %collective-permute-start.8) | collective-permute-done | bytes 294944 | tf_op jit(solution)/shard_map/ppermute | solution.py:32
  130.1 0.1 convert_add_fusion
  130.3 1.3 collective-permute-start.10
  131.6 1.5 collective-permute-start.11
  133.1 1.5 collective-permute-start.9
  134.6 0.0 all-to-all-done.3.mid_ref
  134.6 1.1 slice_bitcast_fusion
  135.6 1.7 collective-permute-start.12
  137.4 0.0 collective-permute-done.10
  137.4 0.0 collective-permute-done.11
  137.4 0.4 collective-permute-done.9
  137.8 5.5 %collective-permute-start.13 = (bf16[32,1152]{1,0:T(8,128)(2,1)S(1)}, bf16[32,1152]{1,0:T(8,128)(2,1)S(1)}, u32[]{:S(2)}, u32[]{:S(2)}) collective-permute-start(bf16[32,1152]{1,0:T(8,128)(2,1)S(1)} %fusion.2), channel_id=1, source_target_pairs={{0,128},{128,0},{1,129},{129,1},{2,130},{130,2},{3,131},{131,3},{4... | collective-permute-start | bytes 221192 | tf_op jit(solution)/shard_map/ppermute | solution.py:27
  143.4 0.0 collective-permute-done.12.got_ref
  143.4 0.8 copy-done.11
  144.2 2.0 %shard_map.117 = bf16[4,128,1024]{2,1,0:T(8,128)(2,1)} custom-call(s32[1]{0:T(128)} %bitcast.1.core_ref.at_ref, bf16[16,2,4,8,512]{4,3,2,1,0:T(8,128)(2,1)} %all-to-all-done.3.mid_ref, bf16[16,4,8,512]{3,2,1,0:T(8,128)(2,1)} %copy-done.11), custom_call_target="tpu_custom_call" | custom-call | flops 1024 | bytes 1024 | tf_op jit(solution)/shard_map/pallas_call | solution.py:54
  146.2 8.3 %collective-permute-start.14 = (bf16[32,1152]{1,0:T(8,128)(2,1)S(1)}, bf16[32,1152]{1,0:T(8,128)(2,1)S(1)}, u32[]{:S(2)}, u32[]{:S(2)}) collective-permute-start(bf16[32,1152]{1,0:T(8,128)(2,1)S(1)} %add_convert_fusion), channel_id=1, source_target_pairs={{0,0},{1,16},{2,2},{3,18},{4,4},{5,20},{6,6},{7,22},{8,32},{9,48},... | collective-permute-start | bytes 221192 | tf_op jit(solution)/shard_map/ppermute | solution.py:409
  154.6 0.1 collective-permute-start.15
  154.7 3.3 %collective-permute-start.16 = (bf16[32,1152]{1,0:T(8,128)(2,1)S(1)}, bf16[32,1152]{1,0:T(8,128)(2,1)S(1)}, u32[]{:S(2)}, u32[]{:S(2)}) collective-permute-start(bf16[32,1152]{1,0:T(8,128)(2,1)S(1)} %add_convert_fusion), channel_id=1, source_target_pairs={{0,64},{1,80},{2,66},{3,82},{4,68},{5,84},{6,70},{7,86},{8,96},{9,... | collective-permute-start | bytes 221192 | tf_op jit(solution)/shard_map/ppermute | solution.py:409
  158.0 1.9 %collective-permute-start.17 = (bf16[32,1152]{1,0:T(8,128)(2,1)S(1)}, bf16[32,1152]{1,0:T(8,128)(2,1)S(1)}, u32[]{:S(2)}, u32[]{:S(2)}) collective-permute-start(bf16[32,1152]{1,0:T(8,128)(2,1)S(1)} %add_convert_fusion), channel_id=1, source_target_pairs={{0,96},{1,112},{2,98},{3,114},{4,100},{5,116},{6,102},{7,118},{8,6... | collective-permute-start | bytes 221192 | tf_op jit(solution)/shard_map/ppermute | solution.py:409
  159.9 0.0 collective-permute-done.15
  160.0 2.9 %collective-permute-done.16 = bf16[32,1152]{1,0:T(8,128)(2,1)S(1)} collective-permute-done((bf16[32,1152]{1,0:T(8,128)(2,1)S(1)}, bf16[32,1152]{1,0:T(8,128)(2,1)S(1)}, u32[]{:S(2)}, u32[]{:S(2)}) %collective-permute-start.16) | collective-permute-done | bytes 73760 | tf_op jit(solution)/shard_map/ppermute | solution.py:409
  162.8 7.4 %collective-permute-done.17 = bf16[32,1152]{1,0:T(8,128)(2,1)S(1)} collective-permute-done((bf16[32,1152]{1,0:T(8,128)(2,1)S(1)}, bf16[32,1152]{1,0:T(8,128)(2,1)S(1)}, u32[]{:S(2)}, u32[]{:S(2)}) %collective-permute-start.17) | collective-permute-done | bytes 73760 | tf_op jit(solution)/shard_map/ppermute | solution.py:409
  170.3 0.7 slice_multiply_fusion
  170.9 0.6 slice_multiply_fusion.1
  (28 shorter events, 0.2 us)
Async XLA Ops:
  0.6 1.2 copy-start.5
  2.9 36.6 %all-to-all-start = ((bf16[16,4,8,1024]{3,2,1,0:T(8,128)(2,1)}), bf16[16,4,8,1024]{3,2,1,0:T(8,128)(2,1)S(1)}, u32[]{:S(2)}, u32[]{:S(2)}) async-start(bf16[16,4,8,1024]{3,2,1,0:T(8,128)(2,1)} %shard_map.109), calls=%async_computation | async-start | bytes 2097152 | tf_op jit(solution)/shard_map/all_to_all | solution.py:36
  18.0 5.2 %collective-permute-start = (bf16[16,4,8,512]{3,2,1,0:T(8,128)(2,1)}, bf16[16,4,8,512]{3,2,1,0:T(8,128)(2,1)S(1)}, u32[]{:S(2)}, u32[]{:S(2)}) collective-permute-start(bf16[16,4,8,512]{3,2,1,0:T(8,128)(2,1)} %get-tuple-element.39), channel_id=1, source_target_pairs={{0,1},{1,0},{2,3},{3,2},{4,5},{5,4},{6,7},{7,6},{8,9},{9,8},{10,11... | collective-permute-start | bytes 1572872 | tf_op jit(solution)/shard_map/ppermute | solution.py:22
  23.2 22.6 %copy-start.2 = (bf16[16,4,8,1024]{3,2,1,0:T(8,128)(2,1)S(1)}, bf16[16,4,8,1024]{3,2,1,0:T(8,128)(2,1)}, u32[]{:S(2)}) copy-start(bf16[16,4,8,1024]{3,2,1,0:T(8,128)(2,1)} %get-tuple-element.46.own_ref) | copy-start | bytes 3145732
  25.4 24.7 %copy-start.10 = (bf16[16,4,8,512]{3,2,1,0:T(8,128)(2,1)S(1)}, bf16[16,4,8,512]{3,2,1,0:T(8,128)(2,1)}, u32[]{:S(2)}) copy-start(bf16[16,4,8,512]{3,2,1,0:T(8,128)(2,1)} %get-tuple-element.45.koth_ref) | copy-start | bytes 1572868
  39.5 6.3 %copy-start.8 = (bf16[16,4,8,1024]{3,2,1,0:T(8,128)(2,1)}, bf16[16,4,8,1024]{3,2,1,0:T(8,128)(2,1)S(1)}, u32[]{:S(2)}) copy-start(bf16[16,4,8,1024]{3,2,1,0:T(8,128)(2,1)S(1)} %all-to-all-done.own_ref.up_ref) | copy-start | bytes 3145732
  39.5 28.0 %all-to-all-start.1 = ((bf16[16,2,4,8,512]{4,3,2,1,0:T(8,128)(2,1)}), bf16[16,2,4,8,512]{4,3,2,1,0:T(8,128)(2,1)}, u32[]{:S(2)}, u32[]{:S(2)}) async-start(bf16[16,2,4,8,512]{4,3,2,1,0:T(8,128)(2,1)} %pad_maximum_fusion), calls=%async_computation.1 | async-start | bytes 2097152 | tf_op jit(solution)/shard_map/all_to_all | solution.py:36
  45.8 11.8 %collective-permute-start.3 = (bf16[16,4,8,1024]{3,2,1,0:T(8,128)(2,1)S(1)}, bf16[16,4,8,1024]{3,2,1,0:T(8,128)(2,1)S(1)}, u32[]{:S(2)}, u32[]{:S(2)}) collective-permute-start(bf16[16,4,8,1024]{3,2,1,0:T(8,128)(2,1)S(1)} %copy-done.2), channel_id=1, source_target_pairs={{0,1},{1,0},{2,3},{3,2},{4,5},{5,4},{6,7},{7,6},{8,9},{9,8},{10,11... | collective-permute-start | bytes 3145736 | tf_op jit(solution)/shard_map/ppermute | solution.py:22
  50.0 2.0 %collective-permute-start.1 = (bf16[16,4,8,512]{3,2,1,0:T(8,128)(2,1)S(1)}, bf16[16,4,8,512]{3,2,1,0:T(8,128)(2,1)S(1)}, u32[]{:S(2)}, u32[]{:S(2)}) collective-permute-start(bf16[16,4,8,512]{3,2,1,0:T(8,128)(2,1)S(1)} %constant_dynamic-slice_fusion), channel_id=1, source_target_pairs={{0,1},{1,0},{2,3},{3,2},{4,5},{5,4},{6,7},{7,6},{8,9},{9,8},{10,11... | collective-permute-start | bytes 1572872 | tf_op jit(solution)/shard_map/ppermute | solution.py:22
  50.1 6.7 %collective-permute-start.2 = (bf16[16,4,8,512]{3,2,1,0:T(8,128)(2,1)S(1)}, bf16[16,4,8,512]{3,2,1,0:T(8,128)(2,1)S(1)}, u32[]{:S(2)}, u32[]{:S(2)}) collective-permute-start(bf16[16,4,8,512]{3,2,1,0:T(8,128)(2,1)S(1)} %copy-done.10), channel_id=1, source_target_pairs={{0,1},{1,0},{2,3},{3,2},{4,5},{5,4},{6,7},{7,6},{8,9},{9,8},{10,11... | collective-permute-start | bytes 1572872 | tf_op jit(solution)/shard_map/ppermute | solution.py:22
  52.0 0.8 copy-start.9
  56.8 0.8 copy-start.6
  57.6 1.0 copy-start.3
  67.6 24.4 %all-to-all-start.2 = ((bf16[16,2,4,8,512]{4,3,2,1,0:T(8,128)(2,1)}), bf16[16,2,4,8,512]{4,3,2,1,0:T(8,128)(2,1)S(1)}, u32[]{:S(2)}, u32[]{:S(2)}) async-start(bf16[16,2,4,8,512]{4,3,2,1,0:T(8,128)(2,1)} %shard_map.112), calls=%async_computation.2 | async-start | bytes 2097152 | tf_op jit(solution)/shard_map/all_to_all | solution.py:36
  78.3 9.3 %copy-start.12 = (f32[128,128]{1,0:T(8,128)S(1)}, f32[128,128]{1,0:T(8,128)}, u32[]{:S(2)}) copy-start(f32[128,128]{1,0:T(8,128)} %shard_map.114) | copy-start | bytes 196612
  78.3 9.3 %collective-permute-start.4 = (f32[128,128]{1,0:T(8,128)}, f32[128,128]{1,0:T(8,128)S(1)}, u32[]{:S(2)}, u32[]{:S(2)}) collective-permute-start(f32[128,128]{1,0:T(8,128)} %shard_map.114), channel_id=1, source_target_pairs={{0,1},{1,0},{2,3},{3,2},{4,5},{5,4},{6,7},{7,6},{8,9},{9,8},{10,11... | collective-permute-start | bytes 196616 | tf_op jit(solution)/shard_map/ppermute | solution.py:22
  87.6 20.5 %copy-start.1 = (bf16[16,4,8,512]{3,2,1,0:T(8,128)(2,1)S(1)}, bf16[16,4,8,512]{3,2,1,0:T(8,128)(2,1)}, u32[]{:S(2)}) copy-start(bf16[16,4,8,512]{3,2,1,0:T(8,128)(2,1)} %get-tuple-element.51.kown_ref) | copy-start | bytes 1572868
  91.9 20.8 %copy-start = (bf16[16,2,4,8,512]{4,3,2,1,0:T(8,128)(2,1)}, bf16[16,2,4,8,512]{4,3,2,1,0:T(8,128)(2,1)S(1)}, u32[]{:S(2)}) copy-start(bf16[16,2,4,8,512]{4,3,2,1,0:T(8,128)(2,1)S(1)} %all-to-all-done.2.mid_ref) | copy-start | bytes 3145732
  91.9 42.6 %all-to-all-start.3 = ((bf16[16,2,4,8,512]{4,3,2,1,0:T(8,128)(2,1)}), bf16[16,2,4,8,512]{4,3,2,1,0:T(8,128)(2,1)}, u32[]{:S(2)}, u32[]{:S(2)}) async-start(bf16[16,2,4,8,512]{4,3,2,1,0:T(8,128)(2,1)} %shard_map.113), calls=%async_computation.3 | async-start | bytes 2097152 | tf_op jit(solution)/shard_map/all_to_all | solution.py:36
  99.9 17.1 %collective-permute-start.5 = (bf16[16,4,8,512]{3,2,1,0:T(8,128)(2,1)}, bf16[16,4,8,512]{3,2,1,0:T(8,128)(2,1)}, u32[]{:S(2)}, u32[]{:S(2)}) collective-permute-start(bf16[16,4,8,512]{3,2,1,0:T(8,128)(2,1)} %slice_bitcast_fusion.1), channel_id=1, source_target_pairs={{0,1},{1,0},{2,3},{3,2},{4,5},{5,4},{6,7},{7,6},{8,9},{9,8},{10,11... | collective-permute-start | bytes 1572872 | tf_op jit(solution)/shard_map/ppermute | solution.py:22
  108.2 1.2 copy-start.4
  109.4 1.0 copy-start.7
  112.8 10.2 %collective-permute-start.6 = (bf16[128,1152]{1,0:T(8,128)(2,1)}, bf16[128,1152]{1,0:T(8,128)(2,1)S(1)}, u32[]{:S(2)}, u32[]{:S(2)}) collective-permute-start(bf16[128,1152]{1,0:T(8,128)(2,1)} %get-tuple-element.61), channel_id=1, source_target_pairs={{0,32},{32,64},{64,96},{96,0},{1,33},{33,65},{65,97},{97,1},{2,34}... | collective-permute-start | bytes 884744 | tf_op jit(solution)/shard_map/ppermute | solution.py:32
  114.0 9.0 %collective-permute-start.7 = (bf16[128,1152]{1,0:T(8,128)(2,1)}, bf16[128,1152]{1,0:T(8,128)(2,1)S(1)}, u32[]{:S(2)}, u32[]{:S(2)}) collective-permute-start(bf16[128,1152]{1,0:T(8,128)(2,1)} %get-tuple-element.62), channel_id=1, source_target_pairs={{0,96},{32,0},{64,32},{96,64},{1,97},{33,1},{65,33},{97,65},{2,98}... | collective-permute-start | bytes 884744 | tf_op jit(solution)/shard_map/ppermute | solution.py:32
  115.4 14.7 %collective-permute-start.8 = (bf16[128,1152]{1,0:T(8,128)(2,1)}, bf16[128,1152]{1,0:T(8,128)(2,1)S(1)}, u32[]{:S(2)}, u32[]{:S(2)}) collective-permute-start(bf16[128,1152]{1,0:T(8,128)(2,1)} %get-tuple-element.63), channel_id=1, source_target_pairs={{0,64},{32,96},{64,0},{96,32},{1,65},{33,97},{65,1},{97,33},{2,66}... | collective-permute-start | bytes 884744 | tf_op jit(solution)/shard_map/ppermute | solution.py:32
  130.3 7.0 %collective-permute-start.10 = (bf16[32,1152]{1,0:T(8,128)(2,1)S(1)}, bf16[32,1152]{1,0:T(8,128)(2,1)S(1)}, u32[]{:S(2)}, u32[]{:S(2)}) collective-permute-start(bf16[32,1152]{1,0:T(8,128)(2,1)S(1)} %get-tuple-element.72), channel_id=1, source_target_pairs={{0,2},{2,4},{4,6},{6,0},{1,3},{3,5},{5,7},{7,1},{8,10},{10,12},{12... | collective-permute-start | bytes 221192 | tf_op jit(solution)/shard_map/ppermute | solution.py:32
  131.6 5.8 %collective-permute-start.11 = (bf16[32,1152]{1,0:T(8,128)(2,1)S(1)}, bf16[32,1152]{1,0:T(8,128)(2,1)S(1)}, u32[]{:S(2)}, u32[]{:S(2)}) collective-permute-start(bf16[32,1152]{1,0:T(8,128)(2,1)S(1)} %get-tuple-element.71), channel_id=1, source_target_pairs={{0,6},{2,0},{4,2},{6,4},{1,7},{3,1},{5,3},{7,5},{8,14},{10,8},{12,... | collective-permute-start | bytes 221192 | tf_op jit(solution)/shard_map/ppermute | solution.py:32
  133.1 4.7 %collective-permute-start.9 = (bf16[32,1152]{1,0:T(8,128)(2,1)S(1)}, bf16[32,1152]{1,0:T(8,128)(2,1)S(1)}, u32[]{:S(2)}, u32[]{:S(2)}) collective-permute-start(bf16[32,1152]{1,0:T(8,128)(2,1)S(1)} %get-tuple-element.70), channel_id=1, source_target_pairs={{0,4},{2,6},{4,0},{6,2},{1,5},{3,7},{5,1},{7,3},{8,12},{10,14},{12... | collective-permute-start | bytes 221192 | tf_op jit(solution)/shard_map/ppermute | solution.py:32
  135.6 7.7 %collective-permute-start.12 = (bf16[16,4,8,512]{3,2,1,0:T(8,128)(2,1)S(1)}, bf16[16,4,8,512]{3,2,1,0:T(8,128)(2,1)S(1)}, u32[]{:S(2)}, u32[]{:S(2)}) collective-permute-start(bf16[16,4,8,512]{3,2,1,0:T(8,128)(2,1)S(1)} %slice_bitcast_fusion), channel_id=1, source_target_pairs={{0,1},{1,0},{2,3},{3,2},{4,5},{5,4},{6,7},{7,6},{8,9},{9,8},{10,11... | collective-permute-start | bytes 1572872 | tf_op jit(solution)/shard_map/ppermute | solution.py:22
  137.8 8.4 %collective-permute-start.13 = (bf16[32,1152]{1,0:T(8,128)(2,1)S(1)}, bf16[32,1152]{1,0:T(8,128)(2,1)S(1)}, u32[]{:S(2)}, u32[]{:S(2)}) collective-permute-start(bf16[32,1152]{1,0:T(8,128)(2,1)S(1)} %fusion.2), channel_id=1, source_target_pairs={{0,128},{128,0},{1,129},{129,1},{2,130},{130,2},{3,131},{131,3},{4... | collective-permute-start | bytes 221192 | tf_op jit(solution)/shard_map/ppermute | solution.py:27
  143.4 0.8 copy-start.11
  146.2 13.7 %collective-permute-start.14 = (bf16[32,1152]{1,0:T(8,128)(2,1)S(1)}, bf16[32,1152]{1,0:T(8,128)(2,1)S(1)}, u32[]{:S(2)}, u32[]{:S(2)}) collective-permute-start(bf16[32,1152]{1,0:T(8,128)(2,1)S(1)} %add_convert_fusion), channel_id=1, source_target_pairs={{0,0},{1,16},{2,2},{3,18},{4,4},{5,20},{6,6},{7,22},{8,32},{9,48},... | collective-permute-start | bytes 221192 | tf_op jit(solution)/shard_map/ppermute | solution.py:409
  154.6 5.4 %collective-permute-start.15 = (bf16[32,1152]{1,0:T(8,128)(2,1)S(1)}, bf16[32,1152]{1,0:T(8,128)(2,1)S(1)}, u32[]{:S(2)}, u32[]{:S(2)}) collective-permute-start(bf16[32,1152]{1,0:T(8,128)(2,1)S(1)} %add_convert_fusion), channel_id=1, source_target_pairs={{0,32},{1,48},{2,34},{3,50},{4,36},{5,52},{6,38},{7,54},{8,0},{9,1... | collective-permute-start | bytes 221192 | tf_op jit(solution)/shard_map/ppermute | solution.py:409
  154.7 8.2 %collective-permute-start.16 = (bf16[32,1152]{1,0:T(8,128)(2,1)S(1)}, bf16[32,1152]{1,0:T(8,128)(2,1)S(1)}, u32[]{:S(2)}, u32[]{:S(2)}) collective-permute-start(bf16[32,1152]{1,0:T(8,128)(2,1)S(1)} %add_convert_fusion), channel_id=1, source_target_pairs={{0,64},{1,80},{2,66},{3,82},{4,68},{5,84},{6,70},{7,86},{8,96},{9,... | collective-permute-start | bytes 221192 | tf_op jit(solution)/shard_map/ppermute | solution.py:409
  158.0 12.2 %collective-permute-start.17 = (bf16[32,1152]{1,0:T(8,128)(2,1)S(1)}, bf16[32,1152]{1,0:T(8,128)(2,1)S(1)}, u32[]{:S(2)}, u32[]{:S(2)}) collective-permute-start(bf16[32,1152]{1,0:T(8,128)(2,1)S(1)} %add_convert_fusion), channel_id=1, source_target_pairs={{0,96},{1,112},{2,98},{3,114},{4,100},{5,116},{6,102},{7,118},{8,6... | collective-permute-start | bytes 221192 | tf_op jit(solution)/shard_map/ppermute | solution.py:409
